TPU v7x, 32 devices: a whole 2x2x4 slice. The times are simulated.
32 devices in a mesh: dp: 8 (over y, x, core), tensor: 4 (over z).
Axes of the slice: x: 2, y: 2, z: 4, core: 2. Of those that a mesh axis runs over, the one named last changes fastest.
Arguments:
- hidden_in: bfloat16 [32768, 768], P(('dp', 'tensor')), may hold values from -6 to 6
- seg_ids: int32 [32768], P('dp'), may hold values from 0 to 559, as said below
- norm1_gain: float32 [768], replicated, may hold values from 0.1 to 1.9
- norm2_gain: float32 [768], replicated, may hold values from 0.1 to 1.9
- qkv_weight: bfloat16 [768, 3, 12, 64], P(None, None, 'tensor'), may hold values from -0.21875 to 0.21875
- attn_weight: bfloat16 [768, 768], P('tensor'), may hold values from -0.875 to 0.875
- mlp_in_weight: bfloat16 [768, 2, 1152], P(None, None, 'tensor'), may hold values from -0.21875 to 0.21875
- mlp_out_weight: bfloat16 [1152, 768], P('tensor'), may hold values from -0.1875 to 0.1875
- out_grad: bfloat16 [32768, 768], P(('dp', 'tensor')), may hold values from -6 to 6
Outputs:
- layer_out: bfloat16 [32768, 768], P(('dp', 'tensor'))
- grad_hidden: bfloat16 [32768, 768], P(('dp', 'tensor'))
- grad_norm1_gain: float32 [768], replicated
- grad_norm2_gain: float32 [768], replicated
- grad_qkv_weight: float32 [768, 3, 12, 64], P(None, None, 'tensor')
- grad_attn_weight: float32 [768, 768], P('tensor')
- grad_mlp_in_weight: float32 [768, 2, 1152], P(None, None, 'tensor')
- grad_mlp_out_weight: float32 [1152, 768], P('tensor')
Inputs may be any that keep to these rules, and one draw needn't show every extreme that they name: `seg_ids`: within each sequence of 2048 tokens the id rises by exactly one from each document to the next; no id is shared by two sequences; a document has 1 to 800 tokens and every sequence holds one document of exactly 800 tokens.
All inputs are finite; a program needn't handle non-finite values.
Results may differ from a plain program's by a relative error of at most 0.02.
Values may be sent and summed in bfloat16 or wider, within the bound.
No kernel may reach another device: no remote copies, remote signals or barrier semaphores. Data moves between devices by JAX's collectives and lax.ppermute only.
A program may use at most 192 MiB of HBM per device.

v0:
```python
import jax
import jax.numpy as jnp
from jax import lax
from jax.sharding import PartitionSpec as P

WINDOW = 128


eps_norm = 1e-05
rope_base = 10000.0


def layer_norm(row_vals, gain_vec):
    average = jnp.mean(row_vals, axis=-1, keepdims=True)
    centered = row_vals - average
    spread_sq = jnp.mean(centered * centered, axis=-1, keepdims=True)
    return centered * lax.rsqrt(spread_sq + eps_norm) * gain_vec


def doc_positions(seg_ids):
    count_all = seg_ids.shape[0]
    places = jnp.arange(count_all, dtype=jnp.int32)
    earlier = jnp.concatenate([jnp.full((1,), -1, jnp.int32), seg_ids[:-1]])
    starts = jnp.where(seg_ids != earlier, places, 0)
    return places - lax.cummax(starts, axis=0)


def rope_tables(positions, head_dim):
    freq_vals = rope_base ** (-jnp.arange(0, head_dim, 2).astype(jnp.float32) / head_dim)
    angles = positions.astype(jnp.float32)[:, None] * freq_vals[None, :]
    angles = jnp.concatenate([angles, angles], axis=1)
    return (jnp.cos(angles), jnp.sin(angles))


def rotate(arr_vals, cosine_tab, sine_tab):
    width_half = arr_vals.shape[-1] // 2
    turned = jnp.concatenate([-arr_vals[..., width_half:], arr_vals[..., :width_half]], axis=-1)
    return arr_vals * cosine_tab[:, None, :] + turned * sine_tab[:, None, :]


def rotate_back(grad_vals, cosine_tab, sine_tab):
    width_half = grad_vals.shape[-1] // 2
    scaled = grad_vals * sine_tab[:, None, :]
    turned = jnp.concatenate([scaled[..., width_half:], -scaled[..., :width_half]], axis=-1)
    return grad_vals * cosine_tab[:, None, :] + turned


def geglu(gate_up):
    width_half = gate_up.shape[1] // 2
    return jax.nn.gelu(gate_up[:, :width_half], approximate=False) * gate_up[:, width_half:]


def matmul(left_arr, right_arr):
    return jnp.dot(left_arr, right_arr, preferred_element_type=jnp.float32)


def row_contract(left_arr, right_arr):
    return lax.dot_general(
        left_arr, right_arr, (((0,), (0,)), ((), ())), preferred_element_type=jnp.float32
    )


def block_mask(seg_q, seg_k, block_rows):
    window_half = WINDOW // 2
    q_place = jnp.arange(block_rows, dtype=jnp.int32)[:, None]
    k_place = jnp.arange(block_rows + 2 * window_half, dtype=jnp.int32)[None, :] - window_half
    return (jnp.abs(q_place - k_place) <= window_half) & (seg_q[:, None] == seg_k[None, :])


def block_scores(queries, keys_ext, seg_query, seg_key, first_row, block_rows):
    key_rows = block_rows + WINDOW
    q_blk = lax.dynamic_slice_in_dim(queries, first_row, block_rows, 0)
    k_blk = lax.dynamic_slice_in_dim(keys_ext, first_row, key_rows, 0)
    seg_q = lax.dynamic_slice_in_dim(seg_query, first_row, block_rows, 0)
    seg_k = lax.dynamic_slice_in_dim(seg_key, first_row, key_rows, 0)
    scale_factor = queries.shape[-1] ** (-0.5)
    scores = (
        jnp.einsum("qhe,khe->hqk", q_blk, k_blk, preferred_element_type=jnp.float32) * scale_factor
    )
    allowed = block_mask(seg_q, seg_k, block_rows)
    return (q_blk, k_blk, jnp.where(allowed[None], scores, -1e30))


def attend(queries, keys_ext, values_ext, seg_query, seg_key, block_rows):
    total_rows = queries.shape[0]

    def one_block(block_idx):
        first_row = block_idx * block_rows
        q_blk, k_blk, scores = block_scores(
            queries, keys_ext, seg_query, seg_key, first_row, block_rows
        )
        v_blk = lax.dynamic_slice_in_dim(values_ext, first_row, block_rows + WINDOW, 0)
        row_top = jnp.max(scores, axis=-1, keepdims=True)
        expo_vals = jnp.exp(scores - row_top)
        row_total = jnp.sum(expo_vals, axis=-1, keepdims=True)
        prob_vals = (expo_vals / row_total).astype(jnp.bfloat16)
        blk_out = jnp.einsum("hqk,khe->qhe", prob_vals, v_blk, preferred_element_type=jnp.float32)
        return (blk_out, (row_top + jnp.log(row_total))[..., 0])

    blk_out, log_norm = lax.map(one_block, jnp.arange(total_rows // block_rows))
    return (blk_out.reshape(queries.shape), log_norm)


def attend_back(queries, keys_ext, values_ext, seg_query, seg_key, log_norm, grad_vals, block_rows):
    total_rows = queries.shape[0]
    key_rows = block_rows + WINDOW
    scale_factor = queries.shape[-1] ** (-0.5)

    def one_block(block_idx, carry_vals):
        grad_q, grad_k, grad_v = carry_vals
        first_row = block_idx * block_rows
        q_blk, k_blk, scores = block_scores(
            queries, keys_ext, seg_query, seg_key, first_row, block_rows
        )
        v_blk = lax.dynamic_slice_in_dim(values_ext, first_row, key_rows, 0)
        g_blk = lax.dynamic_slice_in_dim(grad_vals, first_row, block_rows, 0)
        prob_vals = jnp.exp(scores - log_norm[block_idx][:, :, None])
        low_probs = prob_vals.astype(jnp.bfloat16)
        grad_v_blk = jnp.einsum(
            "hqk,qhe->khe", low_probs, g_blk, preferred_element_type=jnp.float32
        )
        grad_p = jnp.einsum("qhe,khe->hqk", g_blk, v_blk, preferred_element_type=jnp.float32)
        grad_s = prob_vals * (grad_p - jnp.sum(prob_vals * grad_p, axis=-1, keepdims=True))
        low_s = grad_s.astype(jnp.bfloat16)
        grad_q_blk = (
            jnp.einsum("hqk,khe->qhe", low_s, k_blk, preferred_element_type=jnp.float32)
            * scale_factor
        )
        grad_k_blk = (
            jnp.einsum("hqk,qhe->khe", low_s, q_blk, preferred_element_type=jnp.float32)
            * scale_factor
        )
        grad_q = lax.dynamic_update_slice_in_dim(grad_q, grad_q_blk, first_row, 0)
        grad_k = lax.dynamic_update_slice_in_dim(
            grad_k,
            lax.dynamic_slice_in_dim(grad_k, first_row, key_rows, 0) + grad_k_blk,
            first_row,
            0,
        )
        grad_v = lax.dynamic_update_slice_in_dim(
            grad_v,
            lax.dynamic_slice_in_dim(grad_v, first_row, key_rows, 0) + grad_v_blk,
            first_row,
            0,
        )
        return (grad_q, grad_k, grad_v)

    start_vals = (
        jnp.zeros(queries.shape, jnp.float32),
        jnp.zeros(keys_ext.shape, jnp.float32),
        jnp.zeros(values_ext.shape, jnp.float32),
    )
    return lax.fori_loop(0, total_rows // block_rows, one_block, start_vals)


def heads_plan(
    resid,
    seg_ids,
    norm1_gain,
    norm2_gain,
    qkv_weight,
    attn_weight,
    mlp_in_weight,
    mlp_out_weight,
    out_grad,
):
    window_half = WINDOW // 2
    model_width = resid.shape[1]
    head_count = qkv_weight.shape[2]
    head_dim = qkv_weight.shape[3]
    width_local = head_count * head_dim
    normed_one, back_one = jax.vjp(layer_norm, resid, norm1_gain)
    low_one = lax.all_gather(normed_one.astype(jnp.bfloat16), "tensor", axis=0, tiled=True)
    group_rows = low_one.shape[0]
    qkv_mat = qkv_weight.reshape(model_width, 3 * width_local)
    mixed_rows = matmul(low_one, qkv_mat)
    cosine_tab, sine_tab = rope_tables(doc_positions(seg_ids), head_dim)
    q_pre = mixed_rows[:, :width_local].reshape(group_rows, head_count, head_dim)
    k_pre = mixed_rows[:, width_local : 2 * width_local].reshape(group_rows, head_count, head_dim)
    queries = rotate(q_pre, cosine_tab, sine_tab).astype(jnp.bfloat16)
    key_vals = rotate(k_pre, cosine_tab, sine_tab).astype(jnp.bfloat16)
    value_vals = (
        mixed_rows[:, 2 * width_local :]
        .reshape(group_rows, head_count, head_dim)
        .astype(jnp.bfloat16)
    )
    pad_rows = ((window_half, window_half), (0, 0), (0, 0))
    keys_ext = jnp.pad(key_vals, pad_rows)
    values_ext = jnp.pad(value_vals, pad_rows)
    seg_key = jnp.pad(seg_ids, (window_half, window_half), constant_values=-1)
    block_rows = min(512, group_rows)
    attn_vals, log_norm = attend(queries, keys_ext, values_ext, seg_ids, seg_key, block_rows)
    low_attn = attn_vals.reshape(group_rows, width_local).astype(jnp.bfloat16)
    middle = resid + lax.psum_scatter(
        matmul(low_attn, attn_weight), "tensor", scatter_dimension=0, tiled=True
    )
    normed_two, back_two = jax.vjp(layer_norm, middle, norm2_gain)
    low_two = lax.all_gather(normed_two.astype(jnp.bfloat16), "tensor", axis=0, tiled=True)
    in_mat = mlp_in_weight.reshape(model_width, -1)
    act_vals, back_act = jax.vjp(geglu, matmul(low_two, in_mat))
    low_act = act_vals.astype(jnp.bfloat16)
    result = (
        middle
        + lax.psum_scatter(
            matmul(low_act, mlp_out_weight).astype(jnp.bfloat16),
            "tensor",
            scatter_dimension=0,
            tiled=True,
        ).astype(jnp.float32)
    ).astype(jnp.bfloat16)
    low_top = lax.all_gather(out_grad, "tensor", axis=0, tiled=True)
    grad_down = row_contract(low_act, low_top)
    grad_gate_up = back_act(matmul(low_top, mlp_out_weight.T))[0].astype(jnp.bfloat16)
    grad_in = row_contract(low_two, grad_gate_up)
    grad_normed_two = lax.psum_scatter(
        matmul(grad_gate_up, in_mat.T).astype(jnp.bfloat16),
        "tensor",
        scatter_dimension=0,
        tiled=True,
    ).astype(jnp.float32)
    grad_mid_ln, grad_gain_two = back_two(grad_normed_two)
    grad_middle = out_grad.astype(jnp.float32) + grad_mid_ln
    low_mid = lax.all_gather(grad_middle.astype(jnp.bfloat16), "tensor", axis=0, tiled=True)
    grad_attn = row_contract(low_attn, low_mid)
    grad_attn_vals = (
        matmul(low_mid, attn_weight.T)
        .astype(jnp.bfloat16)
        .reshape(group_rows, head_count, head_dim)
    )
    grad_q, grad_k_ext, grad_v_ext = attend_back(
        queries, keys_ext, values_ext, seg_ids, seg_key, log_norm, grad_attn_vals, block_rows
    )
    grad_keys = rotate_back(
        grad_k_ext[window_half : window_half + group_rows], cosine_tab, sine_tab
    )
    grad_queries = rotate_back(grad_q, cosine_tab, sine_tab)
    grad_values = grad_v_ext[window_half : window_half + group_rows]
    grad_mixed = jnp.concatenate(
        [
            grad_queries.reshape(group_rows, width_local),
            grad_keys.reshape(group_rows, width_local),
            grad_values.reshape(group_rows, width_local),
        ],
        axis=1,
    ).astype(jnp.bfloat16)
    grad_qkv = row_contract(low_one, grad_mixed).reshape(qkv_weight.shape)
    grad_normed_one = lax.psum_scatter(
        matmul(grad_mixed, qkv_mat.T).astype(jnp.bfloat16),
        "tensor",
        scatter_dimension=0,
        tiled=True,
    ).astype(jnp.float32)
    grad_res_ln, grad_gain_one = back_one(grad_normed_one)
    grad_hidden = (grad_middle + grad_res_ln).astype(jnp.bfloat16)
    weight_grads = (grad_qkv, grad_attn, grad_in.reshape(mlp_in_weight.shape), grad_down)
    return (result, grad_hidden, grad_gain_one, grad_gain_two, weight_grads)


def body(
    hidden_in,
    seg_ids,
    norm1_gain,
    norm2_gain,
    qkv_weight,
    attn_weight,
    mlp_in_weight,
    mlp_out_weight,
    out_grad,
):
    resid = hidden_in.astype(jnp.float32)
    result, grad_hidden, gain_one, gain_two, weight_grads = heads_plan(
        resid,
        seg_ids,
        norm1_gain,
        norm2_gain,
        qkv_weight,
        attn_weight,
        mlp_in_weight,
        mlp_out_weight,
        out_grad,
    )
    gain_sums = lax.psum((gain_one, gain_two), "tensor")
    totals = lax.psum(
        (
            weight_grads[0],
            weight_grads[1],
            weight_grads[2],
            weight_grads[3],
            gain_sums[0],
            gain_sums[1],
        ),
        "dp",
    )
    return (result, grad_hidden, totals[4], totals[5], totals[0], totals[1], totals[2], totals[3])


def solution(mesh):
    in_specs = (
        P(("dp", "tensor"), None),
        P("dp"),
        P(),
        P(),
        P(None, None, "tensor", None),
        P("tensor", None),
        P(None, None, "tensor"),
        P("tensor", None),
        P(("dp", "tensor"), None),
    )
    out_specs = (
        P(("dp", "tensor"), None),
        P(("dp", "tensor"), None),
        P(),
        P(),
        P(None, None, "tensor", None),
        P("tensor", None),
        P(None, None, "tensor"),
        P("tensor", None),
    )
    return jax.shard_map(body, mesh=mesh, in_specs=in_specs, out_specs=out_specs, check_vma=False)
```

profile of v0, /device:TPU:0, one launch (start us, length us, event | category | flops | bytes accessed | tf_op | source)
XLA Modules:
  0.0 1408.3 jit_solution(5761527856027461849)
XLA Ops:
  13.9 4.4 fusion.76
  18.3 112.8 %all-gather.5.cloned.1.call-done = bf16[4096,768]{1,0:T(8,128)(2,1)} async-done(((bf16[1024,768]{1,0:T(8,128)(2,1)}), bf16[4096,768]{1,0:T(8,128)(2,1)}) %all-gather.5.cloned.1.call-update) | async-done | bytes 6291472 | tf_op jit(solution)/shard_map/all_gather | solution.py:173
  131.1 6.2 fusion.91
  139.4 2.5 fusion.68
  145.5 81.7 %while.33 = (s32[]{:T(128)}, bf16[8,512,3,64]{1,3,2,0:T(8,128)(2,1)}, f32[8,3,512]{2,1,0:T(4,128)}, s32[8]{0:T(128)S(1)}, bf16[4224,3,64]{0,2,1:T(8,128)(2,1)}, ...) while((s32[]{:T(128)}, ...), condition=%wide.region_7.8_spmd, body=%wide.region_4.7_spmd.sunk | while | flops 265092224 | bytes 14259948 | solution.py:100
  151.2 3.1 fusion.140
  160.0 3.1 fusion.140
  168.8 3.1 fusion.140
  177.5 3.1 fusion.140
  186.3 3.1 fusion.140
  195.1 3.1 fusion.140
  203.9 3.1 fusion.140
  212.7 3.1 fusion.140
  231.4 6.4 fusion.92
  237.8 210.2 %reduce-scatter.5.cloned.1.call-done = f32[1024,768]{1,0:T(8,128)} async-done(((f32[4096,768]{1,0:T(8,128)}), f32[1024,768]{1,0:T(8,128)}) %reduce-scatter.5.cloned.1.call-update) | async-done | bytes 3145744 | tf_op jit(solution)/shard_map/reduce_scatter | solution.py:194
  454.2 115.9 %all-gather.7.cloned.1.call-done = bf16[4096,768]{1,0:T(8,128)(2,1)} async-done(((bf16[1024,768]{1,0:T(8,128)(2,1)}), bf16[4096,768]{1,0:T(8,128)(2,1)}) %all-gather.7.cloned.1.call-update) | async-done | bytes 6291472 | tf_op jit(solution)/shard_map/all_gather | solution.py:198
  570.1 9.1 fusion.93
  579.2 105.9 %all-gather.9.cloned.1.call-done = bf16[4096,768]{1,0:T(8,128)(2,1)} async-done(((bf16[1024,768]{1,0:T(8,128)(2,1)}), bf16[4096,768]{1,0:T(8,128)(2,1)}) %all-gather.9.cloned.1.call-update) | async-done | bytes 6291472 | tf_op jit(solution)/shard_map/all_gather | solution.py:211
  685.2 15.0 %fusion.74 = (f32[4096,288]{0,1:T(8,128)}, f32[4096,288]{0,1:T(8,128)S(1)}, f32[4096,288]{0,1:T(8,128)S(1)}) fusion(f32[4096,576]{0,1:T(8,128)} %fusion.93, bf16[4096,768]{1,0:T(8,128)(2,1)} %all-gather.9.cloned.1.call-done, bf16[288,768]{1,0:T(8,128)(2,1)S(1)} %copy-done.39), kind=kOutput, calls=%fused_computation.126 | convolution fusion | flops 1888616448 | bytes 25608192 | tf_op jit(solution)/shard_map/dot_general | solution.py:54
  700.2 2.5 multiply_add_fusion
  704.9 9.8 convolution_convert_fusion.1
  715.6 5.4 convolution_convert_fusion.2
  721.1 102.7 %reduce-scatter.9.cloned.1.call-done = bf16[1024,768]{1,0:T(8,128)(2,1)} async-done(((bf16[4096,768]{1,0:T(8,128)(2,1)}), bf16[1024,768]{1,0:T(8,128)(2,1)}) %reduce-scatter.9.cloned.1.call-update) | async-done | bytes 1572880 | tf_op jit(solution)/shard_map/reduce_scatter | solution.py:215
  823.8 2.7 fusion.61
  826.5 110.8 %reduce-scatter.7.cloned.1.call-done = bf16[1024,768]{1,0:T(8,128)(2,1)} async-done(((bf16[4096,768]{1,0:T(8,128)(2,1)}), bf16[1024,768]{1,0:T(8,128)(2,1)}) %reduce-scatter.7.cloned.1.call-update) | async-done | bytes 1572880 | tf_op jit(solution)/shard_map/reduce_scatter | solution.py:204
  937.2 4.8 fusion.85
  942.0 3.5 fusion.72
  945.6 116.0 %all-gather.11.cloned.1.call-done = bf16[4096,768]{1,0:T(8,128)(2,1)} async-done(((bf16[1024,768]{1,0:T(8,128)(2,1)}), bf16[4096,768]{1,0:T(8,128)(2,1)}) %all-gather.11.cloned.1.call-update) | async-done | bytes 6291472 | tf_op jit(solution)/shard_map/all_gather | solution.py:223
  1061.6 6.1 convolution_convert_fusion.3
  1072.0 99.9 %while.34 = (s32[]{:T(128)}, f32[4096,3,64]{0,2,1:T(8,128)}, f32[4224,3,64]{0,2,1:T(8,128)S(1)}, f32[4224,3,64]{0,2,1:T(8,128)}, bf16[4224,3,64]{0,2,1:T(8,128)(...) while((s32[]{:T(128)}, f32[4096,3,64]{0,2,1:T(8,128)}, ...), condition=%wide.region_17.18_spmd, body=%wide.region_15.17_spmd.sunk | while | flops 640097408 | bytes 34079504 | solution.py:153
  1075.1 2.7 multiply_reduce_fusion.3
  1079.6 2.4 fusion.151
  1087.5 2.7 multiply_reduce_fusion.3
  1092.1 2.5 fusion.151
  1100.0 2.7 multiply_reduce_fusion.3
  1104.6 2.4 fusion.151
  1107.0 2.4 fusion.153
  1112.5 2.7 multiply_reduce_fusion.3
  1117.0 2.5 fusion.151
  1119.5 2.4 fusion.153
  1125.0 2.7 multiply_reduce_fusion.3
  1129.5 2.5 fusion.151
  1132.0 2.5 fusion.153
  1137.5 2.7 multiply_reduce_fusion.3
  1142.0 2.4 fusion.151
  1144.5 2.5 fusion.153
  1150.0 2.7 multiply_reduce_fusion.3
  1154.5 2.4 fusion.151
  1162.5 2.7 multiply_reduce_fusion.3
  1167.0 2.5 fusion.151
  1169.5 2.5 fusion.153
  1171.9 3.0 broadcast_multiply_fusion
  1175.5 2.5 slice.116
  1178.0 3.3 fusion.69
  1183.0 7.1 convolution_convert_fusion
  1191.8 6.1 fusion.95
  1197.9 10.7 fusion.77
  1211.0 5.1 fusion.73
  1216.1 83.2 %reduce-scatter.11.cloned.1.call-done = bf16[1024,768]{1,0:T(8,128)(2,1)} async-done(((bf16[4096,768]{1,0:T(8,128)(2,1)}), bf16[1024,768]{1,0:T(8,128)(2,1)}) %reduce-scatter.11.cloned.1.call-update) | async-done | bytes 1572880 | tf_op jit(solution)/shard_map/reduce_scatter | solution.py:247
  1303.6 11.1 all-reduce.7
  1314.7 14.1 %all-reduce.5 = (f32[768]{0:T(1024)}, f32[768]{0:T(1024)}) all-reduce(f32[768]{0:T(1024)S(1)} %get-tuple-element.443, f32[768]{0:T(1024)S(1)} %get-tuple-element.444), channel_id=1, replica_groups=mesh['dp'=8,'tensor'=4] {'dp'}, use_global_device_ids=true, to_apply=%region_23.24 | all-reduce | flops 1536 | bytes 12288 | tf_op jit(solution)/shard_map/psum | solution.py:283
  1328.8 4.1 add_convert_fusion.1
  1332.9 62.8 %all-reduce.10.cloned.1.call-done = (f32[768,3,3,64]{0,3,2,1:T(8,128)}, f32[192,768]{1,0:T(8,128)}, f32[768,2,288]{0,2,1:T(8,128)}, f32[288,768]{1,0:T(8,128)}) async-done(((f32[768,3,3,64]{0,3,2,1:T(8,128)}, f32[192,768]{1,0:T(8,128)}, f32[768,2,288]{0,2,1:T(8,128)}, f32[288,768]{1,0:T(8,128)}), (f32[768,3,3,64]{0,3,2,1:T(8,128)}, f32[192,768]{1,0:T(8,128)}, f32[768,2,288]{0,2,1:T(8,128)}, ...) | async-done | bytes 5013520 | tf_op jit(solution)/shard_map/psum | solution.py:283
  1395.7 2.9 copy.49
  (285 shorter events, 129.8 us)
Async XLA Ops:
  7.2 563.0 %copy-start = (bf16[768,2,288]{0,2,1:T(8,128)(2,1)S(1)}, bf16[768,2,288]{0,2,1:T(8,128)(2,1)}, u32[]{:S(2)}) copy-start(bf16[768,2,288]{0,2,1:T(8,128)(2,1)} %param.19) | copy-start | bytes 2654212
  7.2 4.0 copy-start.4
  7.2 4.0 copy-start.31
  7.2 123.9 %all-gather.5.cloned.1.call-start = ((), (), s32[]{:S(2)}) async-start(), calls=%async_computation.4 | async-start | bytes 7864320 | tf_op jit(solution)/shard_map/all_gather | solution.py:173
  9.1 3.8 copy-start.29
  9.1 3.9 copy-start.26
  11.1 1.8 copy-start.36
  11.2 1.8 copy-start.33
  12.9 435.1 %reduce-scatter.5.cloned.1.call-start = ((), (), s32[]{:S(2)}) async-start(), calls=%async_computation.5 | async-start | bytes 15728640 | tf_op jit(solution)/shard_map/reduce_scatter | solution.py:194
  18.3 120.7 %copy-start.9 = (f32[4096,64]{0,1:T(8,128)}, f32[4096,64]{0,1:T(8,128)S(1)}, u32[]{:S(2)}) copy-start(f32[4096,64]{0,1:T(8,128)S(1)} %get-tuple-element.474) | copy-start | bytes 3145732
  138.2 1.2 copy-start.11
  227.2 4.2 copy-start.27
  230.2 1.2 copy-start.12
  237.8 332.4 %all-gather.7.cloned.1.call-start = ((), (), s32[]{:S(2)}) async-start(), calls=%async_computation.6 | async-start | bytes 7864320 | tf_op jit(solution)/shard_map/all_gather | solution.py:198
  450.3 1.7 copy-start.2
  450.3 1.7 copy-start.35
  453.6 231.6 %all-gather.9.cloned.1.call-start = ((), (), s32[]{:S(2)}) async-start(), calls=%async_computation.8 | async-start | bytes 7864320 | tf_op jit(solution)/shard_map/all_gather | solution.py:211
  454.2 369.6 %reduce-scatter.9.cloned.1.call-start = ((), (), s32[]{:S(2)}) async-start(), calls=%async_computation.9 | async-start | bytes 7864320 | tf_op jit(solution)/shard_map/reduce_scatter | solution.py:215
  570.1 115.0 %copy-start.39 = (bf16[288,768]{1,0:T(8,128)(2,1)S(1)}, bf16[288,768]{1,0:T(8,128)(2,1)}, u32[]{:S(2)}) copy-start(bf16[288,768]{1,0:T(8,128)(2,1)} %param.20) | copy-start | bytes 1327108
  685.2 15.0 %copy-start.8 = (f32[4096,576]{0,1:T(8,128)S(1)}, f32[4096,576]{0,1:T(8,128)}, u32[]{:S(2)}) copy-start(f32[4096,576]{0,1:T(8,128)} %fusion.93) | copy-start | bytes 28311556
  702.7 2.1 copy-start.14
  702.8 11.9 copy-start.15
  714.6 1.0 copy-start.40
  714.6 222.6 %reduce-scatter.7.cloned.1.call-start = ((), (), s32[]{:S(2)}) async-start(), calls=%async_computation.7 | async-start | bytes 7864320 | tf_op jit(solution)/shard_map/reduce_scatter | solution.py:204
  721.0 102.8 %copy-start.3 = (f32[1024,768]{1,0:T(8,128)S(1)}, f32[1024,768]{1,0:T(8,128)}, u32[]{:S(2)}) copy-start(f32[1024,768]{1,0:T(8,128)} %copy-done.2) | copy-start | bytes 9437188
  721.0 340.6 %all-gather.11.cloned.1.call-start = ((), (), s32[]{:S(2)}) async-start(), calls=%async_computation.10 | async-start | bytes 7864320 | tf_op jit(solution)/shard_map/all_gather | solution.py:223
  937.2 4.8 copy-start.7
  942.0 119.6 %copy-start.28 = (bf16[192,768]{1,0:T(8,128)(2,1)S(1)}, bf16[192,768]{1,0:T(8,128)(2,1)}, u32[]{:S(2)}) copy-start(bf16[192,768]{1,0:T(8,128)(2,1)} %param.18) | copy-start | bytes 884740
  945.6 353.7 %reduce-scatter.11.cloned.1.call-start = ((), (), s32[]{:S(2)}) async-start(), calls=%async_computation.11 | async-start | bytes 7864320 | tf_op jit(solution)/shard_map/reduce_scatter | solution.py:247
  1175.5 2.5 copy-start.10
  1178.0 3.3 copy-start.22
  1178.0 4.9 copy-start.38
  1181.3 1.2 copy-start.18
  1181.3 1.7 copy-start.20
  1190.1 1.7 copy-start.16
  1190.1 205.6 %all-reduce.10.cloned.1.call-start = ((), (), s32[]{:S(2)}) async-start(), calls=%async_computation.12 | async-start | bytes 10027008 | tf_op jit(solution)/shard_map/psum | solution.py:283
  1191.8 16.9 %slice-start.2 = ((s8[6291456]{0:T(1024)(128)(4,1)}), s8[4194304]{0:T(1024)(128)(4,1)S(1)}, s32[]{:S(2)}) async-start(s8[6291456]{0:T(1024)(128)(4,1)} %bitcast.112), calls=%async_computation.15 | async-start | bytes 8388608
  1191.8 19.1 %slice-start = ((s8[6291456]{0:T(1024)(128)(4,1)}), s8[4194304]{0:T(1024)(128)(4,1)S(1)}, s32[]{:S(2)}) async-start(s8[6291456]{0:T(1024)(128)(4,1)} %bitcast.110), calls=%async_computation.13 | async-start | bytes 8388608
  1197.9 10.7 copy-start.13
  1197.9 10.7 slice-start.3
  1197.9 13.0 slice-start.1
  1208.6 2.3 copy-start.19
  1208.6 2.3 copy-start.21
  1208.7 2.3 copy-start.23
  1216.1 83.2 %copy-start.5 = (bf16[1024,768]{1,0:T(8,128)(2,1)S(1)}, bf16[1024,768]{1,0:T(8,128)(2,1)}, u32[]{:S(2)}) copy-start(bf16[1024,768]{1,0:T(8,128)(2,1)} %param.13) | copy-start | bytes 4718596
  1216.1 83.2 %copy-start.30 = (f32[1024]{0:T(1024)S(1)}, f32[1024]{0:T(1024)}, u32[]{:S(2)}) copy-start(f32[1024]{0:T(1024)} %copy-done.29) | copy-start | bytes 12292
  1216.1 83.2 %copy-start.32 = (f32[768]{0:T(1024)S(1)}, f32[768]{0:T(1024)}, u32[]{:S(2)}) copy-start(f32[768]{0:T(1024)} %param.15) | copy-start | bytes 9220
  1216.1 85.6 %copy-start.37 = (f32[1024]{0:T(1024)S(1)}, f32[1024]{0:T(1024)}, u32[]{:S(2)}) copy-start(f32[1024]{0:T(1024)} %copy-done.36) | copy-start | bytes 12292
  1216.1 85.6 %copy-start.34 = (f32[1024]{0:T(1024)S(1)}, f32[1024]{0:T(1024)}, u32[]{:S(2)}) copy-start(f32[1024]{0:T(1024)} %copy-done.33) | copy-start | bytes 12292
  1299.3 2.4 copy-start.6
  1395.7 3.0 copy-start.25
  1395.7 3.8 copy-start.17
  1395.7 5.9 copy-start.1
  1398.7 2.0 copy-start.24
Sparse Core Ops, SparseCore 0:
  13.0 118.0 all-gather.4
  237.9 210.0 reduce-scatter.4
  453.7 116.3 all-gather.6
  571.6 113.5 all-gather.8
  714.8 108.9 reduce-scatter.8
  825.9 111.2 reduce-scatter.6
  945.7 115.8 all-gather.10
  1190.2 108.9 reduce-scatter.10
  1303.6 92.0 all-reduce.9
where the time goes:
time: 1410 us
  waiting for transfers between devices  1020 us (72%)
  matrix products  217 us (15%)
  other arithmetic  71.2 us (5%)
  local copies, waits for them, and re-layouts  42.2 us (3%)
  blocking collectives  25.2 us (2%)
  loops' own time  16.9 us (1%)
  between operations  14.6 us (1%)
    reduce_scatter x1, waiting for transfers between devices, heads_plan(): lax.psum_scatter(matmul(low_attn, attn_weight), 'tensor', scatter_dimensi...  210 us
    all_gather x1, waiting for transfers between devices, heads_plan(): lax.all_gather(grad_middle.astype(jnp.bfloat16), 'tensor', axis=0, tiled=...  116 us
    all_gather x1, waiting for transfers between devices, heads_plan(): lax.all_gather(normed_two.astype(jnp.bfloat16), 'tensor', axis=0, tiled=T...  116 us
    all_gather x1, waiting for transfers between devices, heads_plan(): lax.all_gather(normed_one.astype(jnp.bfloat16), 'tensor', axis=0, tiled=T...  113 us
    reduce_scatter x1, waiting for transfers between devices, heads_plan(): lax.psum_scatter(matmul(low_act, mlp_out_weight).astype(jnp.bfloat16), 't...  111 us
    all_gather x1, waiting for transfers between devices, heads_plan(): low_top = lax.all_gather(out_grad, 'tensor', axis=0, tiled=True)  106 us
    reduce_scatter x1, waiting for transfers between devices, heads_plan(): lax.psum_scatter(matmul(grad_gate_up, in_mat.T).astype(jnp.bfloat16), 'te...  103 us
    reduce_scatter x1, waiting for transfers between devices, heads_plan(): lax.psum_scatter(matmul(grad_mixed, qkv_mat.T).astype(jnp.bfloat16), 'ten...  83.2 us
  transfers between devices with their start and end apart: 9, of which 9 were waited for; matrix products, arithmetic and copies ran while one was open for 4% of the time, Pallas kernels for 0%

commit v1 on v0

v1 whole, which is shorter than its diff:
```python
import jax
import jax.numpy as jnp
from jax import lax
from jax.experimental import pallas as pl
from jax.experimental.pallas import tpu as pltpu
from jax.sharding import PartitionSpec as P

WINDOW = 128
HALF = WINDOW // 2
EPS = 1e-05
ROPE_BASE = 10000.0
BLK = 128
CORE, XBIT, YBIT = 1, 2, 4
bf16 = jnp.bfloat16
f32 = jnp.float32
MIB = 1024 * 1024


def nn(a, b):
    return lax.dot_general(a, b, (((1,), (0,)), ((), ())), preferred_element_type=f32)


def nt(a, b):
    return lax.dot_general(a, b, (((1,), (1,)), ((), ())), preferred_element_type=f32)


def tn(a, b):
    return lax.dot_general(a, b, (((0,), (0,)), ((), ())), preferred_element_type=f32)


def row_stats(x):
    mean = jnp.mean(x, axis=-1, keepdims=True)
    cen = x - mean
    inv = lax.rsqrt(jnp.mean(cen * cen, axis=-1, keepdims=True) + EPS)
    return cen * inv, inv


def fold_rows(x):
    return jnp.sum(x.reshape(x.shape[0] // 8, 8, x.shape[1]), axis=0)


def const_spec(shape):
    zeros = (0,) * len(shape)
    return pl.BlockSpec(shape, lambda i: zeros, pipeline_mode=pl.Buffered(1))


def row_spec(rows, cols):
    return pl.BlockSpec((rows, cols), lambda i: (i, 0))


def params(mib):
    return pltpu.CompilerParams(
        dimension_semantics=("arbitrary",), vmem_limit_bytes=mib * MIB
    )


def turn_lanes(z, lo_sign):
    width = z.shape[1]
    lane = lax.broadcasted_iota(jnp.int32, (1, width), 1)
    first = lane % 64 < 32
    ahead = pltpu.roll(z, width - 32, 1)
    behind = pltpu.roll(z, 32, 1)
    return jnp.where(first, lo_sign * ahead, -lo_sign * behind)


def qkv_kernel(x_ref, gain_ref, w_ref, cos_ref, sin_ref, low_ref, q_ref, k_ref, v_ref):
    normed, _ = row_stats(x_ref[...].astype(f32))
    low = (normed * gain_ref[...]).astype(bf16)
    low_ref[...] = low
    width = low.shape[1]
    cos = jnp.concatenate([cos_ref[...]] * (width // 128), axis=1)
    sin = jnp.concatenate([sin_ref[...]] * (width // 128), axis=1)
    q = nt(low, w_ref[0])
    q_ref[...] = (q * cos + turn_lanes(q, -1.0) * sin).astype(bf16)
    k = nt(low, w_ref[1])
    k_ref[...] = (k * cos + turn_lanes(k, -1.0) * sin).astype(bf16)
    v_ref[...] = nt(low, w_ref[2]).astype(bf16)


def qkv_call(x_ext, gain, w, cos, sin):
    rows, width = x_ext.shape
    blk = rows // 3
    out = jax.ShapeDtypeStruct((rows, width), bf16)
    return pl.pallas_call(
        qkv_kernel,
        grid=(rows // blk,),
        in_specs=[
            row_spec(blk, width),
            const_spec((1, width)),
            const_spec(w.shape),
            row_spec(blk, 128),
            row_spec(blk, 128),
        ],
        out_specs=[row_spec(blk, width)] * 4,
        out_shape=[out] * 4,
        compiler_params=params(40),
        cost_estimate=pl.CostEstimate(
            flops=6 * rows * width * width, bytes_accessed=14 * MIB, transcendentals=0
        ),
        name="qkv",
    )(x_ext, gain, w, cos, sin)


def stack_pair(z, scale):
    lane = lax.broadcasted_iota(jnp.int32, (1, 128), 1)
    low_head = (lane < 64).astype(f32) * scale
    high_head = (lane >= 64).astype(f32) * scale
    return jnp.concatenate([z * low_head.astype(bf16), z * high_head.astype(bf16)], axis=0)


def merge_pair(z):
    rows = z.shape[0] // 2
    lane = lax.broadcasted_iota(jnp.int32, (1, 128), 1)
    return jnp.where(lane < 64, z[:rows], z[rows:])


def attend_kernel(q_ref, k_ref, v_ref, bias_ref, out_ref, lse_ref):
    b = pl.program_id(0)
    start = pl.multiple_of(b * BLK, BLK)
    bias = bias_ref[0]
    bias = jnp.concatenate([bias, bias], axis=1)
    for j in range(q_ref.shape[1] // 128):
        cols = slice(128 * j, 128 * j + 128)
        qs = stack_pair(q_ref[pl.ds(start + HALF, BLK), cols], 0.125)
        kb = k_ref[pl.ds(start, 2 * BLK), cols]
        vb = v_ref[pl.ds(start, 2 * BLK), cols]
        s = nt(kb, qs) + bias
        top = jnp.max(s, axis=0, keepdims=True)
        e = jnp.exp(s - top)
        total = jnp.sum(e, axis=0, keepdims=True)
        low_p = (e * (1.0 / total)).astype(bf16)
        out_ref[:, cols] = merge_pair(tn(low_p, vb)).astype(bf16)
        lse_ref[0, j : j + 1, :] = top + jnp.log(total)


def attend_call(q, k, v, bias, rows):
    ext, width = q.shape
    blocks = rows // BLK
    return pl.pallas_call(
        attend_kernel,
        grid=(blocks,),
        in_specs=[
            const_spec((ext, width)),
            const_spec((ext, width)),
            const_spec((ext, width)),
            pl.BlockSpec((1, 2 * BLK, BLK), lambda i: (i, 0, 0)),
        ],
        out_specs=[row_spec(BLK, width), pl.BlockSpec((1, 8, 2 * BLK), lambda i: (i, 0, 0))],
        out_shape=[
            jax.ShapeDtypeStruct((rows, width), bf16),
            jax.ShapeDtypeStruct((blocks, 8, 2 * BLK), f32),
        ],
        compiler_params=params(32),
        cost_estimate=pl.CostEstimate(
            flops=12 * rows * 256 * width, bytes_accessed=9 * MIB, transcendentals=rows * 3072
        ),
        name="attend",
    )(q, k, v, bias)


def mlp_kernel(
    x_ref,
    og_ref,
    attn_ref,
    gain_ref,
    wa_ref,
    wi_ref,
    wo_ref,
    out_ref,
    gmid_ref,
    lowmid_ref,
    dattn_ref,
    low2_ref,
    act_ref,
    ggu_ref,
    gain_grad_ref,
):
    gain = gain_ref[...]
    middle = x_ref[...].astype(f32) + nn(attn_ref[...], wa_ref[...])
    normed, inv = row_stats(middle)
    low_two = (normed * gain).astype(bf16)
    low2_ref[...] = low_two
    og = og_ref[...]
    ff = wo_ref.shape[0]
    chunk = 384
    result = middle
    grad_n = jnp.zeros(middle.shape, f32)
    for c in range(ff // chunk):
        sl = slice(c * chunk, c * chunk + chunk)
        gate = nt(low_two, wi_ref[0, sl])
        up = nt(low_two, wi_ref[1, sl])
        wo = wo_ref[sl]
        phi = 0.5 + 0.5 * lax.erf(gate * (0.5**0.5))
        gel = gate * phi
        act = (gel * up).astype(bf16)
        act_ref[:, sl] = act
        result = result + nn(act, wo)
        grad_act = nt(og, wo)
        dens = jnp.exp(-0.5 * gate * gate) * 0.3989422804014327
        g_gate = (grad_act * up * (phi + gate * dens)).astype(bf16)
        g_up = (grad_act * gel).astype(bf16)
        ggu_ref[:, sl] = g_gate
        ggu_ref[:, ff + c * chunk : ff + c * chunk + chunk] = g_up
        grad_n = grad_n + nn(g_gate, wi_ref[0, sl]) + nn(g_up, wi_ref[1, sl])
    out_ref[...] = result.astype(bf16)

    @pl.when(pl.program_id(0) == 0)
    def _():
        gain_grad_ref[...] = jnp.zeros(gain_grad_ref.shape, f32)

    gain_grad_ref[...] += fold_rows(grad_n * normed)
    u = grad_n * gain
    grad_mid = og.astype(f32) + inv * (
        u
        - jnp.mean(u, axis=-1, keepdims=True)
        - normed * jnp.mean(u * normed, axis=-1, keepdims=True)
    )
    gmid_ref[...] = grad_mid
    low_mid = grad_mid.astype(bf16)
    lowmid_ref[...] = low_mid
    dattn_ref[...] = nt(low_mid, wa_ref[...]).astype(bf16)


def mlp_call(x, og, attn, gain, wa, wi, wo):
    rows, width = x.shape
    ff = wo.shape[0]
    blk = 256
    low = jax.ShapeDtypeStruct((rows, width), bf16)
    return pl.pallas_call(
        mlp_kernel,
        grid=(rows // blk,),
        in_specs=[row_spec(blk, width)] * 3
        + [const_spec((1, width)), const_spec(wa.shape), const_spec(wi.shape), const_spec(wo.shape)],
        out_specs=[row_spec(blk, width)] * 5
        + [row_spec(blk, ff), row_spec(blk, 2 * ff), pl.BlockSpec((8, width), lambda i: (0, 0))],
        out_shape=[
            low,
            jax.ShapeDtypeStruct((rows, width), f32),
            low,
            low,
            low,
            jax.ShapeDtypeStruct((rows, ff), bf16),
            jax.ShapeDtypeStruct((rows, 2 * ff), bf16),
            jax.ShapeDtypeStruct((8, width), f32),
        ],
        compiler_params=params(48),
        cost_estimate=pl.CostEstimate(
            flops=4 * rows * width * (width + 3 * ff),
            bytes_accessed=30 * MIB,
            transcendentals=2 * rows * ff,
        ),
        name="mlp",
    )(x, og, attn, gain, wa, wi, wo)


def attend_back_kernel(
    q_ref,
    k_ref,
    v_ref,
    do_ref,
    bias_ref,
    lse_ref,
    cos_ref,
    sin_ref,
    dq_ref,
    dk_ref,
    dv_ref,
    edge_ref,
):
    b = pl.program_id(0)
    start = pl.multiple_of(b * BLK, BLK)

    @pl.when(b == 0)
    def _():
        dk_ref[...] = jnp.zeros(dk_ref.shape, f32)
        dv_ref[...] = jnp.zeros(dv_ref.shape, f32)

    bias = bias_ref[0]
    bias = jnp.concatenate([bias, bias], axis=1)
    rows = pl.ds(start, 2 * BLK)
    cos = cos_ref[pl.ds(start + HALF, BLK), :] * 0.125
    sin = sin_ref[pl.ds(start + HALF, BLK), :] * 0.125
    for j in range(q_ref.shape[1] // 128):
        cols = slice(128 * j, 128 * j + 128)
        qs = stack_pair(q_ref[pl.ds(start + HALF, BLK), cols], 0.125)
        dos = stack_pair(do_ref[:, cols], 1.0)
        kb = k_ref[rows, cols]
        vb = v_ref[rows, cols]
        p = jnp.exp(nt(kb, qs) + bias - lse_ref[0, j : j + 1, :])
        dp = nt(vb, dos)
        dot = jnp.sum(p * dp, axis=0, keepdims=True)
        ds = (p * (dp - dot)).astype(bf16)
        dv_ref[rows, cols] += nn(p.astype(bf16), dos)
        dk_ref[rows, cols] += nn(ds, qs)
        dq = merge_pair(tn(ds, kb))
        dq_ref[:, cols] = (dq * cos + turn_lanes(dq * sin, 1.0)).astype(bf16)

    @pl.when(b == pl.num_programs(0) - 1)
    def _():
        width = dk_ref.shape[1]
        ext = dk_ref.shape[0]
        for at, ref in ((0, dk_ref), (width, dv_ref)):
            edge_ref[:HALF, at : at + width] = ref[:HALF, :].astype(bf16)
            edge_ref[HALF:, at : at + width] = ref[ext - HALF :, :].astype(bf16)


def attend_back_call(q, k, v, do, bias, lse, cos, sin):
    ext, width = q.shape
    rows = do.shape[0]
    full = const_spec((ext, width))
    acc = pl.BlockSpec((ext, width), lambda i: (0, 0))
    return pl.pallas_call(
        attend_back_kernel,
        grid=(rows // BLK,),
        in_specs=[
            full,
            full,
            full,
            row_spec(BLK, width),
            pl.BlockSpec((1, 2 * BLK, BLK), lambda i: (i, 0, 0)),
            pl.BlockSpec((1, 8, 2 * BLK), lambda i: (i, 0, 0)),
            const_spec((ext, 128)),
            const_spec((ext, 128)),
        ],
        out_specs=[
            row_spec(BLK, width),
            acc,
            acc,
            pl.BlockSpec((WINDOW, 2 * width), lambda i: (0, 0)),
        ],
        out_shape=[
            jax.ShapeDtypeStruct((rows, width), bf16),
            jax.ShapeDtypeStruct((ext, width), f32),
            jax.ShapeDtypeStruct((ext, width), f32),
            jax.ShapeDtypeStruct((WINDOW, 2 * width), bf16),
        ],
        compiler_params=params(48),
        cost_estimate=pl.CostEstimate(
            flops=30 * rows * 256 * width, bytes_accessed=20 * MIB, transcendentals=rows * 3072
        ),
        name="attend_back",
    )(q, k, v, do, bias, lse, cos, sin)


def mixed_kernel(dq_ref, dk_ref, dv_ref, first_ref, last_ref, cos_ref, sin_ref, mix_ref):
    width = dq_ref.shape[1]
    i = pl.program_id(0)
    mix_ref[:, :width] = dq_ref[...]
    cos = jnp.concatenate([cos_ref[...]] * (width // 128), axis=1)
    sin = jnp.concatenate([sin_ref[...]] * (width // 128), axis=1)
    pad = jnp.zeros((dk_ref.shape[0] - HALF, width), f32)
    is_first = (i == 0).astype(f32)
    is_last = (i == pl.num_programs(0) - 1).astype(f32)

    def joined(ref, at):
        cols = slice(at, at + width)
        head = first_ref[:, cols].astype(f32) * is_first
        tail = last_ref[:, cols].astype(f32) * is_last
        return ref[...] + jnp.concatenate([head, pad], axis=0) + jnp.concatenate([pad, tail], axis=0)

    dk = joined(dk_ref, 0)
    dv = joined(dv_ref, width)
    mix_ref[:, width : 2 * width] = (dk * cos + turn_lanes(dk * sin, 1.0)).astype(bf16)
    mix_ref[:, 2 * width :] = dv.astype(bf16)


def mixed_call(dq, dk, dv, first, last, cos, sin):
    rows, width = dq.shape
    blk = 256
    return pl.pallas_call(
        mixed_kernel,
        grid=(rows // blk,),
        in_specs=[row_spec(blk, width)] * 3
        + [const_spec(first.shape), const_spec(last.shape)]
        + [row_spec(blk, 128)] * 2,
        out_specs=row_spec(blk, 3 * width),
        out_shape=jax.ShapeDtypeStruct((rows, 3 * width), bf16),
        compiler_params=params(32),
        cost_estimate=pl.CostEstimate(
            flops=10 * rows * width, bytes_accessed=14 * MIB, transcendentals=0
        ),
        name="mixed",
    )(dq, dk, dv, first, last, cos, sin)


def input_grad_kernel(mix_ref, w_ref, x_ref, gmid_ref, gain_ref, out_ref, gain_grad_ref):
    grad_n = nn(mix_ref[...], w_ref[...])
    normed, inv = row_stats(x_ref[...].astype(f32))

    @pl.when(pl.program_id(0) == 0)
    def _():
        gain_grad_ref[...] = jnp.zeros(gain_grad_ref.shape, f32)

    gain_grad_ref[...] += fold_rows(grad_n * normed)
    u = grad_n * gain_ref[...]
    out_ref[...] = (
        gmid_ref[...]
        + inv
        * (
            u
            - jnp.mean(u, axis=-1, keepdims=True)
            - normed * jnp.mean(u * normed, axis=-1, keepdims=True)
        )
    ).astype(bf16)


def input_grad_call(mix, w, x, gmid, gain):
    rows, width = x.shape
    blk = 256
    return pl.pallas_call(
        input_grad_kernel,
        grid=(rows // blk,),
        in_specs=[
            row_spec(blk, 3 * width),
            const_spec(w.shape),
            row_spec(blk, width),
            row_spec(blk, width),
            const_spec((1, width)),
        ],
        out_specs=[row_spec(blk, width), pl.BlockSpec((8, width), lambda i: (0, 0))],
        out_shape=[
            jax.ShapeDtypeStruct((rows, width), bf16),
            jax.ShapeDtypeStruct((8, width), f32),
        ],
        compiler_params=params(40),
        cost_estimate=pl.CostEstimate(
            flops=6 * rows * width * width, bytes_accessed=16 * MIB, transcendentals=0
        ),
        name="input_grad",
    )(mix, w, x, gmid, gain)


def dp_swap(x, mask):
    count = lax.axis_size("dp")
    return lax.ppermute(x, "dp", [(i, i ^ mask) for i in range(count)])


def ring_shift(x, step):
    count = lax.axis_size("tensor")
    return lax.ppermute(x, "tensor", [(i, (i + step) % count) for i in range(count)])


def pair_swap(x):
    count = lax.axis_size("tensor")
    return lax.ppermute(x, "tensor", [(i, i ^ 1) for i in range(count)])


def index_dim(x, at, dim):
    return lax.squeeze(lax.dynamic_slice_in_dim(x, at, 1, dim), (dim,))


def core_rows(x, core, dim):
    rows = x.shape[dim]
    size = (rows // 2 + 7) // 8 * 8
    step = (rows - size) // 8
    tiles = x.reshape(x.shape[:dim] + (rows // 8, 8) + x.shape[dim + 1 :])
    part = lax.dynamic_slice_in_dim(tiles, core * step, size // 8, dim)
    return part.reshape(x.shape[:dim] + (size,) + x.shape[dim + 1 :])


def join_cores(a, b, rows, dim):
    size = a.shape[dim]
    keep = rows - size
    return jnp.concatenate([a, lax.slice_in_dim(b, size - keep, size, axis=dim)], axis=dim)


def spread_quads(piece):
    rows = piece.shape[1]
    half = (rows // 2 + 7) // 8 * 8
    from_x = dp_swap(piece, XBIT)
    from_y = dp_swap(piece, YBIT)
    diag = jnp.concatenate(
        [dp_swap(from_y[:, :half], XBIT), dp_swap(from_x[:, half:], YBIT)], axis=1
    )
    mine = [piece, from_x, from_y, diag]
    return mine, [dp_swap(part, CORE) for part in mine]


def gather_pieces(piece):
    steps = lax.axis_size("tensor")
    ring = jnp.stack([ring_shift(piece, s) for s in range(1, steps)])
    return spread_quads(ring)


def by_core(mine, theirs, core):
    first = core == 0
    return jnp.where(first, mine, theirs), jnp.where(first, theirs, mine)


def reduce_pieces(send, keep, quad):
    steps = keep.shape[0]
    half = steps // 2

    def add(a, b):
        return (a.astype(f32) + b.astype(f32)).astype(bf16)

    total = add(keep, dp_swap(send, CORE))
    rows, width = total.shape[2:]
    grid = total.reshape(steps, 2, 2, rows, width)
    x_at, y_at = quad & 1, quad >> 1
    first, second = grid[:half], grid[half:]

    def halve(arr, at, mask, dim):
        got = dp_swap(index_dim(arr, 1 - at, dim), mask)
        return add(index_dim(arr, at, dim), got)

    first = halve(first, x_at, XBIT, 2)
    second = halve(second, y_at, YBIT, 1)
    first = halve(first, y_at, YBIT, 1)
    second = halve(second, x_at, XBIT, 1)
    parts = [first[s] for s in range(half)] + [second[s] for s in range(steps - half)]
    mask = 8
    if lax.axis_size("dp") > mask:
        block = jnp.stack(parts)
        while mask < lax.axis_size("dp"):
            block = add(block, dp_swap(block, mask))
            mask *= 2
        parts = [block[s] for s in range(steps)]
    result = parts[0].astype(f32)
    for s in range(1, steps):
        result = result + ring_shift(parts[s], -s).astype(f32)
    return result.astype(bf16)


def put(buf, part, starts):
    return lax.dynamic_update_slice(buf, part, starts)


def tables(seg_ids, first_row, rows):
    count = seg_ids.shape[0]
    places = jnp.arange(count, dtype=jnp.int32)
    earlier = jnp.concatenate([jnp.full((1,), -1, jnp.int32), seg_ids[:-1]])
    starts = jnp.where(seg_ids != earlier, places, 0)
    positions = places - lax.cummax(starts, axis=0)
    ext = rows + WINDOW
    seg_ext = lax.dynamic_slice(jnp.pad(seg_ids, HALF, constant_values=-1), (first_row,), (ext,))
    pos_ext = lax.dynamic_slice(jnp.pad(positions, HALF), (first_row,), (ext,))
    freq = ROPE_BASE ** (-jnp.arange(0, 64, 2).astype(f32) / 64)
    angles = pos_ext.astype(f32)[:, None] * jnp.concatenate([freq] * 4)[None, :]
    blocks = rows // BLK
    seg_rows = seg_ext.reshape(blocks + 1, BLK)
    seg_k = jnp.concatenate([seg_rows[:-1], seg_rows[1:]], axis=1)
    seg_q = seg_ext[HALF : HALF + rows].reshape(blocks, BLK)
    k_place = jnp.arange(2 * BLK, dtype=jnp.int32)[:, None] - HALF
    q_place = jnp.arange(BLK, dtype=jnp.int32)[None, :]
    near = jnp.abs(k_place - q_place) <= HALF
    allowed = near[None] & (seg_k[:, :, None] == seg_q[:, None, :])
    bias = jnp.where(allowed, 0.0, -1e30).astype(f32)
    return jnp.cos(angles), jnp.sin(angles), bias


def body(
    hidden_in,
    seg_ids,
    norm1_gain,
    norm2_gain,
    qkv_weight,
    attn_weight,
    mlp_in_weight,
    mlp_out_weight,
    out_grad,
):
    rows, width = hidden_in.shape
    steps = lax.axis_size("tensor")
    here = lax.axis_index("tensor")
    at_dp = lax.axis_index("dp")
    core = at_dp & 1
    quad = (at_dp >> 1) & 3
    odd = (here & 1) == 1
    w_qkv = qkv_weight.transpose(1, 2, 3, 0).reshape(3, 4, 48, width)
    w_in = mlp_in_weight.transpose(1, 2, 0).reshape(2, 4, 72, width)
    w_out = mlp_out_weight.reshape(4, 72, width)
    w_attn = attn_weight.reshape(4, 48, width)

    edge = jnp.where(odd, hidden_in[:HALF], hidden_in[-HALF:])
    halo = pair_swap(edge)
    none = jnp.zeros_like(halo)
    x_ext = jnp.concatenate(
        [jnp.where(odd, halo, none), hidden_in, jnp.where(odd, none, halo)], axis=0
    )

    own_qkv = core_rows(index_dim(w_qkv, quad, 1), core, 1).reshape(3 * 24, width)
    mine, theirs = gather_pieces(own_qkv)
    qkv_all = jnp.zeros((3, steps, 4, 48, width), bf16)
    qkv_all = qkv_all.at[:, 0].set(w_qkv)
    for n in range(4):
        a, b = by_core(mine[n], theirs[n], core)
        a = a.reshape(steps - 1, 3, 24, width)
        b = b.reshape(steps - 1, 3, 24, width)
        part = join_cores(a, b, 48, 2).transpose(1, 0, 2, 3)[:, :, None]
        qkv_all = put(qkv_all, part, (0, 1, quad ^ n, 0, 0))
    qkv_all = qkv_all.reshape(3, width, width)

    own_rest = jnp.concatenate(
        [
            index_dim(index_dim(w_in, core, 0), quad, 0),
            core_rows(index_dim(w_out, quad, 0), core, 0),
            core_rows(index_dim(w_attn, quad, 0), core, 0),
        ],
        axis=0,
    )
    mine, theirs = gather_pieces(own_rest)
    in_all = jnp.zeros((2, steps, 4, 72, width), bf16).at[:, 0].set(w_in)
    out_all = jnp.zeros((steps, 4, 72, width), bf16).at[0].set(w_out)
    attn_all = jnp.zeros((steps, 4, 48, width), bf16).at[0].set(w_attn)
    for n in range(4):
        a, b = by_core(mine[n], theirs[n], core)
        pair = jnp.stack([a[:, :72], b[:, :72]])[:, :, None]
        in_all = put(in_all, pair, (0, 1, quad ^ n, 0, 0))
        out_all = put(
            out_all, join_cores(a[:, 72:112], b[:, 72:112], 72, 1)[:, None], (1, quad ^ n, 0, 0)
        )
        attn_all = put(
            attn_all, join_cores(a[:, 112:], b[:, 112:], 48, 1)[:, None], (1, quad ^ n, 0, 0)
        )
    ff = steps * 288
    in_all = in_all.reshape(2, ff, width)
    out_all = out_all.reshape(ff, width)
    attn_all = attn_all.reshape(width, width)

    cos, sin, bias = tables(seg_ids, here * rows, rows)
    gain_one = norm1_gain[None]
    gain_two = norm2_gain[None]
    low_one, q, k, v = qkv_call(x_ext, gain_one, qkv_all, cos, sin)
    low_attn, lse = attend_call(q, k, v, bias, rows)
    result, grad_mid, low_mid, dattn, low_two, low_act, ggu, gain_two_part = mlp_call(
        hidden_in, out_grad, low_attn, gain_two, attn_all, in_all, out_all
    )

    g_in = tn(ggu, low_two).astype(bf16).reshape(2, steps, 4, 72, width)
    g_out = tn(low_act, out_grad).astype(bf16).reshape(steps, 4, 72, width)
    g_attn = tn(low_attn, low_mid).astype(bf16).reshape(steps, 4, 48, width)

    def rest_for(c):
        return jnp.concatenate(
            [index_dim(g_in, c, 0), core_rows(g_out, c, 2), core_rows(g_attn, c, 2)], axis=2
        )

    rest = reduce_pieces(rest_for(1 - core), rest_for(core), quad)

    dq, dk, dv, edges = attend_back_call(q, k, v, dattn, bias, lse, cos, sin)
    got = pair_swap(jnp.where(odd, edges[:HALF], edges[HALF:])).reshape(HALF, 2, width)
    turn = width // steps
    got = jnp.where(odd, jnp.roll(got, turn, 2), jnp.roll(got, -turn, 2)).reshape(HALF, 2 * width)
    none = jnp.zeros_like(got)
    own = slice(HALF, HALF + rows)
    mix = mixed_call(
        dq,
        dk[own],
        dv[own],
        jnp.where(odd, got, none),
        jnp.where(odd, none, got),
        cos[own],
        sin[own],
    )
    g_qkv = tn(mix, low_one[own]).astype(bf16).reshape(3, steps, 4, 48, width)

    def qkv_for(c):
        part = core_rows(g_qkv, c, 3).transpose(1, 2, 0, 3, 4)
        return part.reshape(steps, 4, 72, width)

    qkv_total = reduce_pieces(qkv_for(1 - core), qkv_for(core), quad)
    grad_hidden, gain_one_part = input_grad_call(
        mix, qkv_all.reshape(3 * width, width), hidden_in, grad_mid, gain_one
    )

    gains = jnp.stack([jnp.sum(gain_one_part, axis=0), jnp.sum(gain_two_part, axis=0)])
    gains = jnp.pad(gains, ((0, 6), (0, 0)))
    mask = 1
    while mask < steps:
        gains = gains + lax.ppermute(gains, "tensor", [(i, i ^ mask) for i in range(steps)])
        mask *= 2
    mask = 1
    while mask < lax.axis_size("dp"):
        gains = gains + dp_swap(gains, mask)
        mask *= 2

    mine, theirs = spread_quads(rest[None])
    o_in = jnp.zeros((2, 4, 72, width), f32)
    o_out = jnp.zeros((4, 72, width), f32)
    o_attn = jnp.zeros((4, 48, width), f32)
    for n in range(4):
        a, b = by_core(mine[n][0].astype(f32), theirs[n][0].astype(f32), core)
        o_in = put(o_in, jnp.stack([a[:72], b[:72]])[:, None], (0, quad ^ n, 0, 0))
        o_out = put(o_out, join_cores(a[72:112], b[72:112], 72, 0)[None], (quad ^ n, 0, 0))
        o_attn = put(o_attn, join_cores(a[112:], b[112:], 48, 0)[None], (quad ^ n, 0, 0))
    mine, theirs = spread_quads(qkv_total[None])
    o_qkv = jnp.zeros((3, 4, 48, width), f32)
    for n in range(4):
        a, b = by_core(mine[n][0].astype(f32), theirs[n][0].astype(f32), core)
        part = join_cores(a.reshape(3, 24, width), b.reshape(3, 24, width), 48, 1)
        o_qkv = put(o_qkv, part[:, None], (0, quad ^ n, 0, 0))
    grad_qkv = o_qkv.reshape(3, 3, 64, width).transpose(3, 0, 1, 2)
    grad_in = o_in.reshape(2, 288, width).transpose(2, 0, 1)
    return (
        result,
        grad_hidden,
        gains[0],
        gains[1],
        grad_qkv,
        o_attn.reshape(192, width),
        grad_in,
        o_out.reshape(288, width),
    )


def solution(mesh):
    rows = P(("dp", "tensor"), None)
    in_specs = (
        rows,
        P("dp"),
        P(),
        P(),
        P(None, None, "tensor", None),
        P("tensor", None),
        P(None, None, "tensor"),
        P("tensor", None),
        rows,
    )
    out_specs = (
        rows,
        rows,
        P(),
        P(),
        P(None, None, "tensor", None),
        P("tensor", None),
        P(None, None, "tensor"),
        P("tensor", None),
    )
    return jax.shard_map(body, mesh=mesh, in_specs=in_specs, out_specs=out_specs, check_vma=False)
```

time: 1410 us -> 344 us (0.24)
  waiting for transfers between devices: 1020 us -> 104 us
  matrix products: 217 us -> 16.3 us
  Pallas kernels: 0 us -> 79.7 us
  starting transfers between devices: 0.54 us -> 58.4 us
  other arithmetic: 71.2 us -> 34.4 us
  blocking collectives: 25.2 us -> 0 us
  loops' own time: 16.9 us -> 0 us
    reduce_scatter x4 -> x0, waiting for transfers between devices: 507 us -> none  [the longest x1 210 us: heads_plan(): lax.psum_scatter(matmul(low_attn, attn_weight), 'tensor', scatter_dimensi...]
    all_gather x4 -> x0, waiting for transfers between devices: 451 us -> none  [the longest x1 116 us: heads_plan(): lax.all_gather(grad_middle.astype(jnp.bfloat16), 'tensor', axis=0, tiled=...]
    dot_general x68 -> x4, matrix products: 217 us -> 16.3 us  [tn(): lax.dot_general(a, b, (((0,), (0,)), ((), ())), preferred_element_type=f32)]
    ppermute x0 -> x61, waiting for transfers between devices: none -> 104 us  [the longest x45 84.9 us: dp_swap(): return lax.ppermute(x, 'dp', [(i, i ^ mask) for i in range(count)])]
    pallas_call x0 -> x6, Pallas kernels: none -> 79.7 us  [the longest x1 29.3 us: mlp_call(): pl.pallas_call(mlp_kernel, grid=(rows // blk,), in_specs=[row_spec(blk, w...]
    psum x1 -> x0, waiting for transfers between devices: 62.8 us -> none  [body(): lax.psum((weight_grads[0], weight_grads[1], weight_grads[2], weight_grads...]
    ppermute x0 -> x61, starting transfers between devices: none -> 58.4 us  [the longest x45 31.4 us: dp_swap(): return lax.ppermute(x, 'dp', [(i, i ^ mask) for i in range(count)])]
    reduce_sum x16 -> x2, other arithmetic: 27.1 us -> 0.02 us  [the longest x1 0.01 us: body(): jnp.sum(gain_two_part, axis=0)]
  transfers between devices with their start and end apart: 9 -> 61, of which waited for: 9 -> 22; matrix products, arithmetic and copies ran while one was open for 4% -> 17% of each run, Pallas kernels for 0% -> 7%
where the time goes in v1:
time: 344 us; the launch traced here: 339 us
  waiting for transfers between devices  104 us (30%)
  Pallas kernels  79.7 us (23%)
  starting transfers between devices  58.4 us (17%)
  local copies, waits for them, and re-layouts  42.8 us (12%)
  other arithmetic  34.4 us (10%)
  matrix products  16.3 us (5%)
    ppermute x45, waiting for transfers between devices, dp_swap(): return lax.ppermute(x, 'dp', [(i, i ^ mask) for i in range(count)])  84.9 us
    ppermute x45, starting transfers between devices, dp_swap(): return lax.ppermute(x, 'dp', [(i, i ^ mask) for i in range(count)])  31.4 us
    pallas_call x1, Pallas kernels, mlp_call(): pl.pallas_call(mlp_kernel, grid=(rows // blk,), in_specs=[row_spec(blk, w...  29.3 us
    pallas_call x1, Pallas kernels, attend_back_call(): pl.pallas_call(attend_back_kernel, grid=(rows // BLK,), in_specs=[full, f...  24.2 us
    ppermute x12, starting transfers between devices, ring_shift(): lax.ppermute(x, 'tensor', [(i, (i + step) % count) for i in range(count)])  19.8 us
    ppermute x12, waiting for transfers between devices, ring_shift(): lax.ppermute(x, 'tensor', [(i, (i + step) % count) for i in range(count)])  18.2 us
    dot_general x4, matrix products, tn(): lax.dot_general(a, b, (((0,), (0,)), ((), ())), preferred_element_type=f32)  16.3 us
    unnamed x94, local copies, waits for them, and re-layouts  15.8 us
  transfers between devices with their start and end apart: 61, of which 22 were waited for; matrix products, arithmetic and copies ran while one was open for 17% of the time, Pallas kernels for 7%

profile of v1, /device:TPU:0, one launch (start us, length us, event | category | flops | bytes accessed | tf_op | source)
XLA Modules:
  0.0 338.6 jit_solution(7843793521777463301)
XLA Ops:
  4.1 3.0 collective-permute-start.12
  7.1 2.6 collective-permute-start.13
  11.4 1.9 collective-permute-start.2
  13.3 1.6 slice_select_fusion.1
  14.9 2.5 collective-permute-start
  18.4 3.2 multiply_sine_fusion
  23.0 1.3 scatter.19
  24.3 2.1 scatter.16
  28.7 1.9 slice.611.cos_ref
  30.6 1.9 slice.612.sin_ref
  33.4 1.5 collective-permute-start.14
  34.9 3.4 %collective-permute-done.3 = bf16[72,768]{1,0:T(8,128)(2,1)S(1)} collective-permute-done((bf16[72,768]{1,0:T(8,128)(2,1)}, bf16[72,768]{1,0:T(8,128)(2,1)S(1)}, u32[]{:S(2)}, u32[]{:S(2)}) %collective-permute-start.3) | collective-permute-done | bytes 110624 | tf_op jit(solution)/shard_map/ppermute | solution.py:440
  39.4 1.6 collective-permute-start.5
  40.9 1.5 collective-permute-start.7
  42.5 1.5 pad_maximum_fusion.1.x_ref
  45.8 5.0 %collective-permute-done.7 = bf16[3,72,768]{2,1,0:T(8,128)(2,1)S(1)} collective-permute-done((bf16[3,72,768]{2,1,0:T(8,128)(2,1)S(1)}, bf16[3,72,768]{2,1,0:T(8,128)(2,1)S(1)}, u32[]{:S(2)}, u32[]{:S(2)}) %collective-permute-start.7) | collective-permute-done | bytes 331808 | tf_op jit(solution)/shard_map/ppermute | solution.py:435
  51.4 1.6 collective-permute-start.10
  54.1 12.9 %collective-permute-done.9 = bf16[3,40,768]{2,1,0:T(8,128)(2,1)S(1)} collective-permute-done((bf16[3,40,768]{2,1,0:T(8,128)(2,1)S(1)}, bf16[3,40,768]{2,1,0:T(8,128)(2,1)S(1)}, u32[]{:S(2)}, u32[]{:S(2)}) %collective-permute-start.9) | collective-permute-done | bytes 184352 | tf_op jit(solution)/shard_map/ppermute | solution.py:435
  67.0 1.5 collective-permute-start.18
  71.6 11.1 %collective-permute-done.18 = bf16[3,136,768]{2,1,0:T(8,128)(2,1)S(1)} collective-permute-done((bf16[3,136,768]{2,1,0:T(8,128)(2,1)S(1)}, bf16[3,136,768]{2,1,0:T(8,128)(2,1)S(1)}, u32[]{:S(2)}, u32[]{:S(2)}) %collective-permute-start.18) | collective-permute-done | bytes 626720 | tf_op jit(solution)/shard_map/ppermute | solution.py:435
  82.7 1.6 collective-permute-start.20
  84.3 1.6 collective-permute-start.21
  88.8 7.0 %qkv.1 = (bf16[1152,768]{1,0:T(8,128)(2,1)S(1)}, bf16[1152,768]{1,0:T(8,128)(2,1)S(1)}, bf16[1152,768]{1,0:T(8,128)(2,1)S(1)}, bf16[1152,768]{1,0:T(8,128)(2,1)S(1)}) custom-call(bf16[1152,768]{1,0:T(8,128)(2,1)S(1)} %pad_maximum_fusion.1.x_ref, f32[1,768]{1,0:T(1,128)S(1)} %broadcast_in_dim.149.gain_ref, bf16[3,768,768]{2,1,0:T(8,128)(2,1)S(1)} %bitcast.407, ...), custom_call_target="tpu_custom_call" | custom-call | flops 4076863488 | bytes 14680064 | tf_op jit(solution)/shard_map/qkv/pallas_call | solution.py:84
  97.0 9.8 %attend.1 = (bf16[1024,768]{1,0:T(8,128)(2,1)S(1)}, f32[8,8,256]{2,1,0:T(8,128)S(1)}) custom-call(bf16[1152,768]{1,0:T(8,128)(2,1)S(1)} %get-tuple-element.76.q_ref, bf16[1152,768]{1,0:T(8,128)(2,1)S(1)} %get-tuple-element.77.k_ref, bf16[1152,768]{1,0:T(8,128)(2,1)S(1)} %get-tuple-element.78.v_ref, f32[8,256,128]{2,1,0:T(8,128)S(1)} %copy-done.13), custom_call_target="tpu_custom_call" | custom-call | flops 2415919104 | bytes 9437184 | tf_op jit(solution)/shard_map/attend/pallas_call | solution.py:139
  113.7 29.3 %mlp.1 = (bf16[1024,768]{1,0:T(8,128)(2,1)}, f32[1024,768]{1,0:T(8,128)}, bf16[1024,768]{1,0:T(8,128)(2,1)S(1)}, bf16[1024,768]{1,0:T(8,128)(2,1)S(1)}, bf16[102...) custom-call(bf16[1024,768]{1,0:T(8,128)(2,1)} %x_ref.3, ...), custom_call_target="tpu_custom_call" | custom-call | flops 13287555072 | bytes 31457280 | tf_op jit(solution)/shard_map/mlp/pallas_call | solution.py:229
  143.0 5.5 %convolution_convert_fusion.2 = bf16[1152,768]{1,0:T(8,128)(2,1)} fusion(bf16[1024,1152]{1,0:T(8,128)(2,1)} %get-tuple-element.94, bf16[1024,768]{1,0:T(8,128)(2,1)S(1)} %copy-done.41), kind=kOutput, calls=%fused_computation.5 | convolution fusion | flops 1812824064 | bytes 5701632 | tf_op jit(solution)/shard_map/dot_general | solution.py:28
  148.5 24.2 %attend_back.1 = (bf16[1024,768]{1,0:T(8,128)(2,1)S(1)}, f32[1152,768]{1,0:T(8,128)}, f32[1152,768]{1,0:T(8,128)}, bf16[128,1536]{1,0:T(8,128)(2,1)S(1)}) custom-call(bf16[1152,768]{1,0:T(8,128)(2,1)} %copy-done.15, bf16[1152,768]{1,0:T(8,128)(2,1)} %copy-done.16, bf16[1152,768]{1,0:T(8,128)(2,1)} %copy-done.17, ...), custom_call_target="tpu_custom_call" | custom-call | flops 6039797760 | bytes 20971520 | tf_op jit(solution)/shard_map/attend_back/pallas_call | solution.py:312
  172.9 2.5 convolution_convert_fusion.3
  175.6 1.8 copy-done.26
  177.4 1.9 slice.509.dv_ref
  179.7 1.4 dynamic-slice_bitcast_fusion.3
  183.8 1.9 copy-done
  185.7 2.7 mixed.1.mix_ref
  188.5 4.2 %convolution_convert_fusion.1 = bf16[2304,768]{1,0:T(8,128)(2,1)S(1)} fusion(bf16[1024,2304]{1,0:T(8,128)(2,1)S(1)} %mixed.1.mix_ref, bf16[1152,768]{1,0:T(8,128)(2,1)S(1)} %copy-done.21), kind=kOutput, calls=%fused_computation.2 | convolution fusion | flops 3625648128 | bytes 9830400 | tf_op jit(solution)/shard_map/dot_general | solution.py:28
  192.7 2.4 constant_dynamic-slice_fusion.4
  195.0 1.3 copy.54
  197.8 4.2 %convolution_convert_fusion = bf16[2304,768]{1,0:T(8,128)(2,1)S(1)} fusion(bf16[1024,2304]{1,0:T(8,128)(2,1)S(1)} %bitcast.468, bf16[1024,768]{1,0:T(8,128)(2,1)S(1)} %copy-done.23), kind=kOutput, calls=%fused_computation.1 | convolution fusion | flops 3625648128 | bytes 9830400 | tf_op jit(solution)/shard_map/dot_general | solution.py:28
  203.1 2.0 pad_maximum_fusion
  205.4 4.3 %copy.53 = f32[3,4,4,3,8,768]{5,4,3,0,2,1:T(8,128)} copy(f32[3,4,4,3,8,768]{5,4,3,2,1,0:T(8,128)} %get-tuple-element.103) | data formatting | bytes 7077888 | tf_op jit(solution)/shard_map/convert_element_type | solution.py:495
  209.7 2.3 copy-done.2
  212.1 1.9 copy-done.14
  213.9 6.7 %input_grad.1 = (bf16[1024,768]{1,0:T(8,128)(2,1)}, f32[8,768]{1,0:T(8,128)S(1)}) custom-call(bf16[1024,2304]{1,0:T(8,128)(2,1)S(1)} %copy-done.2, bf16[2304,768]{1,0:T(8,128)(2,1)S(1)} %bitcast.408, bf16[1024,768]{1,0:T(8,128)(2,1)S(1)} %copy-done.9, f32[1024,768]{1,0:T(8,128)S(1)} %copy-done.14, f32[1,768]{1,0:T(1,128)S(1)} %broadcast_in_dim.149.gain_ref), custom_call_target="tpu_custom_call" | custom-call | flops 3623878656 | bytes 16777216 | tf_op jit(solution)/shard_map/input_grad/pallas_call | solution.py:410
  220.6 2.9 fusion
  224.3 1.8 collective-permute-start.24
  228.2 2.7 collective-permute-start.25
  230.9 5.3 %collective-permute-done.30 = bf16[2,2,72,768]{3,2,1,0:T(8,128)(2,1)S(1)} collective-permute-done((bf16[2,2,72,768]{3,2,1,0:T(8,128)(2,1)S(1)}, bf16[2,2,72,768]{3,2,1,0:T(8,128)(2,1)S(1)}, u32[]{:S(2)}, u32[]{:S(2)}) %collective-permute-start.30) | collective-permute-done | bytes 442400 | tf_op jit(solution)/shard_map/ppermute | solution.py:435
  237.0 1.4 collective-permute-done.33
  238.5 2.4 collective-permute-start.34
  240.9 2.5 collective-permute-done.31
  243.5 2.5 collective-permute-start.32
  247.2 1.4 collective-permute-start.36
  250.9 2.8 collective-permute-done.27
  254.2 3.3 collective-permute-done.28
  259.9 2.5 collective-permute-done.40
  264.5 2.4 add_convert_fusion
  270.6 15.1 %collective-permute-done.46 = bf16[2,2,136,768]{3,2,1,0:T(8,128)(2,1)S(1)} collective-permute-done((bf16[2,2,136,768]{3,2,1,0:T(8,128)(2,1)S(1)}, bf16[2,2,136,768]{3,2,1,0:T(8,128)(2,1)S(1)}, u32[]{:S(2)}, u32[]{:S(2)}) %collective-permute-start.46) | collective-permute-done | bytes 835616 | tf_op jit(solution)/shard_map/ppermute | solution.py:435
  286.6 4.3 %collective-permute-done.49 = bf16[2,2,136,768]{3,2,0,1:T(8,128)(2,1)S(1)} collective-permute-done((bf16[2,2,136,768]{3,2,0,1:T(8,128)(2,1)S(1)}, bf16[2,2,136,768]{3,2,0,1:T(8,128)(2,1)S(1)}, u32[]{:S(2)}, u32[]{:S(2)}) %collective-permute-start.49) | collective-permute-done | bytes 835616 | tf_op jit(solution)/shard_map/ppermute | solution.py:435
  292.2 7.2 %collective-permute-done.47 = bf16[2,136,768]{2,1,0:T(8,128)(2,1)S(1)} collective-permute-done((bf16[2,136,768]{2,1,0:T(8,128)(2,1)S(1)}, bf16[2,136,768]{2,1,0:T(8,128)(2,1)S(1)}, u32[]{:S(2)}, u32[]{:S(2)}) %collective-permute-start.47) | collective-permute-done | bytes 417824 | tf_op jit(solution)/shard_map/ppermute | solution.py:435
  299.5 2.8 collective-permute-start.48
  303.2 2.3 collective-permute-start.52
  305.5 2.4 collective-permute-done.48
  308.0 12.3 %collective-permute-done.51 = bf16[136,768]{1,0:T(8,128)(2,1)S(1)} collective-permute-done((bf16[136,768]{1,0:T(8,128)(2,1)S(1)}, bf16[136,768]{1,0:T(8,128)(2,1)S(1)}, u32[]{:S(2)}, u32[]{:S(2)}) %collective-permute-start.51) | collective-permute-done | bytes 208928 | tf_op jit(solution)/shard_map/ppermute | solution.py:440
  322.9 5.9 %collective-permute-done.56 = bf16[1,136,768]{2,1,0:T(8,128)(2,1)S(1)} collective-permute-done((bf16[1,136,768]{2,1,0:T(8,128)(2,1)S(1)}, bf16[1,136,768]{2,1,0:T(8,128)(2,1)S(1)}, u32[]{:S(2)}, u32[]{:S(2)}) %collective-permute-start.56) | collective-permute-done | bytes 208928 | tf_op jit(solution)/shard_map/ppermute | solution.py:435
  332.1 1.6 collective-permute-done.58
  (362 shorter events, 64.2 us)
Async XLA Ops:
  4.1 36.8 %collective-permute-start.12 = (bf16[136,768]{1,0:T(8,128)(2,1)}, bf16[136,768]{1,0:T(8,128)(2,1)}, u32[]{:S(2)}, u32[]{:S(2)}) collective-permute-start(bf16[136,768]{1,0:T(8,128)(2,1)} %pad_maximum_fusion.4), channel_id=1, source_target_pairs={{0,1},{1,2},{2,3},{3,0},{4,5},{5,6},{6,7},{7,4},{8,9},{9,10},{10,1... | collective-permute-start | bytes 626696 | tf_op jit(solution)/shard_map/ppermute | solution.py:440
  7.1 36.9 %collective-permute-start.13 = (bf16[136,768]{1,0:T(8,128)(2,1)}, bf16[136,768]{1,0:T(8,128)(2,1)}, u32[]{:S(2)}, u32[]{:S(2)}) collective-permute-start(bf16[136,768]{1,0:T(8,128)(2,1)} %pad_maximum_fusion.4), channel_id=1, source_target_pairs={{0,2},{1,3},{2,0},{3,1},{4,6},{5,7},{6,4},{7,5},{8,10},{9,11},{10,... | collective-permute-start | bytes 626696 | tf_op jit(solution)/shard_map/ppermute | solution.py:440
  11.4 22.0 %collective-permute-start.1 = (bf16[72,768]{1,0:T(8,128)(2,1)}, bf16[72,768]{1,0:T(8,128)(2,1)}, u32[]{:S(2)}, u32[]{:S(2)}) collective-permute-start(bf16[72,768]{1,0:T(8,128)(2,1)} %bitcast.5), channel_id=1, source_target_pairs={{0,1},{1,2},{2,3},{3,0},{4,5},{5,6},{6,7},{7,4},{8,9},{9,10},{10,1... | collective-permute-start | bytes 331784 | tf_op jit(solution)/shard_map/ppermute | solution.py:440
  11.4 23.5 %collective-permute-start.2 = (bf16[72,768]{1,0:T(8,128)(2,1)}, bf16[72,768]{1,0:T(8,128)(2,1)}, u32[]{:S(2)}, u32[]{:S(2)}) collective-permute-start(bf16[72,768]{1,0:T(8,128)(2,1)} %bitcast.5), channel_id=1, source_target_pairs={{0,2},{1,3},{2,0},{3,1},{4,6},{5,7},{6,4},{7,5},{8,10},{9,11},{10,... | collective-permute-start | bytes 331784 | tf_op jit(solution)/shard_map/ppermute | solution.py:440
  14.9 17.6 %collective-permute-start = (bf16[64,768]{1,0:T(8,128)(2,1)}, bf16[64,768]{1,0:T(8,128)(2,1)}, u32[]{:S(2)}, u32[]{:S(2)}) collective-permute-start(bf16[64,768]{1,0:T(8,128)(2,1)} %slice_select_fusion.1), channel_id=1, source_target_pairs={{0,1},{1,0},{2,3},{3,2},{4,5},{5,4},{6,7},{7,6},{8,9},{9,8},{10,11... | collective-permute-start | bytes 294920 | tf_op jit(solution)/shard_map/ppermute | solution.py:445
  32.5 5.8 %collective-permute-start.3 = (bf16[72,768]{1,0:T(8,128)(2,1)}, bf16[72,768]{1,0:T(8,128)(2,1)S(1)}, u32[]{:S(2)}, u32[]{:S(2)}) collective-permute-start(bf16[72,768]{1,0:T(8,128)(2,1)} %bitcast.5), channel_id=1, source_target_pairs={{0,3},{1,0},{2,1},{3,2},{4,7},{5,4},{6,5},{7,6},{8,11},{9,8},{10,9... | collective-permute-start | bytes 331784 | tf_op jit(solution)/shard_map/ppermute | solution.py:440
  33.4 10.6 %collective-permute-start.14 = (bf16[136,768]{1,0:T(8,128)(2,1)}, bf16[136,768]{1,0:T(8,128)(2,1)S(1)}, u32[]{:S(2)}, u32[]{:S(2)}) collective-permute-start(bf16[136,768]{1,0:T(8,128)(2,1)} %pad_maximum_fusion.4), channel_id=1, source_target_pairs={{0,3},{1,0},{2,1},{3,2},{4,7},{5,4},{6,5},{7,6},{8,11},{9,8},{10,9... | collective-permute-start | bytes 626696 | tf_op jit(solution)/shard_map/ppermute | solution.py:440
  39.3 13.7 %collective-permute-start.4 = (bf16[3,72,768]{2,1,0:T(8,128)(2,1)S(1)}, bf16[3,72,768]{2,1,0:T(8,128)(2,1)S(1)}, u32[]{:S(2)}, u32[]{:S(2)}) collective-permute-start(bf16[3,72,768]{2,1,0:T(8,128)(2,1)S(1)} %pad_maximum_fusion.3), channel_id=1, source_target_pairs={{0,4},{4,0},{8,12},{12,8},{16,20},{20,16},{24,28},{28,24},{1,5},{5... | collective-permute-start | bytes 995336 | tf_op jit(solution)/shard_map/ppermute | solution.py:435
  39.4 12.1 %collective-permute-start.5 = (bf16[3,72,768]{2,1,0:T(8,128)(2,1)S(1)}, bf16[3,72,768]{2,1,0:T(8,128)(2,1)S(1)}, u32[]{:S(2)}, u32[]{:S(2)}) collective-permute-start(bf16[3,72,768]{2,1,0:T(8,128)(2,1)S(1)} %pad_maximum_fusion.3), channel_id=1, source_target_pairs={{0,8},{4,12},{8,0},{12,4},{16,24},{20,28},{24,16},{28,20},{1,9},{5... | collective-permute-start | bytes 995336 | tf_op jit(solution)/shard_map/ppermute | solution.py:435
  40.9 9.9 %collective-permute-start.7 = (bf16[3,72,768]{2,1,0:T(8,128)(2,1)S(1)}, bf16[3,72,768]{2,1,0:T(8,128)(2,1)S(1)}, u32[]{:S(2)}, u32[]{:S(2)}) collective-permute-start(bf16[3,72,768]{2,1,0:T(8,128)(2,1)S(1)} %pad_maximum_fusion.3), channel_id=1, source_target_pairs={{0,16},{4,20},{8,24},{12,28},{16,0},{20,4},{24,8},{28,12},{1,17},{... | collective-permute-start | bytes 995336 | tf_op jit(solution)/shard_map/ppermute | solution.py:435
  45.1 25.2 %collective-permute-start.15 = (bf16[3,136,768]{2,1,0:T(8,128)(2,1)S(1)}, bf16[3,136,768]{2,1,0:T(8,128)(2,1)S(1)}, u32[]{:S(2)}, u32[]{:S(2)}) collective-permute-start(bf16[3,136,768]{2,1,0:T(8,128)(2,1)S(1)} %pad_maximum_fusion.2), channel_id=1, source_target_pairs={{0,4},{4,0},{8,12},{12,8},{16,20},{20,16},{24,28},{28,24},{1,5},{5... | collective-permute-start | bytes 1880072 | tf_op jit(solution)/shard_map/ppermute | solution.py:435
  45.2 39.1 %collective-permute-start.16 = (bf16[3,136,768]{2,1,0:T(8,128)(2,1)S(1)}, bf16[3,136,768]{2,1,0:T(8,128)(2,1)S(1)}, u32[]{:S(2)}, u32[]{:S(2)}) collective-permute-start(bf16[3,136,768]{2,1,0:T(8,128)(2,1)S(1)} %pad_maximum_fusion.2), channel_id=1, source_target_pairs={{0,8},{4,12},{8,0},{12,4},{16,24},{20,28},{24,16},{28,20},{1,9},{5... | collective-permute-start | bytes 1880072 | tf_op jit(solution)/shard_map/ppermute | solution.py:435
  50.8 16.1 %collective-permute-start.9 = (bf16[3,40,768]{2,1,0:T(8,128)(2,1)S(1)}, bf16[3,40,768]{2,1,0:T(8,128)(2,1)S(1)}, u32[]{:S(2)}, u32[]{:S(2)}) collective-permute-start(bf16[3,40,768]{2,1,0:T(8,128)(2,1)S(1)} %slice.577), channel_id=1, source_target_pairs={{0,8},{4,12},{8,0},{12,4},{16,24},{20,28},{24,16},{28,20},{1,9},{5... | collective-permute-start | bytes 552968 | tf_op jit(solution)/shard_map/ppermute | solution.py:435
  51.4 17.1 %collective-permute-start.10 = (bf16[3,32,768]{2,1,0:T(8,128)(2,1)S(1)}, bf16[3,32,768]{2,1,0:T(8,128)(2,1)S(1)}, u32[]{:S(2)}, u32[]{:S(2)}) collective-permute-start(bf16[3,32,768]{2,1,0:T(8,128)(2,1)S(1)} %slice.578), channel_id=1, source_target_pairs={{0,16},{4,20},{8,24},{12,28},{16,0},{20,4},{24,8},{28,12},{1,17},{... | collective-permute-start | bytes 442376 | tf_op jit(solution)/shard_map/ppermute | solution.py:435
  53.0 15.6 %collective-permute-start.6 = (bf16[3,72,768]{2,1,0:T(8,128)(2,1)S(1)}, bf16[3,72,768]{2,1,0:T(8,128)(2,1)S(1)}, u32[]{:S(2)}, u32[]{:S(2)}) collective-permute-start(bf16[3,72,768]{2,1,0:T(8,128)(2,1)S(1)} %collective-permute-done.5), channel_id=1, source_target_pairs={{0,4},{4,0},{8,12},{12,8},{16,20},{20,16},{24,28},{28,24},{1,5},{5... | collective-permute-start | bytes 995336 | tf_op jit(solution)/shard_map/ppermute | solution.py:435
  67.0 15.7 %collective-permute-start.18 = (bf16[3,136,768]{2,1,0:T(8,128)(2,1)S(1)}, bf16[3,136,768]{2,1,0:T(8,128)(2,1)S(1)}, u32[]{:S(2)}, u32[]{:S(2)}) collective-permute-start(bf16[3,136,768]{2,1,0:T(8,128)(2,1)S(1)} %pad_maximum_fusion.2), channel_id=1, source_target_pairs={{0,16},{4,20},{8,24},{12,28},{16,0},{20,4},{24,8},{28,12},{1,17},{... | collective-permute-start | bytes 1880072 | tf_op jit(solution)/shard_map/ppermute | solution.py:435
  68.5 1.7 collective-permute-start.8
  68.6 19.6 %collective-permute-start.11 = (bf16[3,72,768]{2,1,0:T(8,128)(2,1)S(1)}, bf16[3,72,768]{2,1,0:T(8,128)(2,1)S(1)}, u32[]{:S(2)}, u32[]{:S(2)}) collective-permute-start(bf16[3,72,768]{2,1,0:T(8,128)(2,1)S(1)} %constant_dynamic-update-slice_fusion), channel_id=1, source_target_pairs={{0,4},{4,0},{8,12},{12,8},{16,20},{20,16},{24,28},{28,24},{1,5},{5... | collective-permute-start | bytes 995336 | tf_op jit(solution)/shard_map/ppermute | solution.py:435
  82.7 24.1 %collective-permute-start.20 = (bf16[3,72,768]{2,1,0:T(8,128)(2,1)S(1)}, bf16[3,72,768]{2,1,0:T(8,128)(2,1)S(1)}, u32[]{:S(2)}, u32[]{:S(2)}) collective-permute-start(bf16[3,72,768]{2,1,0:T(8,128)(2,1)S(1)} %slice.587), channel_id=1, source_target_pairs={{0,8},{4,12},{8,0},{12,4},{16,24},{20,28},{24,16},{28,20},{1,9},{5... | collective-permute-start | bytes 995336 | tf_op jit(solution)/shard_map/ppermute | solution.py:435
  84.3 22.6 %collective-permute-start.21 = (bf16[3,64,768]{2,1,0:T(8,128)(2,1)S(1)}, bf16[3,64,768]{2,1,0:T(8,128)(2,1)S(1)}, u32[]{:S(2)}, u32[]{:S(2)}) collective-permute-start(bf16[3,64,768]{2,1,0:T(8,128)(2,1)S(1)} %slice.588), channel_id=1, source_target_pairs={{0,16},{4,20},{8,24},{12,28},{16,0},{20,4},{24,8},{28,12},{1,17},{... | collective-permute-start | bytes 884744 | tf_op jit(solution)/shard_map/ppermute | solution.py:435
  86.6 20.4 %collective-permute-start.17 = (bf16[3,136,768]{2,1,0:T(8,128)(2,1)S(1)}, bf16[3,136,768]{2,1,0:T(8,128)(2,1)S(1)}, u32[]{:S(2)}, u32[]{:S(2)}) collective-permute-start(bf16[3,136,768]{2,1,0:T(8,128)(2,1)S(1)} %collective-permute-done.16), channel_id=1, source_target_pairs={{0,4},{4,0},{8,12},{12,8},{16,20},{20,16},{24,28},{28,24},{1,5},{5... | collective-permute-start | bytes 1880072 | tf_op jit(solution)/shard_map/ppermute | solution.py:435
  86.7 21.4 %collective-permute-start.19 = (bf16[3,136,768]{2,1,0:T(8,128)(2,1)S(1)}, bf16[3,136,768]{2,1,0:T(8,128)(2,1)S(1)}, u32[]{:S(2)}, u32[]{:S(2)}) collective-permute-start(bf16[3,136,768]{2,1,0:T(8,128)(2,1)S(1)} %collective-permute-done.18), channel_id=1, source_target_pairs={{0,4},{4,0},{8,12},{12,8},{16,20},{20,16},{24,28},{28,24},{1,5},{5... | collective-permute-start | bytes 1880072 | tf_op jit(solution)/shard_map/ppermute | solution.py:435
  106.9 4.9 %collective-permute-start.22 = (bf16[3,136,768]{2,1,0:T(8,128)(2,1)S(1)}, bf16[3,136,768]{2,1,0:T(8,128)(2,1)S(1)}, u32[]{:S(2)}, u32[]{:S(2)}) collective-permute-start(bf16[3,136,768]{2,1,0:T(8,128)(2,1)S(1)} %constant_dynamic-update-slice_fusion.2), channel_id=1, source_target_pairs={{0,4},{4,0},{8,12},{12,8},{16,20},{20,16},{24,28},{28,24},{1,5},{5... | collective-permute-start | bytes 1880072 | tf_op jit(solution)/shard_map/ppermute | solution.py:435
  113.7 29.4 %copy-start.41 = (bf16[1024,768]{1,0:T(8,128)(2,1)S(1)}, bf16[1024,768]{1,0:T(8,128)(2,1)}, u32[]{:S(2)}) copy-start(bf16[1024,768]{1,0:T(8,128)(2,1)} %og_ref.1) | copy-start | bytes 4718596
  148.5 24.4 %copy-start.19 = (bf16[1024,768]{1,0:T(8,128)(2,1)S(1)}, bf16[1024,768]{1,0:T(8,128)(2,1)}, u32[]{:S(2)}) copy-start(bf16[1024,768]{1,0:T(8,128)(2,1)} %copy-done.18) | copy-start | bytes 4718596
  172.8 8.3 %collective-permute-start.23 = (bf16[64,1536]{1,0:T(8,128)(2,1)S(1)}, bf16[64,1536]{1,0:T(8,128)(2,1)}, u32[]{:S(2)}, u32[]{:S(2)}) collective-permute-start(bf16[64,1536]{1,0:T(8,128)(2,1)S(1)} %slice_select_fusion), channel_id=1, source_target_pairs={{0,1},{1,0},{2,3},{3,2},{4,5},{5,4},{6,7},{7,6},{8,9},{9,8},{10,11... | collective-permute-start | bytes 589832 | tf_op jit(solution)/shard_map/ppermute | solution.py:445
  196.3 24.3 %collective-permute-start.29 = (bf16[4,4,72,768]{3,2,1,0:T(8,128)(2,1)}, bf16[4,4,72,768]{3,2,1,0:T(8,128)(2,1)}, u32[]{:S(2)}, u32[]{:S(2)}) collective-permute-start(bf16[4,4,72,768]{3,2,1,0:T(8,128)(2,1)} %bitcast.88), channel_id=1, source_target_pairs={{0,4},{4,0},{8,12},{12,8},{16,20},{20,16},{24,28},{28,24},{1,5},{5... | collective-permute-start | bytes 5308424 | tf_op jit(solution)/shard_map/ppermute | solution.py:435
  205.2 59.3 %collective-permute-start.45 = (bf16[4,4,136,768]{3,2,1,0:T(8,128)(2,1)}, bf16[4,4,136,768]{3,2,1,0:T(8,128)(2,1)}, u32[]{:S(2)}, u32[]{:S(2)}) collective-permute-start(bf16[4,4,136,768]{3,2,1,0:T(8,128)(2,1)} %pad_maximum_fusion), channel_id=1, source_target_pairs={{0,4},{4,0},{8,12},{12,8},{16,20},{20,16},{24,28},{28,24},{1,5},{5... | collective-permute-start | bytes 10027016 | tf_op jit(solution)/shard_map/ppermute | solution.py:435
  223.7 12.5 %collective-permute-start.30 = (bf16[2,2,72,768]{3,2,1,0:T(8,128)(2,1)S(1)}, bf16[2,2,72,768]{3,2,1,0:T(8,128)(2,1)S(1)}, u32[]{:S(2)}, u32[]{:S(2)}) collective-permute-start(bf16[2,2,72,768]{3,2,1,0:T(8,128)(2,1)S(1)} %dynamic-slice_bitcast_fusion.7), channel_id=1, source_target_pairs={{0,8},{4,12},{8,0},{12,4},{16,24},{20,28},{24,16},{28,20},{1,9},{5... | collective-permute-start | bytes 1327112 | tf_op jit(solution)/shard_map/ppermute | solution.py:435
  224.3 3.9 %collective-permute-start.24 = (f32[8,768]{1,0:T(8,128)S(1)}, f32[8,768]{1,0:T(8,128)S(1)}, u32[]{:S(2)}, u32[]{:S(2)}) collective-permute-start(f32[8,768]{1,0:T(8,128)S(1)} %select_maximum_fusion), channel_id=1, source_target_pairs={{0,1},{1,0},{2,3},{3,2},{4,5},{5,4},{6,7},{7,6},{8,9},{9,8},{10,11... | collective-permute-start | bytes 73736 | tf_op jit(solution)/shard_map/ppermute | solution.py:671
  226.3 12.1 %collective-permute-start.33 = (bf16[2,2,72,768]{3,2,0,1:T(8,128)(2,1)S(1)}, bf16[2,2,72,768]{3,2,0,1:T(8,128)(2,1)S(1)}, u32[]{:S(2)}, u32[]{:S(2)}) collective-permute-start(bf16[2,2,72,768]{3,2,0,1:T(8,128)(2,1)S(1)} %bitcast.460), channel_id=1, source_target_pairs={{0,16},{4,20},{8,24},{12,28},{16,0},{20,4},{24,8},{28,12},{1,17},{... | collective-permute-start | bytes 1327112 | tf_op jit(solution)/shard_map/ppermute | solution.py:435
  228.2 20.4 %collective-permute-start.25 = (f32[8,768]{1,0:T(8,128)S(1)}, f32[8,768]{1,0:T(8,128)S(1)}, u32[]{:S(2)}, u32[]{:S(2)}) collective-permute-start(f32[8,768]{1,0:T(8,128)S(1)} %fusion.48), channel_id=1, source_target_pairs={{0,2},{1,3},{2,0},{3,1},{4,6},{5,7},{6,4},{7,5},{8,10},{9,11},{10,... | collective-permute-start | bytes 73736 | tf_op jit(solution)/shard_map/ppermute | solution.py:671
  236.4 7.0 %collective-permute-start.31 = (bf16[2,72,768]{2,1,0:T(8,128)(2,1)S(1)}, bf16[2,72,768]{2,1,0:T(8,128)(2,1)S(1)}, u32[]{:S(2)}, u32[]{:S(2)}) collective-permute-start(bf16[2,72,768]{2,1,0:T(8,128)(2,1)S(1)} %dynamic-slice_bitcast_fusion.11), channel_id=1, source_target_pairs={{0,16},{4,20},{8,24},{12,28},{16,0},{20,4},{24,8},{28,12},{1,17},{... | collective-permute-start | bytes 663560 | tf_op jit(solution)/shard_map/ppermute | solution.py:435
  238.5 26.0 %copy-start.25 = (bf16[4,4,40,768]{3,2,1,0:T(8,128)(2,1)S(1)}, bf16[4,4,40,768]{3,2,1,0:T(8,128)(2,1)}, u32[]{:S(2)}) copy-start(bf16[4,4,40,768]{3,2,1,0:T(8,128)(2,1)} %get-tuple-element.106) | copy-start | bytes 2949124
  238.5 7.5 %collective-permute-start.34 = (bf16[2,72,768]{2,1,0:T(8,128)(2,1)S(1)}, bf16[2,72,768]{2,1,0:T(8,128)(2,1)S(1)}, u32[]{:S(2)}, u32[]{:S(2)}) collective-permute-start(bf16[2,72,768]{2,1,0:T(8,128)(2,1)S(1)} %dynamic-slice_bitcast_fusion.10), channel_id=1, source_target_pairs={{0,8},{4,12},{8,0},{12,4},{16,24},{20,28},{24,16},{28,20},{1,9},{5... | collective-permute-start | bytes 663560 | tf_op jit(solution)/shard_map/ppermute | solution.py:435
  243.5 14.1 %collective-permute-start.32 = (bf16[72,768]{1,0:T(8,128)(2,1)S(1)}, bf16[72,768]{1,0:T(8,128)(2,1)S(1)}, u32[]{:S(2)}, u32[]{:S(2)}) collective-permute-start(bf16[72,768]{1,0:T(8,128)(2,1)S(1)} %slice_bitcast_fusion.19), channel_id=1, source_target_pairs={{0,3},{1,0},{2,1},{3,2},{4,7},{5,4},{6,5},{7,6},{8,11},{9,8},{10,9... | collective-permute-start | bytes 331784 | tf_op jit(solution)/shard_map/ppermute | solution.py:440
  246.0 11.5 %collective-permute-start.35 = (bf16[72,768]{1,0:T(8,128)(2,1)S(1)}, bf16[72,768]{1,0:T(8,128)(2,1)S(1)}, u32[]{:S(2)}, u32[]{:S(2)}) collective-permute-start(bf16[72,768]{1,0:T(8,128)(2,1)S(1)} %get-tuple-element.150), channel_id=1, source_target_pairs={{0,2},{1,3},{2,0},{3,1},{4,6},{5,7},{6,4},{7,5},{8,10},{9,11},{10,... | collective-permute-start | bytes 331784 | tf_op jit(solution)/shard_map/ppermute | solution.py:440
  247.2 10.3 %collective-permute-start.36 = (bf16[72,768]{1,0:T(8,128)(2,1)S(1)}, bf16[72,768]{1,0:T(8,128)(2,1)S(1)}, u32[]{:S(2)}, u32[]{:S(2)}) collective-permute-start(bf16[72,768]{1,0:T(8,128)(2,1)S(1)} %get-tuple-element.151), channel_id=1, source_target_pairs={{0,1},{1,2},{2,3},{3,0},{4,5},{5,6},{6,7},{7,4},{8,9},{9,10},{10,1... | collective-permute-start | bytes 331784 | tf_op jit(solution)/shard_map/ppermute | solution.py:440
  248.6 1.3 collective-permute-start.26
  249.9 3.8 %collective-permute-start.27 = (f32[8,768]{1,0:T(8,128)S(1)}, f32[8,768]{1,0:T(8,128)S(1)}, u32[]{:S(2)}, u32[]{:S(2)}) collective-permute-start(f32[8,768]{1,0:T(8,128)S(1)} %add.204), channel_id=1, source_target_pairs={{0,8},{4,12},{8,0},{12,4},{16,24},{20,28},{24,16},{28,20},{1,9},{5... | collective-permute-start | bytes 73736 | tf_op jit(solution)/shard_map/ppermute | solution.py:435
  253.7 3.8 %collective-permute-start.28 = (f32[8,768]{1,0:T(8,128)S(1)}, f32[8,768]{1,0:T(8,128)S(1)}, u32[]{:S(2)}, u32[]{:S(2)}) collective-permute-start(f32[8,768]{1,0:T(8,128)S(1)} %add.205), channel_id=1, source_target_pairs={{0,16},{4,20},{8,24},{12,28},{16,0},{20,4},{24,8},{28,12},{1,17},{... | collective-permute-start | bytes 73736 | tf_op jit(solution)/shard_map/ppermute | solution.py:435
  257.6 4.8 %collective-permute-start.40 = (bf16[1,72,768]{2,1,0:T(8,128)(2,1)S(1)}, bf16[1,72,768]{2,1,0:T(8,128)(2,1)S(1)}, u32[]{:S(2)}, u32[]{:S(2)}) collective-permute-start(bf16[1,72,768]{2,1,0:T(8,128)(2,1)S(1)} %bitcast.463), channel_id=1, source_target_pairs={{0,16},{4,20},{8,24},{12,28},{16,0},{20,4},{24,8},{28,12},{1,17},{... | collective-permute-start | bytes 331784 | tf_op jit(solution)/shard_map/ppermute | solution.py:435
  258.2 5.3 %collective-permute-start.38 = (bf16[1,72,768]{2,1,0:T(8,128)(2,1)S(1)}, bf16[1,72,768]{2,1,0:T(8,128)(2,1)S(1)}, u32[]{:S(2)}, u32[]{:S(2)}) collective-permute-start(bf16[1,72,768]{2,1,0:T(8,128)(2,1)S(1)} %bitcast.464), channel_id=1, source_target_pairs={{0,8},{4,12},{8,0},{12,4},{16,24},{20,28},{24,16},{28,20},{1,9},{5... | collective-permute-start | bytes 331784 | tf_op jit(solution)/shard_map/ppermute | solution.py:435
  259.9 8.3 %collective-permute-start.37 = (bf16[1,72,768]{2,1,0:T(8,128)(2,1)S(1)}, bf16[1,72,768]{2,1,0:T(8,128)(2,1)S(1)}, u32[]{:S(2)}, u32[]{:S(2)}) collective-permute-start(bf16[1,72,768]{2,1,0:T(8,128)(2,1)S(1)} %bitcast.465), channel_id=1, source_target_pairs={{0,4},{4,0},{8,12},{12,8},{16,20},{20,16},{24,28},{28,24},{1,5},{5... | collective-permute-start | bytes 331784 | tf_op jit(solution)/shard_map/ppermute | solution.py:435
  262.5 6.6 %collective-permute-start.42 = (bf16[1,40,768]{2,1,0:T(8,128)(2,1)S(1)}, bf16[1,40,768]{2,1,0:T(8,128)(2,1)S(1)}, u32[]{:S(2)}, u32[]{:S(2)}) collective-permute-start(bf16[1,40,768]{2,1,0:T(8,128)(2,1)S(1)} %slice.621), channel_id=1, source_target_pairs={{0,8},{4,12},{8,0},{12,4},{16,24},{20,28},{24,16},{28,20},{1,9},{5... | collective-permute-start | bytes 184328 | tf_op jit(solution)/shard_map/ppermute | solution.py:435
  263.5 5.6 %collective-permute-start.43 = (bf16[1,32,768]{2,1,0:T(8,128)(2,1)S(1)}, bf16[1,32,768]{2,1,0:T(8,128)(2,1)S(1)}, u32[]{:S(2)}, u32[]{:S(2)}) collective-permute-start(bf16[1,32,768]{2,1,0:T(8,128)(2,1)S(1)} %slice.622), channel_id=1, source_target_pairs={{0,16},{4,20},{8,24},{12,28},{16,0},{20,4},{24,8},{28,12},{1,17},{... | collective-permute-start | bytes 147464 | tf_op jit(solution)/shard_map/ppermute | solution.py:435
  267.2 18.5 %collective-permute-start.46 = (bf16[2,2,136,768]{3,2,1,0:T(8,128)(2,1)S(1)}, bf16[2,2,136,768]{3,2,1,0:T(8,128)(2,1)S(1)}, u32[]{:S(2)}, u32[]{:S(2)}) collective-permute-start(bf16[2,2,136,768]{3,2,1,0:T(8,128)(2,1)S(1)} %dynamic-slice_bitcast_fusion.4), channel_id=1, source_target_pairs={{0,8},{4,12},{8,0},{12,4},{16,24},{20,28},{24,16},{28,20},{1,9},{5... | collective-permute-start | bytes 2506760 | tf_op jit(solution)/shard_map/ppermute | solution.py:435
  268.5 2.1 collective-permute-start.41
  268.6 18.0 %collective-permute-start.39 = (bf16[1,72,768]{2,1,0:T(8,128)(2,1)S(1)}, bf16[1,72,768]{2,1,0:T(8,128)(2,1)S(1)}, u32[]{:S(2)}, u32[]{:S(2)}) collective-permute-start(bf16[1,72,768]{2,1,0:T(8,128)(2,1)S(1)} %collective-permute-done.38), channel_id=1, source_target_pairs={{0,4},{4,0},{8,12},{12,8},{16,20},{20,16},{24,28},{28,24},{1,5},{5... | collective-permute-start | bytes 331784 | tf_op jit(solution)/shard_map/ppermute | solution.py:435
  269.1 51.4 %collective-permute-start.44 = (bf16[1,72,768]{2,1,0:T(8,128)(2,1)S(1)}, bf16[1,72,768]{2,1,0:T(8,128)(2,1)S(1)}, u32[]{:S(2)}, u32[]{:S(2)}) collective-permute-start(bf16[1,72,768]{2,1,0:T(8,128)(2,1)S(1)} %constant_dynamic-update-slice_fusion.4), channel_id=1, source_target_pairs={{0,4},{4,0},{8,12},{12,8},{16,20},{20,16},{24,28},{28,24},{1,5},{5... | collective-permute-start | bytes 331784 | tf_op jit(solution)/shard_map/ppermute | solution.py:435
  269.4 21.5 %collective-permute-start.49 = (bf16[2,2,136,768]{3,2,0,1:T(8,128)(2,1)S(1)}, bf16[2,2,136,768]{3,2,0,1:T(8,128)(2,1)S(1)}, u32[]{:S(2)}, u32[]{:S(2)}) collective-permute-start(bf16[2,2,136,768]{3,2,0,1:T(8,128)(2,1)S(1)} %bitcast.450), channel_id=1, source_target_pairs={{0,16},{4,20},{8,24},{12,28},{16,0},{20,4},{24,8},{28,12},{1,17},{... | collective-permute-start | bytes 2506760 | tf_op jit(solution)/shard_map/ppermute | solution.py:435
  286.0 13.4 %collective-permute-start.47 = (bf16[2,136,768]{2,1,0:T(8,128)(2,1)S(1)}, bf16[2,136,768]{2,1,0:T(8,128)(2,1)S(1)}, u32[]{:S(2)}, u32[]{:S(2)}) collective-permute-start(bf16[2,136,768]{2,1,0:T(8,128)(2,1)S(1)} %dynamic-slice_bitcast_fusion.9), channel_id=1, source_target_pairs={{0,16},{4,20},{8,24},{12,28},{16,0},{20,4},{24,8},{28,12},{1,17},{... | collective-permute-start | bytes 1253384 | tf_op jit(solution)/shard_map/ppermute | solution.py:435
  291.1 11.1 %collective-permute-start.50 = (bf16[2,136,768]{2,1,0:T(8,128)(2,1)S(1)}, bf16[2,136,768]{2,1,0:T(8,128)(2,1)S(1)}, u32[]{:S(2)}, u32[]{:S(2)}) collective-permute-start(bf16[2,136,768]{2,1,0:T(8,128)(2,1)S(1)} %dynamic-slice_bitcast_fusion.8), channel_id=1, source_target_pairs={{0,8},{4,12},{8,0},{12,4},{16,24},{20,28},{24,16},{28,20},{1,9},{5... | collective-permute-start | bytes 1253384 | tf_op jit(solution)/shard_map/ppermute | solution.py:435
  299.5 8.4 %collective-permute-start.48 = (bf16[136,768]{1,0:T(8,128)(2,1)S(1)}, bf16[136,768]{1,0:T(8,128)(2,1)S(1)}, u32[]{:S(2)}, u32[]{:S(2)}) collective-permute-start(bf16[136,768]{1,0:T(8,128)(2,1)S(1)} %slice_bitcast_fusion.12), channel_id=1, source_target_pairs={{0,3},{1,0},{2,1},{3,2},{4,7},{5,4},{6,5},{7,6},{8,11},{9,8},{10,9... | collective-permute-start | bytes 626696 | tf_op jit(solution)/shard_map/ppermute | solution.py:440
  302.4 17.9 %collective-permute-start.51 = (bf16[136,768]{1,0:T(8,128)(2,1)S(1)}, bf16[136,768]{1,0:T(8,128)(2,1)S(1)}, u32[]{:S(2)}, u32[]{:S(2)}) collective-permute-start(bf16[136,768]{1,0:T(8,128)(2,1)S(1)} %get-tuple-element.140), channel_id=1, source_target_pairs={{0,2},{1,3},{2,0},{3,1},{4,6},{5,7},{6,4},{7,5},{8,10},{9,11},{10,... | collective-permute-start | bytes 626696 | tf_op jit(solution)/shard_map/ppermute | solution.py:440
  303.2 17.1 %collective-permute-start.52 = (bf16[136,768]{1,0:T(8,128)(2,1)S(1)}, bf16[136,768]{1,0:T(8,128)(2,1)S(1)}, u32[]{:S(2)}, u32[]{:S(2)}) collective-permute-start(bf16[136,768]{1,0:T(8,128)(2,1)S(1)} %get-tuple-element.141), channel_id=1, source_target_pairs={{0,1},{1,2},{2,3},{3,0},{4,5},{5,6},{6,7},{7,4},{8,9},{9,10},{10,1... | collective-permute-start | bytes 626696 | tf_op jit(solution)/shard_map/ppermute | solution.py:440
  320.4 2.4 collective-permute-start.53
  320.6 9.5 %collective-permute-start.54 = (bf16[1,136,768]{2,1,0:T(8,128)(2,1)S(1)}, bf16[1,136,768]{2,1,0:T(8,128)(2,1)S(1)}, u32[]{:S(2)}, u32[]{:S(2)}) collective-permute-start(bf16[1,136,768]{2,1,0:T(8,128)(2,1)S(1)} %bitcast.448), channel_id=1, source_target_pairs={{0,8},{4,12},{8,0},{12,4},{16,24},{20,28},{24,16},{28,20},{1,9},{5... | collective-permute-start | bytes 626696 | tf_op jit(solution)/shard_map/ppermute | solution.py:435
  321.6 7.3 %collective-permute-start.56 = (bf16[1,136,768]{2,1,0:T(8,128)(2,1)S(1)}, bf16[1,136,768]{2,1,0:T(8,128)(2,1)S(1)}, u32[]{:S(2)}, u32[]{:S(2)}) collective-permute-start(bf16[1,136,768]{2,1,0:T(8,128)(2,1)S(1)} %bitcast.449), channel_id=1, source_target_pairs={{0,16},{4,20},{8,24},{12,28},{16,0},{20,4},{24,8},{28,12},{1,17},{... | collective-permute-start | bytes 626696 | tf_op jit(solution)/shard_map/ppermute | solution.py:435
  328.9 4.8 %collective-permute-start.58 = (bf16[1,72,768]{2,1,0:T(8,128)(2,1)S(1)}, bf16[1,72,768]{2,1,0:T(8,128)(2,1)S(1)}, u32[]{:S(2)}, u32[]{:S(2)}) collective-permute-start(bf16[1,72,768]{2,1,0:T(8,128)(2,1)S(1)} %slice.635), channel_id=1, source_target_pairs={{0,8},{4,12},{8,0},{12,4},{16,24},{20,28},{24,16},{28,20},{1,9},{5... | collective-permute-start | bytes 331784 | tf_op jit(solution)/shard_map/ppermute | solution.py:435
  330.1 4.7 %collective-permute-start.59 = (bf16[1,64,768]{2,1,0:T(8,128)(2,1)S(1)}, bf16[1,64,768]{2,1,0:T(8,128)(2,1)S(1)}, u32[]{:S(2)}, u32[]{:S(2)}) collective-permute-start(bf16[1,64,768]{2,1,0:T(8,128)(2,1)S(1)} %slice.636), channel_id=1, source_target_pairs={{0,16},{4,20},{8,24},{12,28},{16,0},{20,4},{24,8},{28,12},{1,17},{... | collective-permute-start | bytes 294920 | tf_op jit(solution)/shard_map/ppermute | solution.py:435
  331.5 3.4 %collective-permute-start.55 = (bf16[1,136,768]{2,1,0:T(8,128)(2,1)S(1)}, bf16[1,136,768]{2,1,0:T(8,128)(2,1)S(1)}, u32[]{:S(2)}, u32[]{:S(2)}) collective-permute-start(bf16[1,136,768]{2,1,0:T(8,128)(2,1)S(1)} %collective-permute-done.54), channel_id=1, source_target_pairs={{0,4},{4,0},{8,12},{12,8},{16,20},{20,16},{24,28},{28,24},{1,5},{5... | collective-permute-start | bytes 626696 | tf_op jit(solution)/shard_map/ppermute | solution.py:435
  331.5 3.5 %collective-permute-start.57 = (bf16[1,136,768]{2,1,0:T(8,128)(2,1)S(1)}, bf16[1,136,768]{2,1,0:T(8,128)(2,1)S(1)}, u32[]{:S(2)}, u32[]{:S(2)}) collective-permute-start(bf16[1,136,768]{2,1,0:T(8,128)(2,1)S(1)} %collective-permute-done.56), channel_id=1, source_target_pairs={{0,4},{4,0},{8,12},{12,8},{16,20},{20,16},{24,28},{28,24},{1,5},{5... | collective-permute-start | bytes 626696 | tf_op jit(solution)/shard_map/ppermute | solution.py:435
  334.8 1.5 collective-permute-start.60
  (41 other events, 182.9 us)

commit v2 on v1

--- a/solution.py
+++ b/solution.py
@@ -1,3 +1,5 @@
+import functools
+
 import jax
 import jax.numpy as jnp
 from jax import lax
@@ -254,6 +256,7 @@
 
 
 def attend_back_kernel(
+    first_pair,
     q_ref,
     k_ref,
     v_ref,
@@ -286,7 +289,7 @@
         dos = stack_pair(do_ref[:, cols], 1.0)
         kb = k_ref[rows, cols]
         vb = v_ref[rows, cols]
-        p = jnp.exp(nt(kb, qs) + bias - lse_ref[0, j : j + 1, :])
+        p = jnp.exp(nt(kb, qs) + bias - lse_ref[0, first_pair + j : first_pair + j + 1, :])
         dp = nt(vb, dos)
         dot = jnp.sum(p * dp, axis=0, keepdims=True)
         ds = (p * (dp - dot)).astype(bf16)
@@ -304,19 +307,20 @@
             edge_ref[HALF:, at : at + width] = ref[ext - HALF :, :].astype(bf16)
 
 
-def attend_back_call(q, k, v, do, bias, lse, cos, sin):
-    ext, width = q.shape
+def attend_back_call(q, k, v, do, bias, lse, cos, sin, at):
+    ext = q.shape[0]
+    width = q.shape[1] // 2
     rows = do.shape[0]
-    full = const_spec((ext, width))
+    full = pl.BlockSpec((ext, width), lambda i: (0, at), pipeline_mode=pl.Buffered(1))
     acc = pl.BlockSpec((ext, width), lambda i: (0, 0))
     return pl.pallas_call(
-        attend_back_kernel,
+        functools.partial(attend_back_kernel, at * (width // 128)),
         grid=(rows // BLK,),
         in_specs=[
             full,
             full,
             full,
-            row_spec(BLK, width),
+            pl.BlockSpec((BLK, width), lambda i: (i, at)),
             pl.BlockSpec((1, 2 * BLK, BLK), lambda i: (i, 0, 0)),
             pl.BlockSpec((1, 8, 2 * BLK), lambda i: (i, 0, 0)),
             const_spec((ext, 128)),
@@ -342,45 +346,59 @@
     )(q, k, v, do, bias, lse, cos, sin)
 
 
-def mixed_kernel(dq_ref, dk_ref, dv_ref, first_ref, last_ref, cos_ref, sin_ref, mix_ref):
-    width = dq_ref.shape[1]
+def mixed_kernel(
+    dq0_ref, dq1_ref, dk0_ref, dk1_ref, dv0_ref, dv1_ref, first_ref, last_ref, cos_ref, sin_ref, mix_ref
+):
+    rows = mix_ref.shape[0]
+    part = dq0_ref.shape[1]
+    width = 2 * part
     i = pl.program_id(0)
-    mix_ref[:, :width] = dq_ref[...]
-    cos = jnp.concatenate([cos_ref[...]] * (width // 128), axis=1)
-    sin = jnp.concatenate([sin_ref[...]] * (width // 128), axis=1)
-    pad = jnp.zeros((dk_ref.shape[0] - HALF, width), f32)
+    own = pl.ds(pl.multiple_of(i * rows, rows) + HALF, rows)
+    cos = jnp.concatenate([cos_ref[own, :]] * (part // 128), axis=1)
+    sin = jnp.concatenate([sin_ref[own, :]] * (part // 128), axis=1)
+    pad = jnp.zeros((rows - HALF, part), f32)
     is_first = (i == 0).astype(f32)
     is_last = (i == pl.num_programs(0) - 1).astype(f32)
 
     def joined(ref, at):
-        cols = slice(at, at + width)
+        cols = slice(at, at + part)
         head = first_ref[:, cols].astype(f32) * is_first
         tail = last_ref[:, cols].astype(f32) * is_last
-        return ref[...] + jnp.concatenate([head, pad], axis=0) + jnp.concatenate([pad, tail], axis=0)
-
-    dk = joined(dk_ref, 0)
-    dv = joined(dv_ref, width)
-    mix_ref[:, width : 2 * width] = (dk * cos + turn_lanes(dk * sin, 1.0)).astype(bf16)
-    mix_ref[:, 2 * width :] = dv.astype(bf16)
-
-
-def mixed_call(dq, dk, dv, first, last, cos, sin):
-    rows, width = dq.shape
+        return ref[own, :] + jnp.concatenate([head, pad], axis=0) + jnp.concatenate([pad, tail], axis=0)
+
+    for h, (dq_ref, dk_ref, dv_ref) in enumerate(
+        ((dq0_ref, dk0_ref, dv0_ref), (dq1_ref, dk1_ref, dv1_ref))
+    ):
+        at = h * part
+        mix_ref[:, at : at + part] = dq_ref[...]
+        dk = joined(dk_ref, at)
+        dk = (dk * cos + turn_lanes(dk * sin, 1.0)).astype(bf16)
+        mix_ref[:, width + at : width + at + part] = dk
+        dv = joined(dv_ref, width + at)
+        mix_ref[:, 2 * width + at : 2 * width + at + part] = dv.astype(bf16)
+
+
+def mixed_call(halves, first, last, cos, sin):
+    (dq0, dk0, dv0), (dq1, dk1, dv1) = halves
+    rows, part = dq0.shape
     blk = 256
+    full = const_spec(dk0.shape)
+    table = const_spec(cos.shape)
     return pl.pallas_call(
         mixed_kernel,
         grid=(rows // blk,),
-        in_specs=[row_spec(blk, width)] * 3
+        in_specs=[row_spec(blk, part)] * 2
+        + [full] * 4
         + [const_spec(first.shape), const_spec(last.shape)]
-        + [row_spec(blk, 128)] * 2,
-        out_specs=row_spec(blk, 3 * width),
-        out_shape=jax.ShapeDtypeStruct((rows, 3 * width), bf16),
+        + [table] * 2,
+        out_specs=row_spec(blk, 6 * part),
+        out_shape=jax.ShapeDtypeStruct((rows, 6 * part), bf16),
         compiler_params=params(32),
         cost_estimate=pl.CostEstimate(
-            flops=10 * rows * width, bytes_accessed=14 * MIB, transcendentals=0
+            flops=20 * rows * part, bytes_accessed=14 * MIB, transcendentals=0
         ),
         name="mixed",
-    )(dq, dk, dv, first, last, cos, sin)
+    )(dq0, dq1, dk0, dk1, dv0, dv1, first, last, cos, sin)
 
 
 def input_grad_kernel(mix_ref, w_ref, x_ref, gmid_ref, gain_ref, out_ref, gain_grad_ref):
@@ -464,22 +482,37 @@
     return jnp.concatenate([a, lax.slice_in_dim(b, size - keep, size, axis=dim)], axis=dim)
 
 
+def hold(value, *after):
+    return lax.optimization_barrier((value,) + after)[0]
+
+
 def spread_quads(piece):
-    rows = piece.shape[1]
-    half = (rows // 2 + 7) // 8 * 8
+    half = (piece.shape[1] // 2 + 7) // 8 * 8
     from_x = dp_swap(piece, XBIT)
     from_y = dp_swap(piece, YBIT)
-    diag = jnp.concatenate(
-        [dp_swap(from_y[:, :half], XBIT), dp_swap(from_x[:, half:], YBIT)], axis=1
-    )
-    mine = [piece, from_x, from_y, diag]
-    return mine, [dp_swap(part, CORE) for part in mine]
-
-
-def gather_pieces(piece):
-    steps = lax.axis_size("tensor")
-    ring = jnp.stack([ring_shift(piece, s) for s in range(1, steps)])
-    return spread_quads(ring)
+    return piece, from_x, from_y, half
+
+
+def spread_diag(piece, from_x, from_y, half):
+    diag_x = dp_swap(from_y[:, :half], XBIT)
+    diag_y = dp_swap(from_x[:, half:], YBIT)
+    early = dp_swap(jnp.stack([piece, from_x, from_y]), CORE)
+    return early, diag_x, diag_y
+
+
+def spread_core(piece, from_x, from_y, early, diag_x, diag_y):
+    diag = jnp.concatenate([diag_x, diag_y], axis=1)
+    late = dp_swap(diag, CORE)
+    return [piece, from_x, from_y, diag], [early[0], early[1], early[2], late]
+
+
+def spread_all(piece):
+    piece, from_x, from_y, half = spread_quads(piece)
+    return spread_core(piece, from_x, from_y, *spread_diag(piece, from_x, from_y, half))
+
+
+def ring_pieces(piece):
+    return jnp.stack([ring_shift(piece, s) for s in range(1, lax.axis_size("tensor"))])
 
 
 def by_core(mine, theirs, core):
@@ -487,27 +520,37 @@
     return jnp.where(first, mine, theirs), jnp.where(first, theirs, mine)
 
 
-def reduce_pieces(send, keep, quad):
-    steps = keep.shape[0]
+def add(a, b):
+    return (a.astype(f32) + b.astype(f32)).astype(bf16)
+
+
+def halve(arr, at, mask, dim):
+    got = dp_swap(index_dim(arr, 1 - at, dim), mask)
+    return index_dim(arr, at, dim), got
+
+
+def reduce_core(send, keep):
+    return add(keep, dp_swap(send, CORE))
+
+
+def reduce_first(total, quad):
+    steps, _, rows, width = total.shape
+    grid = total.reshape(steps, 2, 2, rows, width)
     half = steps // 2
-
-    def add(a, b):
-        return (a.astype(f32) + b.astype(f32)).astype(bf16)
-
-    total = add(keep, dp_swap(send, CORE))
-    rows, width = total.shape[2:]
-    grid = total.reshape(steps, 2, 2, rows, width)
-    x_at, y_at = quad & 1, quad >> 1
-    first, second = grid[:half], grid[half:]
-
-    def halve(arr, at, mask, dim):
-        got = dp_swap(index_dim(arr, 1 - at, dim), mask)
-        return add(index_dim(arr, at, dim), got)
-
-    first = halve(first, x_at, XBIT, 2)
-    second = halve(second, y_at, YBIT, 1)
-    first = halve(first, y_at, YBIT, 1)
-    second = halve(second, x_at, XBIT, 1)
+    return halve(grid[:half], quad & 1, XBIT, 2) + halve(grid[half:], quad >> 1, YBIT, 1)
+
+
+def reduce_second(keep_x, got_x, keep_y, got_y, quad):
+    first = add(keep_x, got_x)
+    second = add(keep_y, got_y)
+    return halve(first, quad >> 1, YBIT, 1) + halve(second, quad & 1, XBIT, 1)
+
+
+def reduce_ring(keep_y, got_y, keep_x, got_x):
+    first = add(keep_y, got_y)
+    second = add(keep_x, got_x)
+    half = first.shape[0]
+    steps = half + second.shape[0]
     parts = [first[s] for s in range(half)] + [second[s] for s in range(steps - half)]
     mask = 8
     if lax.axis_size("dp") > mask:
@@ -516,9 +559,13 @@
             block = add(block, dp_swap(block, mask))
             mask *= 2
         parts = [block[s] for s in range(steps)]
+    return [parts[0]] + [ring_shift(parts[s], -s) for s in range(1, steps)]
+
+
+def reduce_sum(parts):
     result = parts[0].astype(f32)
-    for s in range(1, steps):
-        result = result + ring_shift(parts[s], -s).astype(f32)
+    for part in parts[1:]:
+        result = result + part.astype(f32)
     return result.astype(bf16)
 
 
@@ -580,7 +627,21 @@
     )
 
     own_qkv = core_rows(index_dim(w_qkv, quad, 1), core, 1).reshape(3 * 24, width)
-    mine, theirs = gather_pieces(own_qkv)
+    own_rest = jnp.concatenate(
+        [
+            index_dim(index_dim(w_in, core, 0), quad, 0),
+            core_rows(index_dim(w_out, quad, 0), core, 0),
+            core_rows(index_dim(w_attn, quad, 0), core, 0),
+        ],
+        axis=0,
+    )
+    ring_qkv = ring_pieces(own_qkv)
+    ring_rest = ring_pieces(hold(own_rest, own_qkv))
+
+    quads_qkv = spread_quads(ring_qkv)
+    diag_qkv = spread_diag(*quads_qkv)
+    quads_rest = spread_quads(hold(ring_rest, quads_qkv[1], quads_qkv[2]))
+    mine, theirs = spread_core(*quads_qkv[:3], *diag_qkv)
     qkv_all = jnp.zeros((3, steps, 4, 48, width), bf16)
     qkv_all = qkv_all.at[:, 0].set(w_qkv)
     for n in range(4):
@@ -591,15 +652,14 @@
         qkv_all = put(qkv_all, part, (0, 1, quad ^ n, 0, 0))
     qkv_all = qkv_all.reshape(3, width, width)
 
-    own_rest = jnp.concatenate(
-        [
-            index_dim(index_dim(w_in, core, 0), quad, 0),
-            core_rows(index_dim(w_out, quad, 0), core, 0),
-            core_rows(index_dim(w_attn, quad, 0), core, 0),
-        ],
-        axis=0,
-    )
-    mine, theirs = gather_pieces(own_rest)
+    cos, sin, bias = tables(seg_ids, here * rows, rows)
+    gain_one = norm1_gain[None]
+    gain_two = norm2_gain[None]
+    low_one, q, k, v = qkv_call(x_ext, gain_one, hold(qkv_all, ring_rest), cos, sin)
+    low_attn, lse = attend_call(hold(q, *quads_rest[1:3]), k, v, bias, rows)
+
+    diag_rest = spread_diag(*quads_rest)
+    mine, theirs = spread_core(*quads_rest[:3], *diag_rest)
     in_all = jnp.zeros((2, steps, 4, 72, width), bf16).at[:, 0].set(w_in)
     out_all = jnp.zeros((steps, 4, 72, width), bf16).at[0].set(w_out)
     attn_all = jnp.zeros((steps, 4, 48, width), bf16).at[0].set(w_attn)
@@ -618,11 +678,6 @@
     out_all = out_all.reshape(ff, width)
     attn_all = attn_all.reshape(width, width)
 
-    cos, sin, bias = tables(seg_ids, here * rows, rows)
-    gain_one = norm1_gain[None]
-    gain_two = norm2_gain[None]
-    low_one, q, k, v = qkv_call(x_ext, gain_one, qkv_all, cos, sin)
-    low_attn, lse = attend_call(q, k, v, bias, rows)
     result, grad_mid, low_mid, dattn, low_two, low_act, ggu, gain_two_part = mlp_call(
         hidden_in, out_grad, low_attn, gain_two, attn_all, in_all, out_all
     )
@@ -636,33 +691,56 @@
             [index_dim(g_in, c, 0), core_rows(g_out, c, 2), core_rows(g_attn, c, 2)], axis=2
         )
 
-    rest = reduce_pieces(rest_for(1 - core), rest_for(core), quad)
-
-    dq, dk, dv, edges = attend_back_call(q, k, v, dattn, bias, lse, cos, sin)
+    send, keep = rest_for(1 - core), rest_for(core)
+    dattn = hold(dattn, send)
+    back_first = attend_back_call(q, k, v, dattn, bias, lse, cos, sin, 0)
+    core_rest = reduce_core(send, keep)
+    first_rest = reduce_first(core_rest, quad)
+    dattn = hold(dattn, core_rest, back_first[0])
+    back_second = attend_back_call(q, k, v, dattn, bias, lse, cos, sin, 1)
+    part = width // 2
+    edges = jnp.concatenate(
+        [
+            back_first[3][:, :part],
+            back_second[3][:, :part],
+            back_first[3][:, part:],
+            back_second[3][:, part:],
+        ],
+        axis=1,
+    )
     got = pair_swap(jnp.where(odd, edges[:HALF], edges[HALF:])).reshape(HALF, 2, width)
     turn = width // steps
     got = jnp.where(odd, jnp.roll(got, turn, 2), jnp.roll(got, -turn, 2)).reshape(HALF, 2 * width)
     none = jnp.zeros_like(got)
     own = slice(HALF, HALF + rows)
     mix = mixed_call(
-        dq,
-        dk[own],
-        dv[own],
+        (back_first[:3], back_second[:3]),
         jnp.where(odd, got, none),
         jnp.where(odd, none, got),
-        cos[own],
-        sin[own],
-    )
-    g_qkv = tn(mix, low_one[own]).astype(bf16).reshape(3, steps, 4, 48, width)
+        cos,
+        sin,
+    )
+    g_qkv = tn(mix, low_one[HALF : HALF + rows]).astype(bf16).reshape(3, steps, 4, 48, width)
 
     def qkv_for(c):
         part = core_rows(g_qkv, c, 3).transpose(1, 2, 0, 3, 4)
         return part.reshape(steps, 4, 72, width)
 
-    qkv_total = reduce_pieces(qkv_for(1 - core), qkv_for(core), quad)
+    send_qkv, keep_qkv = qkv_for(1 - core), qkv_for(core)
+    second_rest = reduce_second(*first_rest, quad)
     grad_hidden, gain_one_part = input_grad_call(
-        mix, qkv_all.reshape(3 * width, width), hidden_in, grad_mid, gain_one
-    )
+        hold(mix, send_qkv, *second_rest[::2]),
+        qkv_all.reshape(3 * width, width),
+        hidden_in,
+        grad_mid,
+        gain_one,
+    )
+    core_qkv = reduce_core(send_qkv, keep_qkv)
+    first_qkv = reduce_first(core_qkv, quad)
+    ring_back = reduce_ring(*second_rest)
+    second_qkv = reduce_second(*first_qkv, quad)
+    rest = reduce_sum(ring_back)
+    qkv_total = reduce_sum(reduce_ring(*second_qkv))
 
     gains = jnp.stack([jnp.sum(gain_one_part, axis=0), jnp.sum(gain_two_part, axis=0)])
     gains = jnp.pad(gains, ((0, 6), (0, 0)))
@@ -675,21 +753,20 @@
         gains = gains + dp_swap(gains, mask)
         mask *= 2
 
-    mine, theirs = spread_quads(rest[None])
+    mine, theirs = spread_all(jnp.concatenate([rest, qkv_total])[None])
+    cut = rest.shape[0]
     o_in = jnp.zeros((2, 4, 72, width), f32)
     o_out = jnp.zeros((4, 72, width), f32)
     o_attn = jnp.zeros((4, 48, width), f32)
+    o_qkv = jnp.zeros((3, 4, 48, width), f32)
     for n in range(4):
         a, b = by_core(mine[n][0].astype(f32), theirs[n][0].astype(f32), core)
         o_in = put(o_in, jnp.stack([a[:72], b[:72]])[:, None], (0, quad ^ n, 0, 0))
         o_out = put(o_out, join_cores(a[72:112], b[72:112], 72, 0)[None], (quad ^ n, 0, 0))
-        o_attn = put(o_attn, join_cores(a[112:], b[112:], 48, 0)[None], (quad ^ n, 0, 0))
-    mine, theirs = spread_quads(qkv_total[None])
-    o_qkv = jnp.zeros((3, 4, 48, width), f32)
-    for n in range(4):
-        a, b = by_core(mine[n][0].astype(f32), theirs[n][0].astype(f32), core)
-        part = join_cores(a.reshape(3, 24, width), b.reshape(3, 24, width), 48, 1)
-        o_qkv = put(o_qkv, part[:, None], (0, quad ^ n, 0, 0))
+        o_attn = put(o_attn, join_cores(a[112:cut], b[112:cut], 48, 0)[None], (quad ^ n, 0, 0))
+        a = a[cut:].reshape(3, 24, width)
+        b = b[cut:].reshape(3, 24, width)
+        o_qkv = put(o_qkv, join_cores(a, b, 48, 1)[:, None], (0, quad ^ n, 0, 0))
     grad_qkv = o_qkv.reshape(3, 3, 64, width).transpose(3, 0, 1, 2)
     grad_in = o_in.reshape(2, 288, width).transpose(2, 0, 1)
     return (

time: 344 us -> 320 us (0.930)
  waiting for transfers between devices: 104 us -> 74.2 us
  starting transfers between devices: 58.4 us -> 45.3 us
  local copies, waits for them, and re-layouts: 42.8 us -> 53.3 us
  Pallas kernels: 79.7 us -> 85 us
  other arithmetic: 34.4 us -> 39.4 us
    ppermute x45 -> x31, waiting for transfers between devices: 84.9 us -> 48.8 us  [dp_swap(): return lax.ppermute(x, 'dp', [(i, i ^ mask) for i in range(count)])]
    ppermute x45 -> x31, starting transfers between devices: 31.4 us -> 22 us  [dp_swap(): return lax.ppermute(x, 'dp', [(i, i ^ mask) for i in range(count)])]
    unnamed x94 -> x143, local copies, waits for them, and re-layouts: 15.8 us -> 23.3 us
    convert_element_type x10 -> x11, other arithmetic: 6.31 us -> 13.6 us  [add(): return (a.astype(f32) + b.astype(f32)).astype(bf16)]
    pallas_call x1 -> x2, Pallas kernels: 24.2 us -> 29.6 us  [attend_back_call(): pl.pallas_call(functools.partial(attend_back_kernel, at * (width // 128))...]
    slice x22 -> x19, local copies, waits for them, and re-layouts: 6.35 us -> 1.47 us  [the longest x3 0.97 us: spread_diag(): diag_x = dp_swap(from_y[:, :half], XBIT)]
    squeeze x8 -> x9, local copies, waits for them, and re-layouts: 1.38 us -> 5.94 us  [index_dim(): return lax.squeeze(lax.dynamic_slice_in_dim(x, at, 1, dim), (dim,))]
    ppermute x2, starting transfers between devices: 4.53 us -> 0.81 us  [body(): lax.ppermute(gains, 'tensor', [(i, i ^ mask) for i in range(steps)])]
  transfers between devices with their start and end apart: 61 -> 47, of which waited for: 22 -> 18; matrix products, arithmetic and copies ran while one was open for 17% -> 17% of each run, Pallas kernels for 7% -> 13%
where the time goes in v2:
time: 320 us; the launch traced here: 314 us
  Pallas kernels  85 us (27%)
  waiting for transfers between devices  74.2 us (23%)
  local copies, waits for them, and re-layouts  53.3 us (17%)
  starting transfers between devices  45.3 us (14%)
  other arithmetic  39.4 us (12%)
  matrix products  14.1 us (4%)
    ppermute x31, waiting for transfers between devices, dp_swap(): return lax.ppermute(x, 'dp', [(i, i ^ mask) for i in range(count)])  48.8 us
    pallas_call x2, Pallas kernels, attend_back_call(): pl.pallas_call(functools.partial(attend_back_kernel, at * (width // 128))...  29.6 us
    pallas_call x1, Pallas kernels, mlp_call(): pl.pallas_call(mlp_kernel, grid=(rows // blk,), in_specs=[row_spec(blk, w...  29.5 us
    unnamed x143, local copies, waits for them, and re-layouts  23.3 us
    ppermute x31, starting transfers between devices, dp_swap(): return lax.ppermute(x, 'dp', [(i, i ^ mask) for i in range(count)])  22 us
    ppermute x12, waiting for transfers between devices, ring_shift(): lax.ppermute(x, 'tensor', [(i, (i + step) % count) for i in range(count)])  19.7 us
    ppermute x12, starting transfers between devices, ring_shift(): lax.ppermute(x, 'tensor', [(i, (i + step) % count) for i in range(count)])  17.9 us
    dot_general x4, matrix products, tn(): lax.dot_general(a, b, (((0,), (0,)), ((), ())), preferred_element_type=f32)  14.1 us
  transfers between devices with their start and end apart: 47, of which 18 were waited for; matrix products, arithmetic and copies ran while one was open for 17% of the time, Pallas kernels for 13%

profile of v2, /device:TPU:0, one launch (start us, length us, event | category | flops | bytes accessed | tf_op | source)
XLA Modules:
  0.0 314.0 jit_solution(1320794119917306358)
XLA Ops:
  5.1 3.0 collective-permute-start.10
  8.1 2.6 collective-permute-start.11
  11.0 2.0 collective-permute-start.3
  14.1 3.3 %multiply_sine_fusion = (f32[1152,128]{1,0:T(8,128)}, f32[1152,128]{1,0:T(8,128)}) fusion(f32[128]{0:T(128)S(1)} %pad_maximum_fusion.11, f32[1152]{0:T(1024)S(1)} %fusion.42), kind=kLoop, calls=%fused_computation.28 | loop fusion | flops 147456 | bytes 1184768 | tf_op jit(solution)/shard_map/sin | solution.py:596
  17.4 14.3 %collective-permute-done.2 = bf16[72,768]{1,0:T(8,128)(2,1)S(1)} collective-permute-done((bf16[72,768]{1,0:T(8,128)(2,1)S(1)}, bf16[72,768]{1,0:T(8,128)(2,1)S(1)}, u32[]{:S(2)}, u32[]{:S(2)}) %collective-permute-start.2) | collective-permute-done | bytes 110624 | tf_op jit(solution)/shard_map/ppermute | solution.py:458
  31.7 2.6 collective-permute-start.12
  35.9 1.5 collective-permute-start.5
  37.4 1.3 and_select_fusion.bias_ref
  38.8 1.3 scatter.19
  40.1 2.0 scatter.16
  44.4 1.6 collective-permute-start.4
  48.8 1.2 pad_maximum_fusion.5
  50.0 3.7 %collective-permute-done.4 = bf16[3,72,768]{2,1,0:T(8,128)(2,1)S(1)} collective-permute-done((bf16[3,72,768]{2,1,0:T(8,128)(2,1)}, bf16[3,72,768]{2,1,0:T(8,128)(2,1)S(1)}, u32[]{:S(2)}, u32[]{:S(2)}) %collective-permute-start.4) | collective-permute-done | bytes 331808 | tf_op jit(solution)/shard_map/ppermute | solution.py:453
  53.7 2.4 collective-permute-start.13
  56.1 2.1 collective-permute-start.8
  59.4 9.9 %collective-permute-done.8 = bf16[3,32,768]{2,1,0:T(8,128)(2,1)S(1)} collective-permute-done((bf16[3,32,768]{2,1,0:T(8,128)(2,1)S(1)}, bf16[3,32,768]{2,1,0:T(8,128)(2,1)S(1)}, u32[]{:S(2)}, u32[]{:S(2)}) %collective-permute-start.8) | collective-permute-done | bytes 147488 | tf_op jit(solution)/shard_map/ppermute | solution.py:453
  71.8 8.1 %collective-permute-done.16 = bf16[3,72,768]{2,1,0:T(8,128)(2,1)S(1)} collective-permute-done((bf16[3,72,768]{2,1,0:T(8,128)(2,1)S(1)}, bf16[3,72,768]{2,1,0:T(8,128)(2,1)S(1)}, u32[]{:S(2)}, u32[]{:S(2)}) %collective-permute-start.16) | collective-permute-done | bytes 331808 | tf_op jit(solution)/shard_map/ppermute | solution.py:453
  82.6 6.5 %qkv.1 = (bf16[1152,768]{1,0:T(8,128)(2,1)S(1)}, bf16[1152,768]{1,0:T(8,128)(2,1)S(1)}, bf16[1152,768]{1,0:T(8,128)(2,1)S(1)}, bf16[1152,768]{1,0:T(8,128)(2,1)S(1)}) custom-call(bf16[1152,768]{1,0:T(8,128)(2,1)S(1)} %pad_maximum_fusion.2.x_ref, f32[1,768]{1,0:T(1,128)S(1)} %broadcast_in_dim.146.gain_ref, bf16[3,768,768]{2,1,0:T(8,128)(2,1)S(1)} %bitcast.459, ...), custom_call_target="tpu_custom_call" | custom-call | flops 4076863488 | bytes 14680064 | tf_op jit(solution)/shard_map/qkv/pallas_call | solution.py:86
  89.1 1.2 copy-done.30
  90.4 9.8 %attend.1 = (bf16[1024,768]{1,0:T(8,128)(2,1)S(1)}, f32[8,8,256]{2,1,0:T(8,128)S(1)}) custom-call(bf16[1152,768]{1,0:T(8,128)(2,1)S(1)} %get-tuple-element.91.q_ref, bf16[1152,768]{1,0:T(8,128)(2,1)S(1)} %get-tuple-element.92.k_ref, bf16[1152,768]{1,0:T(8,128)(2,1)S(1)} %get-tuple-element.93.v_ref, f32[8,256,128]{2,1,0:T(8,128)S(1)} %copy-done.14), custom_call_target="tpu_custom_call" | custom-call | flops 2415919104 | bytes 9437184 | tf_op jit(solution)/shard_map/attend/pallas_call | solution.py:141
  108.9 29.5 %mlp.1 = (bf16[1024,768]{1,0:T(8,128)(2,1)}, f32[1024,768]{1,0:T(8,128)}, bf16[1024,768]{1,0:T(8,128)(2,1)S(1)}, bf16[1024,768]{1,0:T(8,128)(2,1)S(1)}, bf16[102...) custom-call(bf16[1024,768]{1,0:T(8,128)(2,1)} %x_ref.3, ...), custom_call_target="tpu_custom_call" | custom-call | flops 13287555072 | bytes 31457280 | tf_op jit(solution)/shard_map/mlp/pallas_call | solution.py:231
  138.4 4.3 %convolution_convert_fusion.2 = bf16[1152,768]{1,0:T(8,128)(2,1)S(1)} fusion(bf16[1024,1152]{1,0:T(8,128)(2,1)} %get-tuple-element.99, bf16[1024,768]{1,0:T(8,128)(2,1)S(1)} %copy-done.65), kind=kOutput, calls=%fused_computation.5 | convolution fusion | flops 1812824064 | bytes 5701632 | tf_op jit(solution)/shard_map/dot_general | solution.py:30
  142.8 1.5 convolution_convert_fusion.3
  145.2 4.2 %convolution_convert_fusion.1 = bf16[2304,768]{1,0:T(8,128)(2,1)S(1)} fusion(bf16[1024,2304]{1,0:T(8,128)(2,1)S(1)} %copy-done.66, bf16[1024,768]{1,0:T(8,128)(2,1)S(1)} %get-tuple-element.98), kind=kOutput, calls=%fused_computation.2 | convolution fusion | flops 3625648128 | bytes 9830400 | tf_op jit(solution)/shard_map/dot_general | solution.py:30
  149.3 1.5 dynamic-slice_bitcast_fusion.1
  152.7 1.8 pad_maximum_fusion
  157.2 1.2 copy-done.15
  158.4 1.4 copy-done.27
  160.7 14.3 %attend_back.2 = (bf16[1024,384]{1,0:T(8,128)(2,1)S(1)}, f32[1152,384]{1,0:T(8,128)}, f32[1152,384]{1,0:T(8,128)}, bf16[128,768]{1,0:T(8,128)(2,1)S(1)}) custom-call(bf16[1152,768]{1,0:T(8,128)(2,1)} %copy-done.23, bf16[1152,768]{1,0:T(8,128)(2,1)} %copy-done.24, bf16[1152,768]{1,0:T(8,128)(2,1)} %copy-done.25, bf16[1024,768]{1,0:T(8,128)(2,1)S(1)} %copy-done.27, ...), custom_call_target="tpu_custom_call" | custom-call | flops 3019898880 | bytes 20971520 | tf_op jit(solution)/shard_map/attend_back/pallas_call | solution.py:316
  175.0 2.6 add_convert_fusion
  177.9 15.3 %attend_back.3 = (bf16[1024,384]{1,0:T(8,128)(2,1)S(1)}, f32[1152,384]{1,0:T(8,128)}, f32[1152,384]{1,0:T(8,128)}, bf16[128,768]{1,0:T(8,128)(2,1)S(1)}) custom-call(bf16[1152,768]{1,0:T(8,128)(2,1)} %copy-done.23, bf16[1152,768]{1,0:T(8,128)(2,1)} %copy-done.24, bf16[1152,768]{1,0:T(8,128)(2,1)} %copy-done.25, bf16[1024,768]{1,0:T(8,128)(2,1)S(1)} %copy-done.27, ...), custom_call_target="tpu_custom_call" | custom-call | flops 3019898880 | bytes 20971520 | tf_op jit(solution)/shard_map/attend_back/pallas_call | solution.py:316
  193.3 4.2 %collective-permute-start.20 = (bf16[64,1536]{1,0:T(8,128)(2,1)S(1)}, bf16[64,1536]{1,0:T(8,128)(2,1)}, u32[]{:S(2)}, u32[]{:S(2)}) collective-permute-start(bf16[64,1536]{1,0:T(8,128)(2,1)S(1)} %slice_select_fusion), channel_id=1, source_target_pairs={{0,1},{1,0},{2,3},{3,2},{4,5},{5,4},{6,7},{7,6},{8,9},{9,8},{10,11... | collective-permute-start | bytes 589832 | tf_op jit(solution)/shard_map/ppermute | solution.py:463
  200.9 1.8 collective-permute-done.20
  202.7 1.7 reshape.463
  204.4 1.5 fusion.55
  207.8 1.5 copy-done.10
  209.3 1.5 copy-done.11
  210.8 1.5 copy-done.12
  214.5 2.9 mixed.1.mix_ref
  217.4 4.2 %convolution_convert_fusion = bf16[2304,768]{1,0:T(8,128)(2,1)S(1)} fusion(bf16[1024,2304]{1,0:T(8,128)(2,1)S(1)} %mixed.1.mix_ref, bf16[1152,768]{1,0:T(8,128)(2,1)S(1)} %copy-done.31), kind=kOutput, calls=%fused_computation.1 | convolution fusion | flops 3625648128 | bytes 9830400 | tf_op jit(solution)/shard_map/dot_general | solution.py:30
  221.6 2.3 bitcast_convert_fusion
  223.9 1.3 copy.74
  226.0 1.4 fusion.1
  230.8 2.4 copy.75
  233.3 1.4 fusion.2
  235.4 5.3 %collective-permute-done.30 = bf16[2,136,768]{2,1,0:T(8,128)(2,1)} collective-permute-done((bf16[2,136,768]{2,1,0:T(8,128)(2,1)}, bf16[2,136,768]{2,1,0:T(8,128)(2,1)}, u32[]{:S(2)}, u32[]{:S(2)}) %collective-permute-start.30) | collective-permute-done | bytes 417824 | tf_op jit(solution)/shard_map/ppermute | solution.py:453
  242.6 1.7 collective-permute-start.32
  244.3 1.6 collective-permute-done.28
  247.6 2.1 fusion
  253.8 6.7 %input_grad.1 = (bf16[1024,768]{1,0:T(8,128)(2,1)}, f32[8,768]{1,0:T(8,128)S(1)}) custom-call(bf16[1024,2304]{1,0:T(8,128)(2,1)S(1)} %bitcast.458, bf16[2304,768]{1,0:T(8,128)(2,1)S(1)} %bitcast.460, bf16[1024,768]{1,0:T(8,128)(2,1)S(1)} %copy-done.8, f32[1024,768]{1,0:T(8,128)S(1)} %copy-done.22, f32[1,768]{1,0:T(1,128)S(1)} %broadcast_in_dim.146.gain_ref), custom_call_target="tpu_custom_call" | custom-call | flops 3623878656 | bytes 16777216 | tf_op jit(solution)/shard_map/input_grad/pallas_call | solution.py:428
  261.9 1.3 fusion.5
  263.2 1.6 collective-permute-start.35
  267.1 2.1 collective-permute-done.35
  269.3 2.1 collective-permute-start.36
  272.1 2.5 collective-permute-start.39
  274.7 1.2 fusion.22
  276.0 3.4 %collective-permute-done.39 = bf16[72,768]{1,0:T(8,128)(2,1)S(1)} collective-permute-done((bf16[72,768]{1,0:T(8,128)(2,1)S(1)}, bf16[72,768]{1,0:T(8,128)(2,1)S(1)}, u32[]{:S(2)}, u32[]{:S(2)}) %collective-permute-start.39) | collective-permute-done | bytes 110624 | tf_op jit(solution)/shard_map/ppermute | solution.py:458
  279.4 2.0 collective-permute-done.40
  282.9 3.8 %collective-permute-done.23 = f32[8,768]{1,0:T(8,128)S(1)} collective-permute-done((f32[8,768]{1,0:T(8,128)S(1)}, f32[8,768]{1,0:T(8,128)S(1)}, u32[]{:S(2)}, u32[]{:S(2)}) %collective-permute-start.23) | collective-permute-done | bytes 24608 | tf_op jit(solution)/shard_map/ppermute | solution.py:749
  287.5 3.8 %collective-permute-done.42 = bf16[1,208,768]{2,1,0:T(8,128)(2,1)S(1)} collective-permute-done((bf16[1,208,768]{2,1,0:T(8,128)(2,1)S(1)}, bf16[1,208,768]{2,1,0:T(8,128)(2,1)S(1)}, u32[]{:S(2)}, u32[]{:S(2)}) %collective-permute-start.42) | collective-permute-done | bytes 319520 | tf_op jit(solution)/shard_map/ppermute | solution.py:453
  292.8 3.9 %collective-permute-done.44 = bf16[1,104,768]{2,1,0:T(8,128)(2,1)S(1)} collective-permute-done((bf16[1,104,768]{2,1,0:T(8,128)(2,1)S(1)}, bf16[1,104,768]{2,1,0:T(8,128)(2,1)S(1)}, u32[]{:S(2)}, u32[]{:S(2)}) %collective-permute-start.44) | collective-permute-done | bytes 159776 | tf_op jit(solution)/shard_map/ppermute | solution.py:453
  299.0 2.8 collective-permute-done.26
  302.0 3.6 %collective-permute-done.27 = f32[8,768]{1,0:T(8,128)S(1)} collective-permute-done((f32[8,768]{1,0:T(8,128)S(1)}, f32[8,768]{1,0:T(8,128)S(1)}, u32[]{:S(2)}, u32[]{:S(2)}) %collective-permute-start.27) | collective-permute-done | bytes 24608 | tf_op jit(solution)/shard_map/ppermute | solution.py:453
  306.6 2.3 collective-permute-done.43
  (374 shorter events, 70.0 us)
Async XLA Ops:
  0.6 12.5 %copy-start.62 = (s32[4096]{0:T(1024)S(1)}, s32[4096]{0:T(1024)}, u32[]{:S(2)}) copy-start(s32[4096]{0:T(1024)} %param.18) | copy-start | bytes 49156
  5.1 43.1 %collective-permute-start.10 = (bf16[136,768]{1,0:T(8,128)(2,1)}, bf16[136,768]{1,0:T(8,128)(2,1)}, u32[]{:S(2)}, u32[]{:S(2)}) collective-permute-start(bf16[136,768]{1,0:T(8,128)(2,1)} %pad_maximum_fusion.10), channel_id=1, source_target_pairs={{0,1},{1,2},{2,3},{3,0},{4,5},{5,6},{6,7},{7,4},{8,9},{9,10},{10,1... | collective-permute-start | bytes 626696 | tf_op jit(solution)/shard_map/ppermute | solution.py:458
  8.1 40.7 %collective-permute-start.11 = (bf16[136,768]{1,0:T(8,128)(2,1)}, bf16[136,768]{1,0:T(8,128)(2,1)}, u32[]{:S(2)}, u32[]{:S(2)}) collective-permute-start(bf16[136,768]{1,0:T(8,128)(2,1)} %pad_maximum_fusion.10), channel_id=1, source_target_pairs={{0,2},{1,3},{2,0},{3,1},{4,6},{5,7},{6,4},{7,5},{8,10},{9,11},{10,... | collective-permute-start | bytes 626696 | tf_op jit(solution)/shard_map/ppermute | solution.py:458
  10.7 21.0 %collective-permute-start.2 = (bf16[72,768]{1,0:T(8,128)(2,1)S(1)}, bf16[72,768]{1,0:T(8,128)(2,1)S(1)}, u32[]{:S(2)}, u32[]{:S(2)}) collective-permute-start(bf16[72,768]{1,0:T(8,128)(2,1)S(1)} %bitcast.519), channel_id=1, source_target_pairs={{0,2},{1,3},{2,0},{3,1},{4,6},{5,7},{6,4},{7,5},{8,10},{9,11},{10,... | collective-permute-start | bytes 331784 | tf_op jit(solution)/shard_map/ppermute | solution.py:458
  11.0 23.3 %collective-permute-start.3 = (bf16[72,768]{1,0:T(8,128)(2,1)S(1)}, bf16[72,768]{1,0:T(8,128)(2,1)S(1)}, u32[]{:S(2)}, u32[]{:S(2)}) collective-permute-start(bf16[72,768]{1,0:T(8,128)(2,1)S(1)} %bitcast.520), channel_id=1, source_target_pairs={{0,3},{1,0},{2,1},{3,2},{4,7},{5,4},{6,5},{7,6},{8,11},{9,8},{10,9... | collective-permute-start | bytes 331784 | tf_op jit(solution)/shard_map/ppermute | solution.py:458
  13.1 21.3 %collective-permute-start.1 = (bf16[72,768]{1,0:T(8,128)(2,1)S(1)}, bf16[72,768]{1,0:T(8,128)(2,1)S(1)}, u32[]{:S(2)}, u32[]{:S(2)}) collective-permute-start(bf16[72,768]{1,0:T(8,128)(2,1)S(1)} %bitcast.521), channel_id=1, source_target_pairs={{0,1},{1,2},{2,3},{3,0},{4,5},{5,6},{6,7},{7,4},{8,9},{9,10},{10,1... | collective-permute-start | bytes 331784 | tf_op jit(solution)/shard_map/ppermute | solution.py:458
  13.5 25.2 %copy-start.53 = (bf16[288,768]{1,0:T(8,128)(2,1)S(1)}, bf16[288,768]{1,0:T(8,128)(2,1)}, u32[]{:S(2)}) copy-start(bf16[288,768]{1,0:T(8,128)(2,1)} %param.24) | copy-start | bytes 1327108
  31.7 17.1 %collective-permute-start.12 = (bf16[136,768]{1,0:T(8,128)(2,1)}, bf16[136,768]{1,0:T(8,128)(2,1)}, u32[]{:S(2)}, u32[]{:S(2)}) collective-permute-start(bf16[136,768]{1,0:T(8,128)(2,1)} %pad_maximum_fusion.10), channel_id=1, source_target_pairs={{0,3},{1,0},{2,1},{3,2},{4,7},{5,4},{6,5},{7,6},{8,11},{9,8},{10,9... | collective-permute-start | bytes 626696 | tf_op jit(solution)/shard_map/ppermute | solution.py:458
  35.9 11.0 %collective-permute-start.5 = (bf16[3,72,768]{2,1,0:T(8,128)(2,1)}, bf16[3,72,768]{2,1,0:T(8,128)(2,1)}, u32[]{:S(2)}, u32[]{:S(2)}) collective-permute-start(bf16[3,72,768]{2,1,0:T(8,128)(2,1)} %get-tuple-element.193), channel_id=1, source_target_pairs={{0,16},{4,20},{8,24},{12,28},{16,0},{20,4},{24,8},{28,12},{1,17},{... | collective-permute-start | bytes 995336 | tf_op jit(solution)/shard_map/ppermute | solution.py:453
  44.4 13.8 %copy-start.50 = (bf16[1,3,72,768]{3,2,1,0:T(8,128)(2,1)S(1)}, bf16[1,3,72,768]{3,2,1,0:T(8,128)(2,1)}, u32[]{:S(2)}) copy-start(bf16[1,3,72,768]{3,2,1,0:T(8,128)(2,1)} %get-tuple-element.192) | copy-start | bytes 995332
  44.4 9.3 %collective-permute-start.4 = (bf16[3,72,768]{2,1,0:T(8,128)(2,1)}, bf16[3,72,768]{2,1,0:T(8,128)(2,1)S(1)}, u32[]{:S(2)}, u32[]{:S(2)}) collective-permute-start(bf16[3,72,768]{2,1,0:T(8,128)(2,1)} %get-tuple-element.193), channel_id=1, source_target_pairs={{0,8},{4,12},{8,0},{12,4},{16,24},{20,28},{24,16},{28,20},{1,9},{5... | collective-permute-start | bytes 995336 | tf_op jit(solution)/shard_map/ppermute | solution.py:453
  46.9 22.5 %collective-permute-start = (bf16[64,768]{1,0:T(8,128)(2,1)S(1)}, bf16[64,768]{1,0:T(8,128)(2,1)S(1)}, u32[]{:S(2)}, u32[]{:S(2)}) collective-permute-start(bf16[64,768]{1,0:T(8,128)(2,1)S(1)} %slice_select_fusion.1), channel_id=1, source_target_pairs={{0,1},{1,0},{2,3},{3,2},{4,5},{5,4},{6,7},{7,6},{8,9},{9,8},{10,11... | collective-permute-start | bytes 294920 | tf_op jit(solution)/shard_map/ppermute | solution.py:463
  48.2 11.1 %collective-permute-start.7 = (bf16[3,40,768]{2,1,0:T(8,128)(2,1)S(1)}, bf16[3,40,768]{2,1,0:T(8,128)(2,1)S(1)}, u32[]{:S(2)}, u32[]{:S(2)}) collective-permute-start(bf16[3,40,768]{2,1,0:T(8,128)(2,1)S(1)} %slice.606), channel_id=1, source_target_pairs={{0,8},{4,12},{8,0},{12,4},{16,24},{20,28},{24,16},{28,20},{1,9},{5... | collective-permute-start | bytes 552968 | tf_op jit(solution)/shard_map/ppermute | solution.py:453
  50.0 19.4 %copy-start.7 = (bf16[1024,768]{1,0:T(8,128)(2,1)S(1)}, bf16[1024,768]{1,0:T(8,128)(2,1)}, u32[]{:S(2)}) copy-start(bf16[1024,768]{1,0:T(8,128)(2,1)} %x_ref.3) | copy-start | bytes 4718596
  53.7 16.5 %collective-permute-start.13 = (bf16[3,136,768]{2,1,0:T(8,128)(2,1)S(1)}, bf16[3,136,768]{2,1,0:T(8,128)(2,1)S(1)}, u32[]{:S(2)}, u32[]{:S(2)}) collective-permute-start(bf16[3,136,768]{2,1,0:T(8,128)(2,1)S(1)} %pad_maximum_fusion.5), channel_id=1, source_target_pairs={{0,8},{4,12},{8,0},{12,4},{16,24},{20,28},{24,16},{28,20},{1,9},{5... | collective-permute-start | bytes 1880072 | tf_op jit(solution)/shard_map/ppermute | solution.py:453
  56.1 13.5 %collective-permute-start.14 = (bf16[3,136,768]{2,1,0:T(8,128)(2,1)S(1)}, bf16[3,136,768]{2,1,0:T(8,128)(2,1)S(1)}, u32[]{:S(2)}, u32[]{:S(2)}) collective-permute-start(bf16[3,136,768]{2,1,0:T(8,128)(2,1)S(1)} %pad_maximum_fusion.5), channel_id=1, source_target_pairs={{0,16},{4,20},{8,24},{12,28},{16,0},{20,4},{24,8},{28,12},{1,17},{... | collective-permute-start | bytes 1880072 | tf_op jit(solution)/shard_map/ppermute | solution.py:453
  56.1 13.2 %collective-permute-start.8 = (bf16[3,32,768]{2,1,0:T(8,128)(2,1)S(1)}, bf16[3,32,768]{2,1,0:T(8,128)(2,1)S(1)}, u32[]{:S(2)}, u32[]{:S(2)}) collective-permute-start(bf16[3,32,768]{2,1,0:T(8,128)(2,1)S(1)} %slice.607), channel_id=1, source_target_pairs={{0,16},{4,20},{8,24},{12,28},{16,0},{20,4},{24,8},{28,12},{1,17},{... | collective-permute-start | bytes 442376 | tf_op jit(solution)/shard_map/ppermute | solution.py:453
  59.3 20.7 %collective-permute-start.6 = (bf16[3,3,72,768]{3,2,1,0:T(8,128)(2,1)S(1)}, bf16[3,3,72,768]{3,2,1,0:T(8,128)(2,1)S(1)}, u32[]{:S(2)}, u32[]{:S(2)}) collective-permute-start(bf16[3,3,72,768]{3,2,1,0:T(8,128)(2,1)S(1)} %pad_maximum_fusion.3), channel_id=1, source_target_pairs={{0,4},{4,0},{8,12},{12,8},{16,20},{20,16},{24,28},{28,24},{1,5},{5... | collective-permute-start | bytes 2985992 | tf_op jit(solution)/shard_map/ppermute | solution.py:453
  69.3 2.1 collective-permute-start.9
  69.6 10.3 %collective-permute-start.16 = (bf16[3,72,768]{2,1,0:T(8,128)(2,1)S(1)}, bf16[3,72,768]{2,1,0:T(8,128)(2,1)S(1)}, u32[]{:S(2)}, u32[]{:S(2)}) collective-permute-start(bf16[3,72,768]{2,1,0:T(8,128)(2,1)S(1)} %slice.619), channel_id=1, source_target_pairs={{0,8},{4,12},{8,0},{12,4},{16,24},{20,28},{24,16},{28,20},{1,9},{5... | collective-permute-start | bytes 995336 | tf_op jit(solution)/shard_map/ppermute | solution.py:453
  70.3 9.7 %collective-permute-start.17 = (bf16[3,64,768]{2,1,0:T(8,128)(2,1)S(1)}, bf16[3,64,768]{2,1,0:T(8,128)(2,1)S(1)}, u32[]{:S(2)}, u32[]{:S(2)}) collective-permute-start(bf16[3,64,768]{2,1,0:T(8,128)(2,1)S(1)} %slice.620), channel_id=1, source_target_pairs={{0,16},{4,20},{8,24},{12,28},{16,0},{20,4},{24,8},{28,12},{1,17},{... | collective-permute-start | bytes 884744 | tf_op jit(solution)/shard_map/ppermute | solution.py:453
  71.7 8.4 %copy-start.57 = (bf16[72,768]{1,0:T(8,128)(2,1)S(1)}, bf16[72,768]{1,0:T(8,128)(2,1)}, u32[]{:S(2)}) copy-start(bf16[72,768]{1,0:T(8,128)(2,1)} %copy-done.56) | copy-start | bytes 331780
  71.7 8.4 %copy-start.59 = (bf16[72,768]{1,0:T(8,128)(2,1)S(1)}, bf16[72,768]{1,0:T(8,128)(2,1)}, u32[]{:S(2)}) copy-start(bf16[72,768]{1,0:T(8,128)(2,1)} %copy-done.58) | copy-start | bytes 331780
  71.7 8.4 %copy-start.61 = (bf16[72,768]{1,0:T(8,128)(2,1)S(1)}, bf16[72,768]{1,0:T(8,128)(2,1)}, u32[]{:S(2)}) copy-start(bf16[72,768]{1,0:T(8,128)(2,1)} %copy-done.60) | copy-start | bytes 331780
  71.7 29.7 %collective-permute-start.15 = (bf16[3,3,136,768]{3,2,1,0:T(8,128)(2,1)S(1)}, bf16[3,3,136,768]{3,2,1,0:T(8,128)(2,1)S(1)}, u32[]{:S(2)}, u32[]{:S(2)}) collective-permute-start(bf16[3,3,136,768]{3,2,1,0:T(8,128)(2,1)S(1)} %pad_maximum_fusion.1), channel_id=1, source_target_pairs={{0,4},{4,0},{8,12},{12,8},{16,20},{20,16},{24,28},{28,24},{1,5},{5... | collective-permute-start | bytes 5640200 | tf_op jit(solution)/shard_map/ppermute | solution.py:453
  79.9 20.3 %collective-permute-start.18 = (bf16[3,136,768]{2,1,0:T(8,128)(2,1)S(1)}, bf16[3,136,768]{2,1,0:T(8,128)(2,1)S(1)}, u32[]{:S(2)}, u32[]{:S(2)}) collective-permute-start(bf16[3,136,768]{2,1,0:T(8,128)(2,1)S(1)} %constant_dynamic-update-slice_fusion.2), channel_id=1, source_target_pairs={{0,4},{4,0},{8,12},{12,8},{16,20},{20,16},{24,28},{28,24},{1,5},{5... | collective-permute-start | bytes 1880072 | tf_op jit(solution)/shard_map/ppermute | solution.py:453
  90.4 9.8 %copy-start.23 = (bf16[1152,768]{1,0:T(8,128)(2,1)}, bf16[1152,768]{1,0:T(8,128)(2,1)S(1)}, u32[]{:S(2)}) copy-start(bf16[1152,768]{1,0:T(8,128)(2,1)S(1)} %get-tuple-element.91.q_ref) | copy-start | bytes 5308420
  90.4 9.8 %copy-start.24 = (bf16[1152,768]{1,0:T(8,128)(2,1)}, bf16[1152,768]{1,0:T(8,128)(2,1)S(1)}, u32[]{:S(2)}) copy-start(bf16[1152,768]{1,0:T(8,128)(2,1)S(1)} %get-tuple-element.92.k_ref) | copy-start | bytes 5308420
  90.4 9.8 %copy-start.25 = (bf16[1152,768]{1,0:T(8,128)(2,1)}, bf16[1152,768]{1,0:T(8,128)(2,1)S(1)}, u32[]{:S(2)}) copy-start(bf16[1152,768]{1,0:T(8,128)(2,1)S(1)} %get-tuple-element.93.v_ref) | copy-start | bytes 5308420
  108.8 29.6 %copy-start.65 = (bf16[1024,768]{1,0:T(8,128)(2,1)S(1)}, bf16[1024,768]{1,0:T(8,128)(2,1)}, u32[]{:S(2)}) copy-start(bf16[1024,768]{1,0:T(8,128)(2,1)} %og_ref.1) | copy-start | bytes 4718596
  154.6 20.4 %collective-permute-start.19 = (bf16[4,4,136,768]{3,2,1,0:T(8,128)(2,1)}, bf16[4,4,136,768]{3,2,1,0:T(8,128)(2,1)}, u32[]{:S(2)}, u32[]{:S(2)}) collective-permute-start(bf16[4,4,136,768]{3,2,1,0:T(8,128)(2,1)} %pad_maximum_fusion), channel_id=1, source_target_pairs={{0,4},{4,0},{8,12},{12,8},{16,20},{20,16},{24,28},{28,24},{1,5},{5... | collective-permute-start | bytes 10027016 | tf_op jit(solution)/shard_map/ppermute | solution.py:453
  160.7 14.3 %copy-start.34 = (bf16[4,4,72,768]{3,2,1,0:T(8,128)(2,1)S(1)}, bf16[4,4,72,768]{3,2,1,0:T(8,128)(2,1)}, u32[]{:S(2)}) copy-start(bf16[4,4,72,768]{3,2,1,0:T(8,128)(2,1)} %get-tuple-element.128) | copy-start | bytes 5308420
  160.7 14.3 %copy-start.39 = (bf16[4,4,40,768]{3,2,1,0:T(8,128)(2,1)S(1)}, bf16[4,4,40,768]{3,2,1,0:T(8,128)(2,1)}, u32[]{:S(2)}) copy-start(bf16[4,4,40,768]{3,2,1,0:T(8,128)(2,1)} %get-tuple-element.144) | copy-start | bytes 2949124
  160.7 14.3 %copy-start.43 = (bf16[4,4,24,768]{3,2,1,0:T(8,128)(2,1)S(1)}, bf16[4,4,24,768]{3,2,1,0:T(8,128)(2,1)}, u32[]{:S(2)}) copy-start(bf16[4,4,24,768]{3,2,1,0:T(8,128)(2,1)} %get-tuple-element.158) | copy-start | bytes 1769476
  177.9 19.6 %copy-start.37 = (bf16[2,4,136,768]{3,2,1,0:T(8,128)(2,1)}, bf16[2,4,136,768]{3,2,1,0:T(8,128)(2,1)S(1)}, u32[]{:S(2)}) copy-start(bf16[2,4,136,768]{3,2,1,0:T(8,128)(2,1)S(1)} %get-tuple-element.130) | copy-start | bytes 5013508
  177.9 21.1 %copy-start.35 = (bf16[2,4,136,768]{3,2,1,0:T(8,128)(2,1)}, bf16[2,4,136,768]{3,2,1,0:T(8,128)(2,1)S(1)}, u32[]{:S(2)}) copy-start(bf16[2,4,136,768]{3,2,1,0:T(8,128)(2,1)S(1)} %get-tuple-element.131) | copy-start | bytes 5013508
  193.3 9.4 %collective-permute-start.20 = (bf16[64,1536]{1,0:T(8,128)(2,1)S(1)}, bf16[64,1536]{1,0:T(8,128)(2,1)}, u32[]{:S(2)}, u32[]{:S(2)}) collective-permute-start(bf16[64,1536]{1,0:T(8,128)(2,1)S(1)} %slice_select_fusion), channel_id=1, source_target_pairs={{0,1},{1,0},{2,3},{3,2},{4,5},{5,4},{6,7},{7,6},{8,9},{9,8},{10,11... | collective-permute-start | bytes 589832 | tf_op jit(solution)/shard_map/ppermute | solution.py:463
  198.4 26.8 %collective-permute-start.22 = (bf16[2,2,136,768]{3,2,1,0:T(8,128)(2,1)}, bf16[2,2,136,768]{3,2,1,0:T(8,128)(2,1)}, u32[]{:S(2)}, u32[]{:S(2)}) collective-permute-start(bf16[2,2,136,768]{3,2,1,0:T(8,128)(2,1)} %dynamic-slice_bitcast_fusion.5), channel_id=1, source_target_pairs={{0,16},{4,20},{8,24},{12,28},{16,0},{20,4},{24,8},{28,12},{1,17},{... | collective-permute-start | bytes 2506760 | tf_op jit(solution)/shard_map/ppermute | solution.py:453
  199.9 33.3 %collective-permute-start.21 = (bf16[2,2,136,768]{3,2,1,0:T(8,128)(2,1)}, bf16[2,2,136,768]{3,2,1,0:T(8,128)(2,1)}, u32[]{:S(2)}, u32[]{:S(2)}) collective-permute-start(bf16[2,2,136,768]{3,2,1,0:T(8,128)(2,1)} %dynamic-slice_bitcast_fusion.6), channel_id=1, source_target_pairs={{0,8},{4,12},{8,0},{12,4},{16,24},{20,28},{24,16},{28,20},{1,9},{5... | collective-permute-start | bytes 2506760 | tf_op jit(solution)/shard_map/ppermute | solution.py:453
  225.2 22.3 %collective-permute-start.33 = (bf16[4,4,72,768]{3,2,1,0:T(8,128)(2,1)}, bf16[4,4,72,768]{3,2,1,0:T(8,128)(2,1)}, u32[]{:S(2)}, u32[]{:S(2)}) collective-permute-start(bf16[4,4,72,768]{3,2,1,0:T(8,128)(2,1)} %bitcast.106), channel_id=1, source_target_pairs={{0,4},{4,0},{8,12},{12,8},{16,20},{20,16},{24,28},{28,24},{1,5},{5... | collective-permute-start | bytes 5308424 | tf_op jit(solution)/shard_map/ppermute | solution.py:453
  229.0 11.6 %collective-permute-start.30 = (bf16[2,136,768]{2,1,0:T(8,128)(2,1)}, bf16[2,136,768]{2,1,0:T(8,128)(2,1)}, u32[]{:S(2)}, u32[]{:S(2)}) collective-permute-start(bf16[2,136,768]{2,1,0:T(8,128)(2,1)} %dynamic-slice_bitcast_fusion.10), channel_id=1, source_target_pairs={{0,8},{4,12},{8,0},{12,4},{16,24},{20,28},{24,16},{28,20},{1,9},{5... | collective-permute-start | bytes 1253384 | tf_op jit(solution)/shard_map/ppermute | solution.py:453
  234.8 11.1 %collective-permute-start.28 = (bf16[2,136,768]{2,1,0:T(8,128)(2,1)S(1)}, bf16[2,136,768]{2,1,0:T(8,128)(2,1)S(1)}, u32[]{:S(2)}, u32[]{:S(2)}) collective-permute-start(bf16[2,136,768]{2,1,0:T(8,128)(2,1)S(1)} %dynamic-slice_bitcast_fusion.11), channel_id=1, source_target_pairs={{0,16},{4,20},{8,24},{12,28},{16,0},{20,4},{24,8},{28,12},{1,17},{... | collective-permute-start | bytes 1253384 | tf_op jit(solution)/shard_map/ppermute | solution.py:453
  242.6 32.0 %collective-permute-start.31 = (bf16[136,768]{1,0:T(8,128)(2,1)}, bf16[136,768]{1,0:T(8,128)(2,1)}, u32[]{:S(2)}, u32[]{:S(2)}) collective-permute-start(bf16[136,768]{1,0:T(8,128)(2,1)} %get-tuple-element.190), channel_id=1, source_target_pairs={{0,2},{1,3},{2,0},{3,1},{4,6},{5,7},{6,4},{7,5},{8,10},{9,11},{10,... | collective-permute-start | bytes 626696 | tf_op jit(solution)/shard_map/ppermute | solution.py:458
  242.6 32.1 %collective-permute-start.32 = (bf16[136,768]{1,0:T(8,128)(2,1)}, bf16[136,768]{1,0:T(8,128)(2,1)}, u32[]{:S(2)}, u32[]{:S(2)}) collective-permute-start(bf16[136,768]{1,0:T(8,128)(2,1)} %get-tuple-element.191), channel_id=1, source_target_pairs={{0,1},{1,2},{2,3},{3,0},{4,5},{5,6},{6,7},{7,4},{8,9},{9,10},{10,1... | collective-permute-start | bytes 626696 | tf_op jit(solution)/shard_map/ppermute | solution.py:458
  246.7 28.0 %collective-permute-start.29 = (bf16[136,768]{1,0:T(8,128)(2,1)}, bf16[136,768]{1,0:T(8,128)(2,1)}, u32[]{:S(2)}, u32[]{:S(2)}) collective-permute-start(bf16[136,768]{1,0:T(8,128)(2,1)} %slice_bitcast_fusion.24), channel_id=1, source_target_pairs={{0,3},{1,0},{2,1},{3,2},{4,7},{5,4},{6,5},{7,6},{8,11},{9,8},{10,9... | collective-permute-start | bytes 626696 | tf_op jit(solution)/shard_map/ppermute | solution.py:458
  250.6 11.2 %collective-permute-start.34 = (bf16[2,2,72,768]{3,2,1,0:T(8,128)(2,1)}, bf16[2,2,72,768]{3,2,1,0:T(8,128)(2,1)}, u32[]{:S(2)}, u32[]{:S(2)}) collective-permute-start(bf16[2,2,72,768]{3,2,1,0:T(8,128)(2,1)} %dynamic-slice_bitcast_fusion.9), channel_id=1, source_target_pairs={{0,8},{4,12},{8,0},{12,4},{16,24},{20,28},{24,16},{28,20},{1,9},{5... | collective-permute-start | bytes 1327112 | tf_op jit(solution)/shard_map/ppermute | solution.py:453
  253.2 11.5 %collective-permute-start.37 = (bf16[2,2,72,768]{3,2,0,1:T(8,128)(2,1)}, bf16[2,2,72,768]{3,2,0,1:T(8,128)(2,1)}, u32[]{:S(2)}, u32[]{:S(2)}) collective-permute-start(bf16[2,2,72,768]{3,2,0,1:T(8,128)(2,1)} %bitcast.455), channel_id=1, source_target_pairs={{0,16},{4,20},{8,24},{12,28},{16,0},{20,4},{24,8},{28,12},{1,17},{... | collective-permute-start | bytes 1327112 | tf_op jit(solution)/shard_map/ppermute | solution.py:453
  263.2 6.0 %collective-permute-start.35 = (bf16[2,72,768]{2,1,0:T(8,128)(2,1)S(1)}, bf16[2,72,768]{2,1,0:T(8,128)(2,1)S(1)}, u32[]{:S(2)}, u32[]{:S(2)}) collective-permute-start(bf16[2,72,768]{2,1,0:T(8,128)(2,1)S(1)} %dynamic-slice_bitcast_fusion.15), channel_id=1, source_target_pairs={{0,16},{4,20},{8,24},{12,28},{16,0},{20,4},{24,8},{28,12},{1,17},{... | collective-permute-start | bytes 663560 | tf_op jit(solution)/shard_map/ppermute | solution.py:453
  264.8 10.0 %copy-start.48 = (bf16[2,136,768]{2,1,0:T(8,128)(2,1)S(1)}, bf16[2,136,768]{2,1,0:T(8,128)(2,1)}, u32[]{:S(2)}) copy-start(bf16[2,136,768]{2,1,0:T(8,128)(2,1)} %copy-done.47) | copy-start | bytes 1253380
  266.0 6.0 %collective-permute-start.38 = (bf16[2,72,768]{2,1,0:T(8,128)(2,1)S(1)}, bf16[2,72,768]{2,1,0:T(8,128)(2,1)S(1)}, u32[]{:S(2)}, u32[]{:S(2)}) collective-permute-start(bf16[2,72,768]{2,1,0:T(8,128)(2,1)S(1)} %dynamic-slice_bitcast_fusion.14), channel_id=1, source_target_pairs={{0,8},{4,12},{8,0},{12,4},{16,24},{20,28},{24,16},{28,20},{1,9},{5... | collective-permute-start | bytes 663560 | tf_op jit(solution)/shard_map/ppermute | solution.py:453
  269.3 6.7 %collective-permute-start.36 = (bf16[72,768]{1,0:T(8,128)(2,1)S(1)}, bf16[72,768]{1,0:T(8,128)(2,1)S(1)}, u32[]{:S(2)}, u32[]{:S(2)}) collective-permute-start(bf16[72,768]{1,0:T(8,128)(2,1)S(1)} %slice_bitcast_fusion.29), channel_id=1, source_target_pairs={{0,3},{1,0},{2,1},{3,2},{4,7},{5,4},{6,5},{7,6},{8,11},{9,8},{10,9... | collective-permute-start | bytes 331784 | tf_op jit(solution)/shard_map/ppermute | solution.py:458
  272.1 7.4 %collective-permute-start.39 = (bf16[72,768]{1,0:T(8,128)(2,1)S(1)}, bf16[72,768]{1,0:T(8,128)(2,1)S(1)}, u32[]{:S(2)}, u32[]{:S(2)}) collective-permute-start(bf16[72,768]{1,0:T(8,128)(2,1)S(1)} %get-tuple-element.196), channel_id=1, source_target_pairs={{0,2},{1,3},{2,0},{3,1},{4,6},{5,7},{6,4},{7,5},{8,10},{9,11},{10,... | collective-permute-start | bytes 331784 | tf_op jit(solution)/shard_map/ppermute | solution.py:458
  274.5 6.9 %collective-permute-start.40 = (bf16[72,768]{1,0:T(8,128)(2,1)S(1)}, bf16[72,768]{1,0:T(8,128)(2,1)S(1)}, u32[]{:S(2)}, u32[]{:S(2)}) collective-permute-start(bf16[72,768]{1,0:T(8,128)(2,1)S(1)} %get-tuple-element.197), channel_id=1, source_target_pairs={{0,1},{1,2},{2,3},{3,0},{4,5},{5,6},{6,7},{7,4},{8,9},{9,10},{10,1... | collective-permute-start | bytes 331784 | tf_op jit(solution)/shard_map/ppermute | solution.py:458
  281.5 10.9 %collective-permute-start.41 = (bf16[1,208,768]{2,1,0:T(8,128)(2,1)S(1)}, bf16[1,208,768]{2,1,0:T(8,128)(2,1)S(1)}, u32[]{:S(2)}, u32[]{:S(2)}) collective-permute-start(bf16[1,208,768]{2,1,0:T(8,128)(2,1)S(1)} %get-tuple-element.195), channel_id=1, source_target_pairs={{0,8},{4,12},{8,0},{12,4},{16,24},{20,28},{24,16},{28,20},{1,9},{5... | collective-permute-start | bytes 958472 | tf_op jit(solution)/shard_map/ppermute | solution.py:453
  282.6 8.7 %collective-permute-start.42 = (bf16[1,208,768]{2,1,0:T(8,128)(2,1)S(1)}, bf16[1,208,768]{2,1,0:T(8,128)(2,1)S(1)}, u32[]{:S(2)}, u32[]{:S(2)}) collective-permute-start(bf16[1,208,768]{2,1,0:T(8,128)(2,1)S(1)} %get-tuple-element.195), channel_id=1, source_target_pairs={{0,16},{4,20},{8,24},{12,28},{16,0},{20,4},{24,8},{28,12},{1,17},{... | collective-permute-start | bytes 958472 | tf_op jit(solution)/shard_map/ppermute | solution.py:453
  282.8 3.9 %collective-permute-start.23 = (f32[8,768]{1,0:T(8,128)S(1)}, f32[8,768]{1,0:T(8,128)S(1)}, u32[]{:S(2)}, u32[]{:S(2)}) collective-permute-start(f32[8,768]{1,0:T(8,128)S(1)} %select_maximum_fusion), channel_id=1, source_target_pairs={{0,1},{1,0},{2,3},{3,2},{4,5},{5,4},{6,7},{7,6},{8,9},{9,8},{10,11... | collective-permute-start | bytes 73736 | tf_op jit(solution)/shard_map/ppermute | solution.py:749
  286.7 5.9 %collective-permute-start.24 = (f32[8,768]{1,0:T(8,128)S(1)}, f32[8,768]{1,0:T(8,128)S(1)}, u32[]{:S(2)}, u32[]{:S(2)}) collective-permute-start(f32[8,768]{1,0:T(8,128)S(1)} %fusion.46), channel_id=1, source_target_pairs={{0,2},{1,3},{2,0},{3,1},{4,6},{5,7},{6,4},{7,5},{8,10},{9,11},{10,... | collective-permute-start | bytes 73736 | tf_op jit(solution)/shard_map/ppermute | solution.py:749
  291.3 5.3 %collective-permute-start.44 = (bf16[1,104,768]{2,1,0:T(8,128)(2,1)S(1)}, bf16[1,104,768]{2,1,0:T(8,128)(2,1)S(1)}, u32[]{:S(2)}, u32[]{:S(2)}) collective-permute-start(bf16[1,104,768]{2,1,0:T(8,128)(2,1)S(1)} %slice.668), channel_id=1, source_target_pairs={{0,8},{4,12},{8,0},{12,4},{16,24},{20,28},{24,16},{28,20},{1,9},{5... | collective-permute-start | bytes 479240 | tf_op jit(solution)/shard_map/ppermute | solution.py:453
  292.4 5.3 %collective-permute-start.45 = (bf16[1,104,768]{2,1,0:T(8,128)(2,1)S(1)}, bf16[1,104,768]{2,1,0:T(8,128)(2,1)S(1)}, u32[]{:S(2)}, u32[]{:S(2)}) collective-permute-start(bf16[1,104,768]{2,1,0:T(8,128)(2,1)S(1)} %slice.669), channel_id=1, source_target_pairs={{0,16},{4,20},{8,24},{12,28},{16,0},{20,4},{24,8},{28,12},{1,17},{... | collective-permute-start | bytes 479240 | tf_op jit(solution)/shard_map/ppermute | solution.py:453
  292.7 5.2 %collective-permute-start.25 = (f32[8,768]{1,0:T(8,128)S(1)}, f32[8,768]{1,0:T(8,128)S(1)}, u32[]{:S(2)}, u32[]{:S(2)}) collective-permute-start(f32[8,768]{1,0:T(8,128)S(1)} %fusion.65), channel_id=1, source_target_pairs={{0,4},{4,0},{8,12},{12,8},{16,20},{20,16},{24,28},{28,24},{1,5},{5... | collective-permute-start | bytes 73736 | tf_op jit(solution)/shard_map/ppermute | solution.py:453
  297.8 8.6 %collective-permute-start.46 = (bf16[1,208,768]{2,1,0:T(8,128)(2,1)S(1)}, bf16[1,208,768]{2,1,0:T(8,128)(2,1)S(1)}, u32[]{:S(2)}, u32[]{:S(2)}) collective-permute-start(bf16[1,208,768]{2,1,0:T(8,128)(2,1)S(1)} %constant_dynamic-update-slice_fusion.4), channel_id=1, source_target_pairs={{0,4},{4,0},{8,12},{12,8},{16,20},{20,16},{24,28},{28,24},{1,5},{5... | collective-permute-start | bytes 958472 | tf_op jit(solution)/shard_map/ppermute | solution.py:453
  297.9 3.9 %collective-permute-start.26 = (f32[8,768]{1,0:T(8,128)S(1)}, f32[8,768]{1,0:T(8,128)S(1)}, u32[]{:S(2)}, u32[]{:S(2)}) collective-permute-start(f32[8,768]{1,0:T(8,128)S(1)} %add.214), channel_id=1, source_target_pairs={{0,8},{4,12},{8,0},{12,4},{16,24},{20,28},{24,16},{28,20},{1,9},{5... | collective-permute-start | bytes 73736 | tf_op jit(solution)/shard_map/ppermute | solution.py:453
  301.8 3.8 %collective-permute-start.27 = (f32[8,768]{1,0:T(8,128)S(1)}, f32[8,768]{1,0:T(8,128)S(1)}, u32[]{:S(2)}, u32[]{:S(2)}) collective-permute-start(f32[8,768]{1,0:T(8,128)S(1)} %add.215), channel_id=1, source_target_pairs={{0,16},{4,20},{8,24},{12,28},{16,0},{20,4},{24,8},{28,12},{1,17},{... | collective-permute-start | bytes 73736 | tf_op jit(solution)/shard_map/ppermute | solution.py:453
  306.3 2.6 collective-permute-start.43
  (52 other events, 133.7 us)

commit v3 on v2

--- a/solution.py
+++ b/solution.py
@@ -16,6 +16,7 @@
 bf16 = jnp.bfloat16
 f32 = jnp.float32
 MIB = 1024 * 1024
+SMALL = pl.CostEstimate(flops=1000, bytes_accessed=1000, transcendentals=0)
 
 
 def nn(a, b):
@@ -96,9 +97,7 @@
         out_specs=[row_spec(blk, width)] * 4,
         out_shape=[out] * 4,
         compiler_params=params(40),
-        cost_estimate=pl.CostEstimate(
-            flops=6 * rows * width * width, bytes_accessed=14 * MIB, transcendentals=0
-        ),
+        cost_estimate=SMALL,
         name="qkv",
     )(x_ext, gain, w, cos, sin)
 
@@ -153,9 +152,7 @@
             jax.ShapeDtypeStruct((blocks, 8, 2 * BLK), f32),
         ],
         compiler_params=params(32),
-        cost_estimate=pl.CostEstimate(
-            flops=12 * rows * 256 * width, bytes_accessed=9 * MIB, transcendentals=rows * 3072
-        ),
+        cost_estimate=SMALL,
         name="attend",
     )(q, k, v, bias)
 
@@ -246,11 +243,7 @@
             jax.ShapeDtypeStruct((8, width), f32),
         ],
         compiler_params=params(48),
-        cost_estimate=pl.CostEstimate(
-            flops=4 * rows * width * (width + 3 * ff),
-            bytes_accessed=30 * MIB,
-            transcendentals=2 * rows * ff,
-        ),
+        cost_estimate=SMALL,
         name="mlp",
     )(x, og, attn, gain, wa, wi, wo)
 
@@ -266,9 +259,10 @@
     cos_ref,
     sin_ref,
     dq_ref,
+    dk_out_ref,
+    dv_out_ref,
     dk_ref,
     dv_ref,
-    edge_ref,
 ):
     b = pl.program_id(0)
     start = pl.multiple_of(b * BLK, BLK)
@@ -300,16 +294,12 @@
 
     @pl.when(b == pl.num_programs(0) - 1)
     def _():
-        width = dk_ref.shape[1]
-        ext = dk_ref.shape[0]
-        for at, ref in ((0, dk_ref), (width, dv_ref)):
-            edge_ref[:HALF, at : at + width] = ref[:HALF, :].astype(bf16)
-            edge_ref[HALF:, at : at + width] = ref[ext - HALF :, :].astype(bf16)
-
-
-def attend_back_call(q, k, v, do, bias, lse, cos, sin, at):
+        dk_out_ref[...] = dk_ref[...].astype(bf16)
+        dv_out_ref[...] = dv_ref[...].astype(bf16)
+
+
+def attend_back_call(q, k, v, do, bias, lse, cos, sin, at, width):
     ext = q.shape[0]
-    width = q.shape[1] // 2
     rows = do.shape[0]
     full = pl.BlockSpec((ext, width), lambda i: (0, at), pipeline_mode=pl.Buffered(1))
     acc = pl.BlockSpec((ext, width), lambda i: (0, 0))
@@ -330,75 +320,68 @@
             row_spec(BLK, width),
             acc,
             acc,
-            pl.BlockSpec((WINDOW, 2 * width), lambda i: (0, 0)),
         ],
         out_shape=[
             jax.ShapeDtypeStruct((rows, width), bf16),
-            jax.ShapeDtypeStruct((ext, width), f32),
-            jax.ShapeDtypeStruct((ext, width), f32),
-            jax.ShapeDtypeStruct((WINDOW, 2 * width), bf16),
-        ],
+            jax.ShapeDtypeStruct((ext, width), bf16),
+            jax.ShapeDtypeStruct((ext, width), bf16),
+        ],
+        scratch_shapes=[pltpu.VMEM((ext, width), f32)] * 2,
         compiler_params=params(48),
-        cost_estimate=pl.CostEstimate(
-            flops=30 * rows * 256 * width, bytes_accessed=20 * MIB, transcendentals=rows * 3072
-        ),
+        cost_estimate=SMALL,
         name="attend_back",
     )(q, k, v, do, bias, lse, cos, sin)
 
 
-def mixed_kernel(
-    dq0_ref, dq1_ref, dk0_ref, dk1_ref, dv0_ref, dv1_ref, first_ref, last_ref, cos_ref, sin_ref, mix_ref
-):
+def mixed_kernel(first_ref, last_ref, cos_ref, sin_ref, *refs):
+    mix_ref = refs[-1]
     rows = mix_ref.shape[0]
-    part = dq0_ref.shape[1]
-    width = 2 * part
+    width = mix_ref.shape[1] // 3
     i = pl.program_id(0)
     own = pl.ds(pl.multiple_of(i * rows, rows) + HALF, rows)
-    cos = jnp.concatenate([cos_ref[own, :]] * (part // 128), axis=1)
-    sin = jnp.concatenate([sin_ref[own, :]] * (part // 128), axis=1)
-    pad = jnp.zeros((rows - HALF, part), f32)
     is_first = (i == 0).astype(f32)
     is_last = (i == pl.num_programs(0) - 1).astype(f32)
-
-    def joined(ref, at):
-        cols = slice(at, at + part)
-        head = first_ref[:, cols].astype(f32) * is_first
-        tail = last_ref[:, cols].astype(f32) * is_last
-        return ref[own, :] + jnp.concatenate([head, pad], axis=0) + jnp.concatenate([pad, tail], axis=0)
-
-    for h, (dq_ref, dk_ref, dv_ref) in enumerate(
-        ((dq0_ref, dk0_ref, dv0_ref), (dq1_ref, dk1_ref, dv1_ref))
-    ):
-        at = h * part
+    at = 0
+    for n in range(len(refs) // 3):
+        dq_ref, dk_ref, dv_ref = refs[3 * n : 3 * n + 3]
+        part = dq_ref.shape[1]
+        pad = jnp.zeros((rows - HALF, part), f32)
+        cos = jnp.concatenate([cos_ref[own, :]] * (part // 128), axis=1)
+        sin = jnp.concatenate([sin_ref[own, :]] * (part // 128), axis=1)
+
+        def joined(ref, start):
+            cols = slice(start, start + part)
+            head = first_ref[:, cols].astype(f32) * is_first
+            tail = last_ref[:, cols].astype(f32) * is_last
+            ends = jnp.concatenate([head, pad], axis=0) + jnp.concatenate([pad, tail], axis=0)
+            return ref[own, :].astype(f32) + ends
+
         mix_ref[:, at : at + part] = dq_ref[...]
         dk = joined(dk_ref, at)
         dk = (dk * cos + turn_lanes(dk * sin, 1.0)).astype(bf16)
         mix_ref[:, width + at : width + at + part] = dk
         dv = joined(dv_ref, width + at)
         mix_ref[:, 2 * width + at : 2 * width + at + part] = dv.astype(bf16)
-
-
-def mixed_call(halves, first, last, cos, sin):
-    (dq0, dk0, dv0), (dq1, dk1, dv1) = halves
-    rows, part = dq0.shape
+        at += part
+
+
+def mixed_call(pieces, first, last, cos, sin):
+    rows = pieces[0][0].shape[0]
+    width = sum(piece[0].shape[1] for piece in pieces)
     blk = 256
-    full = const_spec(dk0.shape)
-    table = const_spec(cos.shape)
+    specs = []
+    for dq, dk, dv in pieces:
+        specs += [row_spec(blk, dq.shape[1]), const_spec(dk.shape), const_spec(dv.shape)]
     return pl.pallas_call(
         mixed_kernel,
         grid=(rows // blk,),
-        in_specs=[row_spec(blk, part)] * 2
-        + [full] * 4
-        + [const_spec(first.shape), const_spec(last.shape)]
-        + [table] * 2,
-        out_specs=row_spec(blk, 6 * part),
-        out_shape=jax.ShapeDtypeStruct((rows, 6 * part), bf16),
+        in_specs=[const_spec(x.shape) for x in (first, last, cos, sin)] + specs,
+        out_specs=row_spec(blk, 3 * width),
+        out_shape=jax.ShapeDtypeStruct((rows, 3 * width), bf16),
         compiler_params=params(32),
-        cost_estimate=pl.CostEstimate(
-            flops=20 * rows * part, bytes_accessed=14 * MIB, transcendentals=0
-        ),
+        cost_estimate=SMALL,
         name="mixed",
-    )(dq0, dq1, dk0, dk1, dv0, dv1, first, last, cos, sin)
+    )(first, last, cos, sin, *[x for piece in pieces for x in piece])
 
 
 def input_grad_kernel(mix_ref, w_ref, x_ref, gmid_ref, gain_ref, out_ref, gain_grad_ref):
@@ -441,9 +424,7 @@
             jax.ShapeDtypeStruct((8, width), f32),
         ],
         compiler_params=params(40),
-        cost_estimate=pl.CostEstimate(
-            flops=6 * rows * width * width, bytes_accessed=16 * MIB, transcendentals=0
-        ),
+        cost_estimate=SMALL,
         name="input_grad",
     )(mix, w, x, gmid, gain)
 
@@ -506,9 +487,10 @@
     return [piece, from_x, from_y, diag], [early[0], early[1], early[2], late]
 
 
-def spread_all(piece):
-    piece, from_x, from_y, half = spread_quads(piece)
-    return spread_core(piece, from_x, from_y, *spread_diag(piece, from_x, from_y, half))
+def spread_all(piece, *after):
+    mine = jnp.stack([piece] + [dp_swap(piece, mask) for mask in (XBIT, YBIT, XBIT | YBIT)])
+    theirs = dp_swap(hold(mine, *after), CORE)
+    return mine, theirs
 
 
 def ring_pieces(piece):
@@ -527,10 +509,6 @@
 def halve(arr, at, mask, dim):
     got = dp_swap(index_dim(arr, 1 - at, dim), mask)
     return index_dim(arr, at, dim), got
-
-
-def reduce_core(send, keep):
-    return add(keep, dp_swap(send, CORE))
 
 
 def reduce_first(total, quad):
@@ -546,7 +524,7 @@
     return halve(first, quad >> 1, YBIT, 1) + halve(second, quad & 1, XBIT, 1)
 
 
-def reduce_ring(keep_y, got_y, keep_x, got_x):
+def reduce_ring(keep_y, got_y, keep_x, got_x, extra=None):
     first = add(keep_y, got_y)
     second = add(keep_x, got_x)
     half = first.shape[0]
@@ -559,6 +537,8 @@
             block = add(block, dp_swap(block, mask))
             mask *= 2
         parts = [block[s] for s in range(steps)]
+    if extra is not None:
+        parts = [jnp.concatenate([part, extra]) for part in parts]
     return [parts[0]] + [ring_shift(parts[s], -s) for s in range(1, steps)]
 
 
@@ -619,31 +599,34 @@
     w_out = mlp_out_weight.reshape(4, 72, width)
     w_attn = attn_weight.reshape(4, 48, width)
 
-    edge = jnp.where(odd, hidden_in[:HALF], hidden_in[-HALF:])
+    own_qkv = core_rows(index_dim(w_qkv, quad, 1), core, 1).reshape(3 * 24, width)
+    ring_qkv = ring_pieces(own_qkv)
+    x_held = hold(hidden_in, ring_qkv)
+    edge = jnp.where(odd, x_held[:HALF], x_held[-HALF:])
     halo = pair_swap(edge)
     none = jnp.zeros_like(halo)
     x_ext = jnp.concatenate(
-        [jnp.where(odd, halo, none), hidden_in, jnp.where(odd, none, halo)], axis=0
-    )
-
-    own_qkv = core_rows(index_dim(w_qkv, quad, 1), core, 1).reshape(3 * 24, width)
+        [jnp.where(odd, halo, none), x_held, jnp.where(odd, none, halo)], axis=0
+    )
+
+    quads_qkv = spread_quads(ring_qkv)
+    diag_qkv = spread_diag(*quads_qkv)
+    wi_held = hold(w_in, quads_qkv[1], quads_qkv[2])
+    wo_held = hold(w_out, quads_qkv[1], quads_qkv[2])
+    wa_held = hold(w_attn, quads_qkv[1], quads_qkv[2])
     own_rest = jnp.concatenate(
         [
-            index_dim(index_dim(w_in, core, 0), quad, 0),
-            core_rows(index_dim(w_out, quad, 0), core, 0),
-            core_rows(index_dim(w_attn, quad, 0), core, 0),
+            index_dim(index_dim(wi_held, core, 0), quad, 0),
+            core_rows(index_dim(wo_held, quad, 0), core, 0),
+            core_rows(index_dim(wa_held, quad, 0), core, 0),
         ],
         axis=0,
     )
-    ring_qkv = ring_pieces(own_qkv)
-    ring_rest = ring_pieces(hold(own_rest, own_qkv))
-
-    quads_qkv = spread_quads(ring_qkv)
-    diag_qkv = spread_diag(*quads_qkv)
-    quads_rest = spread_quads(hold(ring_rest, quads_qkv[1], quads_qkv[2]))
+    ring_rest = ring_pieces(own_rest)
+    quads_rest = spread_quads(ring_rest)
     mine, theirs = spread_core(*quads_qkv[:3], *diag_qkv)
     qkv_all = jnp.zeros((3, steps, 4, 48, width), bf16)
-    qkv_all = qkv_all.at[:, 0].set(w_qkv)
+    qkv_all = qkv_all.at[:, 0].set(hold(w_qkv, quads_qkv[1], quads_qkv[2]))
     for n in range(4):
         a, b = by_core(mine[n], theirs[n], core)
         a = a.reshape(steps - 1, 3, 24, width)
@@ -652,17 +635,21 @@
         qkv_all = put(qkv_all, part, (0, 1, quad ^ n, 0, 0))
     qkv_all = qkv_all.reshape(3, width, width)
 
-    cos, sin, bias = tables(seg_ids, here * rows, rows)
+    cos, sin, bias = tables(hold(seg_ids, ring_qkv), here * rows, rows)
     gain_one = norm1_gain[None]
     gain_two = norm2_gain[None]
     low_one, q, k, v = qkv_call(x_ext, gain_one, hold(qkv_all, ring_rest), cos, sin)
-    low_attn, lse = attend_call(hold(q, *quads_rest[1:3]), k, v, bias, rows)
-
-    diag_rest = spread_diag(*quads_rest)
-    mine, theirs = spread_core(*quads_rest[:3], *diag_rest)
-    in_all = jnp.zeros((2, steps, 4, 72, width), bf16).at[:, 0].set(w_in)
-    out_all = jnp.zeros((steps, 4, 72, width), bf16).at[0].set(w_out)
-    attn_all = jnp.zeros((steps, 4, 48, width), bf16).at[0].set(w_attn)
+    low_attn, lse = attend_call(q, k, v, bias, rows)
+
+    piece, from_x, from_y, half = quads_rest
+    early, diag_x, diag_y = spread_diag(piece, hold(from_x, q), hold(from_y, q), half)
+    mine, theirs = spread_core(piece, from_x, from_y, early, hold(diag_x, low_attn), diag_y)
+    wi_held = hold(w_in, q)
+    wo_held = hold(w_out, q)
+    wa_held = hold(w_attn, q)
+    in_all = jnp.zeros((2, steps, 4, 72, width), bf16).at[:, 0].set(wi_held)
+    out_all = jnp.zeros((steps, 4, 72, width), bf16).at[0].set(wo_held)
+    attn_all = jnp.zeros((steps, 4, 48, width), bf16).at[0].set(wa_held)
     for n in range(4):
         a, b = by_core(mine[n], theirs[n], core)
         pair = jnp.stack([a[:, :72], b[:, :72]])[:, :, None]
@@ -682,91 +669,102 @@
         hidden_in, out_grad, low_attn, gain_two, attn_all, in_all, out_all
     )
 
-    g_in = tn(ggu, low_two).astype(bf16).reshape(2, steps, 4, 72, width)
-    g_out = tn(low_act, out_grad).astype(bf16).reshape(steps, 4, 72, width)
-    g_attn = tn(low_attn, low_mid).astype(bf16).reshape(steps, 4, 48, width)
-
-    def rest_for(c):
-        return jnp.concatenate(
-            [index_dim(g_in, c, 0), core_rows(g_out, c, 2), core_rows(g_attn, c, 2)], axis=2
-        )
-
-    send, keep = rest_for(1 - core), rest_for(core)
-    dattn = hold(dattn, send)
-    back_first = attend_back_call(q, k, v, dattn, bias, lse, cos, sin, 0)
-    core_rest = reduce_core(send, keep)
+    def halves(x):
+        cols = width // 2
+        return [lax.dynamic_slice_in_dim(x, c * cols, cols, 1) for c in (1 - core, core)]
+
+    def grads(x, ys, *lead):
+        shape = lead + (steps, 4, x.shape[1] // (4 * steps * lead[0] if lead else 4 * steps))
+        return [tn(x, y).astype(bf16).reshape(shape + (width // 2,)) for y in ys]
+
+    g_in = grads(ggu, halves(low_two), 2)
+    g_out = grads(low_act, halves(out_grad))
+    g_attn = grads(low_attn, halves(low_mid))
+    got_in = dp_swap(g_in[0], CORE)
+    got_out = dp_swap(g_out[0], CORE)
+    got_attn = dp_swap(g_attn[0], CORE)
+    dattn = hold(dattn, *g_in, *g_out, *g_attn)
+    piece_a = attend_back_call(q, k, v, dattn, bias, lse, cos, sin, 2, 256)
+    sum_in = add(g_in[1], hold(got_in, piece_a[0]))
+    core_rest = jnp.concatenate(
+        [sum_in[0], sum_in[1], add(g_out[1], got_out), add(g_attn[1], got_attn)], axis=2
+    )
     first_rest = reduce_first(core_rest, quad)
-    dattn = hold(dattn, core_rest, back_first[0])
-    back_second = attend_back_call(q, k, v, dattn, bias, lse, cos, sin, 1)
-    part = width // 2
-    edges = jnp.concatenate(
-        [
-            back_first[3][:, :part],
-            back_second[3][:, :part],
-            back_first[3][:, part:],
-            back_second[3][:, part:],
-        ],
-        axis=1,
-    )
-    got = pair_swap(jnp.where(odd, edges[:HALF], edges[HALF:])).reshape(HALF, 2, width)
+    dattn = hold(dattn, core_rest, piece_a[0])
+    piece_b = attend_back_call(q, k, v, dattn, bias, lse, cos, sin, 0, 384)
+    dattn = hold(dattn, *first_rest[1::2], piece_b[0])
+    piece_c = attend_back_call(q, k, v, dattn, bias, lse, cos, sin, 3, 128)
+    second_rest = reduce_second(*first_rest, quad)
+    pieces = (piece_b, piece_c, piece_a)
+    ends = [
+        jnp.concatenate([jnp.where(odd, x[:HALF], x[-HALF:]) for x in (p[n] for p in pieces)], axis=1)
+        for n in (1, 2)
+    ]
+    got = pair_swap(jnp.stack(ends, axis=1))
     turn = width // steps
     got = jnp.where(odd, jnp.roll(got, turn, 2), jnp.roll(got, -turn, 2)).reshape(HALF, 2 * width)
     none = jnp.zeros_like(got)
     own = slice(HALF, HALF + rows)
-    mix = mixed_call(
-        (back_first[:3], back_second[:3]),
-        jnp.where(odd, got, none),
-        jnp.where(odd, none, got),
-        cos,
-        sin,
-    )
-    g_qkv = tn(mix, low_one[HALF : HALF + rows]).astype(bf16).reshape(3, steps, 4, 48, width)
-
-    def qkv_for(c):
-        part = core_rows(g_qkv, c, 3).transpose(1, 2, 0, 3, 4)
-        return part.reshape(steps, 4, 72, width)
-
-    send_qkv, keep_qkv = qkv_for(1 - core), qkv_for(core)
-    second_rest = reduce_second(*first_rest, quad)
+    mix = mixed_call(pieces, jnp.where(odd, got, none), jnp.where(odd, none, got), cos, sin)
+    g_qkv = [
+        tn(mix, y).astype(bf16).reshape(3, steps, 4, 48, width // 2)
+        for y in halves(low_one[HALF : HALF + rows])
+    ]
+    got_qkv = dp_swap(g_qkv[0], CORE)
+    core_qkv = add(g_qkv[1], got_qkv).transpose(1, 2, 0, 3, 4).reshape(steps, 4, 144, width // 2)
+    first_qkv = reduce_first(core_qkv, quad)
+    ring_back = reduce_ring(*second_rest)
     grad_hidden, gain_one_part = input_grad_call(
-        hold(mix, send_qkv, *second_rest[::2]),
+        hold(mix, core_qkv, *second_rest[1::2]),
         qkv_all.reshape(3 * width, width),
         hidden_in,
         grad_mid,
         gain_one,
     )
-    core_qkv = reduce_core(send_qkv, keep_qkv)
-    first_qkv = reduce_first(core_qkv, quad)
-    ring_back = reduce_ring(*second_rest)
-    second_qkv = reduce_second(*first_qkv, quad)
-    rest = reduce_sum(ring_back)
-    qkv_total = reduce_sum(reduce_ring(*second_qkv))
-
     gains = jnp.stack([jnp.sum(gain_one_part, axis=0), jnp.sum(gain_two_part, axis=0)])
-    gains = jnp.pad(gains, ((0, 6), (0, 0)))
-    mask = 1
-    while mask < steps:
-        gains = gains + lax.ppermute(gains, "tensor", [(i, i ^ mask) for i in range(steps)])
-        mask *= 2
-    mask = 1
+    mask = 8
     while mask < lax.axis_size("dp"):
         gains = gains + dp_swap(gains, mask)
         mask *= 2
 
-    mine, theirs = spread_all(jnp.concatenate([rest, qkv_total])[None])
-    cut = rest.shape[0]
+    def coded(x):
+        high = lax.reduce_precision(x, 8, 7)
+        return jnp.concatenate([high, x - high]).astype(bf16).reshape(8, width // 2)
+
+    def decoded(x):
+        both = x.astype(f32).reshape(x.shape[:-2] + (2, 2, width))
+        return both[..., 0, :, :] + both[..., 1, :, :]
+
+    second_qkv = reduce_second(*first_qkv, quad)
+    parts = reduce_ring(*second_qkv, coded(gains))
+    slots = jnp.zeros((steps, 8, width // 2), bf16)
+    for s in range(steps):
+        slots = put(slots, parts[s][None, 144:], ((here + s) % steps if s else here, 0, 0))
+    gains = jnp.sum(decoded(slots), axis=0)
+    rest = reduce_sum(ring_back)
+    qkv_total = reduce_sum([part[:144] for part in parts])
+
+    mine, theirs = spread_all(jnp.concatenate([rest, qkv_total, coded(gains)]))
+    full = jnp.where(
+        core == 0,
+        jnp.concatenate([mine, theirs], axis=2),
+        jnp.concatenate([theirs, mine], axis=2),
+    )
     o_in = jnp.zeros((2, 4, 72, width), f32)
     o_out = jnp.zeros((4, 72, width), f32)
     o_attn = jnp.zeros((4, 48, width), f32)
     o_qkv = jnp.zeros((3, 4, 48, width), f32)
+    slots = jnp.zeros((4, 8, width), bf16)
     for n in range(4):
-        a, b = by_core(mine[n][0].astype(f32), theirs[n][0].astype(f32), core)
-        o_in = put(o_in, jnp.stack([a[:72], b[:72]])[:, None], (0, quad ^ n, 0, 0))
-        o_out = put(o_out, join_cores(a[72:112], b[72:112], 72, 0)[None], (quad ^ n, 0, 0))
-        o_attn = put(o_attn, join_cores(a[112:cut], b[112:cut], 48, 0)[None], (quad ^ n, 0, 0))
-        a = a[cut:].reshape(3, 24, width)
-        b = b[cut:].reshape(3, 24, width)
-        o_qkv = put(o_qkv, join_cores(a, b, 48, 1)[:, None], (0, quad ^ n, 0, 0))
+        a = full[n]
+        slots = put(slots, a[None, 408:], (quad ^ n, 0, 0))
+        a = a[:408].astype(f32)
+        o_in = put(o_in, a[:144].reshape(2, 1, 72, width), (0, quad ^ n, 0, 0))
+        o_out = put(o_out, a[None, 144:216], (quad ^ n, 0, 0))
+        o_attn = put(o_attn, a[None, 216:264], (quad ^ n, 0, 0))
+        o_qkv = put(o_qkv, a[264:].reshape(3, 1, 48, width), (0, quad ^ n, 0, 0))
+    cols = width // 2
+    gains = jnp.sum(decoded(slots[..., :cols]), axis=0) + jnp.sum(decoded(slots[..., cols:]), axis=0)
     grad_qkv = o_qkv.reshape(3, 3, 64, width).transpose(3, 0, 1, 2)
     grad_in = o_in.reshape(2, 288, width).transpose(2, 0, 1)
     return (

time: 320 us -> 305 us (0.953)
  waiting for transfers between devices: 74.2 us -> 60.8 us
  other arithmetic: 39.4 us -> 26.1 us
  matrix products: 14.1 us -> 22.1 us
  starting transfers between devices: 45.3 us -> 52.5 us
    ppermute x31 -> x28, waiting for transfers between devices: 48.8 us -> 38.1 us  [dp_swap(): return lax.ppermute(x, 'dp', [(i, i ^ mask) for i in range(count)])]
    dot_general x4 -> x8, matrix products: 14.1 us -> 22.1 us  [tn(): lax.dot_general(a, b, (((0,), (0,)), ((), ())), preferred_element_type=f32)]
    dynamic_update_slice x32 -> x16, other arithmetic: 7.47 us -> 0.62 us  [put(): return lax.dynamic_update_slice(buf, part, starts)]
    slice x17 -> x5, local copies, waits for them, and re-layouts: 0.31 us -> 6.24 us  [the longest x4 3.59 us: body(): o_in = put(o_in, a[:144].reshape(2, 1, 72, width), (0, quad ^ n, 0, 0))]
    convert_element_type x11, other arithmetic: 13.6 us -> 7.78 us  [add(): return (a.astype(f32) + b.astype(f32)).astype(bf16)]
    ppermute x12, starting transfers between devices: 17.9 us -> 23.2 us  [ring_shift(): lax.ppermute(x, 'tensor', [(i, (i + step) % count) for i in range(count)])]
    dynamic_update_slice x0 -> x24, local copies, waits for them, and re-layouts: none -> 4.92 us  [put(): return lax.dynamic_update_slice(buf, part, starts)]
    squeeze x9 -> x6, local copies, waits for them, and re-layouts: 5.94 us -> 1.11 us  [index_dim(): return lax.squeeze(lax.dynamic_slice_in_dim(x, at, 1, dim), (dim,))]
  transfers between devices with their start and end apart: 47 -> 42, of which waited for: 18 -> 22; matrix products, arithmetic and copies ran while one was open for 17% -> 16% of each run, Pallas kernels for 13% -> 16%
where the time goes in v3:
time: 305 us; the launch traced here: 299 us
  Pallas kernels  84.8 us (28%)
  waiting for transfers between devices  60.8 us (20%)
  starting transfers between devices  52.5 us (17%)
  local copies, waits for them, and re-layouts  50.1 us (16%)
  other arithmetic  26.1 us (9%)
  matrix products  22.1 us (7%)
    ppermute x28, waiting for transfers between devices, dp_swap(): return lax.ppermute(x, 'dp', [(i, i ^ mask) for i in range(count)])  38.1 us
    pallas_call x1, Pallas kernels, mlp_call(): pl.pallas_call(mlp_kernel, grid=(rows // blk,), in_specs=[row_spec(blk, w...  29.5 us
    pallas_call x3, Pallas kernels, attend_back_call(): pl.pallas_call(functools.partial(attend_back_kernel, at * (width // 128))...  28.7 us
    ppermute x12, starting transfers between devices, ring_shift(): lax.ppermute(x, 'tensor', [(i, (i + step) % count) for i in range(count)])  23.2 us
    dot_general x8, matrix products, tn(): lax.dot_general(a, b, (((0,), (0,)), ((), ())), preferred_element_type=f32)  22.1 us
    ppermute x28, starting transfers between devices, dp_swap(): return lax.ppermute(x, 'dp', [(i, i ^ mask) for i in range(count)])  21.4 us
    unnamed x164, local copies, waits for them, and re-layouts  21.1 us
    ppermute x12, waiting for transfers between devices, ring_shift(): lax.ppermute(x, 'tensor', [(i, (i + step) % count) for i in range(count)])  19.7 us
  transfers between devices with their start and end apart: 42, of which 22 were waited for; matrix products, arithmetic and copies ran while one was open for 16% of the time, Pallas kernels for 16%

profile of v3, /device:TPU:0, one launch (start us, length us, event | category | flops | bytes accessed | tf_op | source)
XLA Modules:
  0.0 299.2 jit_solution(17938451166349772901)
XLA Ops:
  1.8 3.1 %collective-permute-start = (bf16[72,768]{1,0:T(8,128)(2,1)S(1)}, bf16[72,768]{1,0:T(8,128)(2,1)S(1)}, u32[]{:S(2)}, u32[]{:S(2)}) collective-permute-start(bf16[72,768]{1,0:T(8,128)(2,1)S(1)} %bitcast.426), channel_id=1, source_target_pairs={{0,1},{1,2},{2,3},{3,0},{4,5},{5,6},{6,7},{7,4},{8,9},{9,10},{10,1... | collective-permute-start | bytes 331784 | tf_op jit(solution)/shard_map/ppermute | solution.py:439
  4.8 2.6 collective-permute-start.1
  7.4 1.3 collective-permute-start.2
  10.9 3.9 %collective-permute-done.1 = bf16[72,768]{1,0:T(8,128)(2,1)S(1)} collective-permute-done((bf16[72,768]{1,0:T(8,128)(2,1)S(1)}, bf16[72,768]{1,0:T(8,128)(2,1)S(1)}, u32[]{:S(2)}, u32[]{:S(2)}) %collective-permute-start.1) | collective-permute-done | bytes 110624 | tf_op jit(solution)/shard_map/ppermute | solution.py:439
  15.4 1.5 collective-permute-start.4
  17.0 1.5 collective-permute-start.5
  19.3 2.9 collective-permute-start.3
  22.2 2.1 multiply_sine_fusion
  25.1 1.3 collective-permute-done.5
  29.0 1.6 collective-permute-start.8
  31.5 3.0 collective-permute-start.10
  35.5 2.9 collective-permute-start.12
  40.0 1.6 collective-permute-done.10
  41.5 7.9 %collective-permute-done.11 = bf16[136,768]{1,0:T(8,128)(2,1)S(1)} collective-permute-done((bf16[136,768]{1,0:T(8,128)(2,1)S(1)}, bf16[136,768]{1,0:T(8,128)(2,1)S(1)}, u32[]{:S(2)}, u32[]{:S(2)}) %collective-permute-start.11) | collective-permute-done | bytes 208928 | tf_op jit(solution)/shard_map/ppermute | solution.py:439
  49.6 1.6 collective-permute-start.13
  53.1 7.1 %qkv.1 = (bf16[1152,768]{1,0:T(8,128)(2,1)S(1)}, bf16[1152,768]{1,0:T(8,128)(2,1)S(1)}, bf16[1152,768]{1,0:T(8,128)(2,1)S(1)}, bf16[1152,768]{1,0:T(8,128)(2,1)S(1)}) custom-call(bf16[1152,768]{1,0:T(8,128)(2,1)S(1)} %pad_maximum_fusion.2.x_ref, f32[1,768]{1,0:T(1,128)S(1)} %broadcast_in_dim.122.gain_ref, bf16[3,768,768]{2,1,0:T(8,128)(2,1)S(1)} %bitcast.358, ...), custom_call_target="tpu_custom_call" | custom-call | flops 1000 | bytes 1000 | tf_op jit(solution)/shard_map/qkv/pallas_call | solution.py:87
  60.2 1.2 copy-done.19
  61.4 4.2 %collective-permute-done.13 = bf16[3,136,768]{2,1,0:T(8,128)(2,1)S(1)} collective-permute-done((bf16[3,136,768]{2,1,0:T(8,128)(2,1)S(1)}, bf16[3,136,768]{2,1,0:T(8,128)(2,1)S(1)}, u32[]{:S(2)}, u32[]{:S(2)}) %collective-permute-start.13) | collective-permute-done | bytes 626720 | tf_op jit(solution)/shard_map/ppermute | solution.py:434
  65.6 1.2 collective-permute-done.14
  67.4 1.5 pad_maximum_fusion.1
  70.0 9.9 %attend.1 = (bf16[1024,768]{1,0:T(8,128)(2,1)S(1)}, f32[8,8,256]{2,1,0:T(8,128)S(1)}) custom-call(bf16[1152,768]{1,0:T(8,128)(2,1)S(1)} %get-tuple-element.106.q_ref, bf16[1152,768]{1,0:T(8,128)(2,1)S(1)} %get-tuple-element.107.k_ref, bf16[1152,768]{1,0:T(8,128)(2,1)S(1)} %get-tuple-element.108.v_ref, f32[8,256,128]{2,1,0:T(8,128)S(1)} %and_select_fusion.bias_ref), custom_call_target="tpu_custom_call" | custom-call | flops 1000 | bytes 1000 | tf_op jit(solution)/shard_map/attend/pallas_call | solution.py:140
  85.7 1.4 broadcast_select_fusion.1
  88.5 1.7 broadcast_select_fusion.3
  92.2 1.7 copy-done.32
  93.9 29.5 %mlp.1 = (bf16[1024,768]{1,0:T(8,128)(2,1)}, f32[1024,768]{1,0:T(8,128)}, bf16[1024,768]{1,0:T(8,128)(2,1)S(1)}, bf16[1024,768]{1,0:T(8,128)(2,1)S(1)}, bf16[102...) custom-call(bf16[1024,768]{1,0:T(8,128)(2,1)} %x_ref.3, ...), custom_call_target="tpu_custom_call" | custom-call | flops 1000 | bytes 1000 | tf_op jit(solution)/shard_map/mlp/pallas_call | solution.py:228
  123.4 4.6 %convolution_convert_fusion.5 = bf16[1152,384]{1,0:T(8,128)(2,1)} fusion(bf16[1024,1152]{1,0:T(8,128)(2,1)} %get-tuple-element.120, bf16[1024,768]{1,0:T(8,128)(2,1)S(1)} %copy-done.54, s32[]{:T(128)S(6)} %select_n.334), kind=kOutput, calls=%fused_computation.9 | convolution fusion | flops 906412032 | bytes 4030468 | tf_op jit(solution)/shard_map/dot_general | solution.py:31
  128.0 4.0 %convolution_convert_fusion.3 = bf16[2304,384]{1,0:T(8,128)(2,1)} fusion(bf16[1024,2304]{1,0:T(8,128)(2,1)S(1)} %copy-done.79, bf16[1024,768]{1,0:T(8,128)(2,1)S(1)} %get-tuple-element.119, s32[]{:T(128)S(6)} %select_n.334), kind=kOutput, calls=%fused_computation.3 | convolution fusion | flops 1812824064 | bytes 7274500 | tf_op jit(solution)/shard_map/dot_general | solution.py:31
  132.4 1.8 convolution_convert_fusion.7
  134.7 1.4 convolution_convert_fusion.4
  137.2 2.7 convolution_convert_fusion.2
  140.0 9.3 %attend_back.3 = (bf16[1024,256]{1,0:T(8,128)(2,1)S(1)}, bf16[1152,256]{1,0:T(8,128)(2,1)S(1)}, bf16[1152,256]{1,0:T(8,128)(2,1)S(1)}) custom-call(bf16[1152,768]{1,0:T(8,128)(2,1)} %copy-done, bf16[1152,768]{1,0:T(8,128)(2,1)} %copy-done.1, bf16[1152,768]{1,0:T(8,128)(2,1)} %copy-done.2, bf16[1024,768]{1,0:T(8,128)(2,1)S(1)} %get-tuple-element.129.do_ref, ...), custom_call_target="tpu_custom_call" | custom-call | flops 1000 | bytes 1000 | tf_op jit(solution)/shard_map/attend_back/pallas_call | solution.py:306
  149.3 1.6 add_convert_fusion.2
  154.8 1.5 collective-permute-start.22
  158.3 1.5 collective-permute-start.23
  159.8 2.7 slice.598
  164.1 1.2 copy-done.5
  168.3 12.6 %attend_back.4 = (bf16[1024,384]{1,0:T(8,128)(2,1)S(1)}, bf16[1152,384]{1,0:T(8,128)(2,1)S(1)}, bf16[1152,384]{1,0:T(8,128)(2,1)S(1)}) custom-call(bf16[1152,768]{1,0:T(8,128)(2,1)} %copy-done, bf16[1152,768]{1,0:T(8,128)(2,1)} %copy-done.1, bf16[1152,768]{1,0:T(8,128)(2,1)} %copy-done.2, bf16[1024,768]{1,0:T(8,128)(2,1)} %copy-done.14, ...), custom_call_target="tpu_custom_call" | custom-call | flops 1000 | bytes 1000 | tf_op jit(solution)/shard_map/attend_back/pallas_call | solution.py:306
  180.9 6.8 %attend_back.5 = (bf16[1024,128]{1,0:T(8,128)(2,1)S(1)}, bf16[1152,128]{1,0:T(8,128)(2,1)S(1)}, bf16[1152,128]{1,0:T(8,128)(2,1)S(1)}) custom-call(bf16[1152,768]{1,0:T(8,128)(2,1)} %copy-done, bf16[1152,768]{1,0:T(8,128)(2,1)} %copy-done.1, bf16[1152,768]{1,0:T(8,128)(2,1)} %copy-done.2, bf16[1024,768]{1,0:T(8,128)(2,1)S(1)} %copy-done.15, ...), custom_call_target="tpu_custom_call" | custom-call | flops 1000 | bytes 1000 | tf_op jit(solution)/shard_map/attend_back/pallas_call | solution.py:306
  187.9 5.1 %collective-permute-start.24 = (bf16[64,2,768]{2,0,1:T(8,128)(2,1)S(1)}, bf16[64,2,768]{2,0,1:T(8,128)(2,1)S(1)}, u32[]{:S(2)}, u32[]{:S(2)}) collective-permute-start(bf16[64,2,768]{2,0,1:T(8,128)(2,1)S(1)} %pad_maximum_fusion.13), channel_id=1, source_target_pairs={{0,1},{1,0},{2,3},{3,2},{4,5},{5,4},{6,7},{7,6},{8,9},{9,8},{10,11... | collective-permute-start | bytes 589832 | tf_op jit(solution)/shard_map/ppermute | solution.py:444
  193.0 1.4 fusion.3
  195.0 2.7 collective-permute-done.24
  198.1 2.7 mixed.1.mix_ref
  200.9 2.7 convolution_convert_fusion
  203.6 1.4 copy.63
  205.0 1.4 fusion.2
  207.7 3.8 %convolution_convert_fusion.1 = bf16[2304,384]{1,0:T(8,128)(2,1)} fusion(bf16[1024,2304]{1,0:T(8,128)(2,1)S(1)} %mixed.1.mix_ref, bf16[1024,768]{1,0:T(8,128)(2,1)S(1)} %copy-done.55, s32[]{:T(128)S(6)} %select_n.335), kind=kOutput, calls=%fused_computation.1 | convolution fusion | flops 1812824064 | bytes 7274500 | tf_op jit(solution)/shard_map/dot_general | solution.py:31
  211.5 7.5 %collective-permute-done.26 = bf16[2,264,384]{2,1,0:T(8,128)(2,1)S(1)} collective-permute-done((bf16[2,264,384]{2,1,0:T(8,128)(2,1)S(1)}, bf16[2,264,384]{2,1,0:T(8,128)(2,1)S(1)}, u32[]{:S(2)}, u32[]{:S(2)}) %collective-permute-start.26) | collective-permute-done | bytes 405536 | tf_op jit(solution)/shard_map/ppermute | solution.py:434
  219.8 6.8 %input_grad.1 = (bf16[1024,768]{1,0:T(8,128)(2,1)}, f32[8,768]{1,0:T(8,128)S(1)}) custom-call(bf16[1024,2304]{1,0:T(8,128)(2,1)S(1)} %mixed.1.mix_ref, bf16[2304,768]{1,0:T(8,128)(2,1)S(1)} %bitcast.359, bf16[1024,768]{1,0:T(8,128)(2,1)S(1)} %copy-done.13, f32[1024,768]{1,0:T(8,128)S(1)} %copy-done.16, f32[1,768]{1,0:T(1,128)S(1)} %broadcast_in_dim.122.gain_ref), custom_call_target="tpu_custom_call" | custom-call | flops 1000 | bytes 1000 | tf_op jit(solution)/shard_map/input_grad/pallas_call | solution.py:411
  228.8 1.2 fusion.7
  230.1 2.3 collective-permute-start.27
  233.5 1.9 fusion.1
  239.2 8.2 %collective-permute-done.34 = bf16[2,2,144,384]{3,2,0,1:T(8,128)(2,1)S(1)} collective-permute-done((bf16[2,2,144,384]{3,2,0,1:T(8,128)(2,1)S(1)}, bf16[2,2,144,384]{3,2,0,1:T(8,128)(2,1)S(1)}, u32[]{:S(2)}, u32[]{:S(2)}) %collective-permute-start.34) | collective-permute-done | bytes 442400 | tf_op jit(solution)/shard_map/ppermute | solution.py:434
  248.6 2.3 collective-permute-start.32
  250.9 2.6 collective-permute-done.35
  255.0 5.8 %collective-permute-start.33 = (bf16[152,384]{1,0:T(8,128)(2,1)S(1)}, bf16[152,384]{1,0:T(8,128)(2,1)S(1)}, u32[]{:S(2)}, u32[]{:S(2)}) collective-permute-start(bf16[152,384]{1,0:T(8,128)(2,1)S(1)} %get-tuple-element.219), channel_id=1, source_target_pairs={{0,3},{1,0},{2,1},{3,2},{4,7},{5,4},{6,5},{7,6},{8,11},{9,8},{10,9... | collective-permute-start | bytes 350216 | tf_op jit(solution)/shard_map/ppermute | solution.py:439
  261.5 1.6 collective-permute-done.33
  263.7 4.2 %collective-permute-done.36 = bf16[152,384]{1,0:T(8,128)(2,1)S(1)} collective-permute-done((bf16[152,384]{1,0:T(8,128)(2,1)S(1)}, bf16[152,384]{1,0:T(8,128)(2,1)S(1)}, u32[]{:S(2)}, u32[]{:S(2)}) %collective-permute-start.36) | collective-permute-done | bytes 116768 | tf_op jit(solution)/shard_map/ppermute | solution.py:439
  270.6 1.5 collective-permute-start.39
  272.2 1.4 collective-permute-start.40
  273.6 3.5 %collective-permute-done.38 = bf16[416,384]{1,0:T(8,128)(2,1)S(1)} collective-permute-done((bf16[416,384]{1,0:T(8,128)(2,1)S(1)}, bf16[416,384]{1,0:T(8,128)(2,1)S(1)}, u32[]{:S(2)}, u32[]{:S(2)}) %collective-permute-start.38) | collective-permute-done | bytes 319520 | tf_op jit(solution)/shard_map/ppermute | solution.py:434
  277.1 3.0 %collective-permute-done.39 = bf16[416,384]{1,0:T(8,128)(2,1)S(1)} collective-permute-done((bf16[416,384]{1,0:T(8,128)(2,1)S(1)}, bf16[416,384]{1,0:T(8,128)(2,1)S(1)}, u32[]{:S(2)}, u32[]{:S(2)}) %collective-permute-start.39) | collective-permute-done | bytes 319520 | tf_op jit(solution)/shard_map/ppermute | solution.py:434
  280.1 1.4 collective-permute-done.40
  281.8 3.0 collective-permute-done.41
  284.8 2.8 maximum_select_fusion
  (393 shorter events, 64.4 us)
Async XLA Ops:
  0.6 17.9 %copy-start.75 = (s32[4096]{0:T(1024)S(1)}, s32[4096]{0:T(1024)}, u32[]{:S(2)}) copy-start(s32[4096]{0:T(1024)} %param.18) | copy-start | bytes 49156
  0.6 18.6 %copy-start.12 = (bf16[1024,768]{1,0:T(8,128)(2,1)S(1)}, bf16[1024,768]{1,0:T(8,128)(2,1)}, u32[]{:S(2)}) copy-start(bf16[1024,768]{1,0:T(8,128)(2,1)} %x_ref.3) | copy-start | bytes 4718596
  1.8 9.1 %collective-permute-start = (bf16[72,768]{1,0:T(8,128)(2,1)S(1)}, bf16[72,768]{1,0:T(8,128)(2,1)S(1)}, u32[]{:S(2)}, u32[]{:S(2)}) collective-permute-start(bf16[72,768]{1,0:T(8,128)(2,1)S(1)} %bitcast.426), channel_id=1, source_target_pairs={{0,1},{1,2},{2,3},{3,0},{4,5},{5,6},{6,7},{7,4},{8,9},{9,10},{10,1... | collective-permute-start | bytes 331784 | tf_op jit(solution)/shard_map/ppermute | solution.py:439
  4.8 9.9 %collective-permute-start.1 = (bf16[72,768]{1,0:T(8,128)(2,1)S(1)}, bf16[72,768]{1,0:T(8,128)(2,1)S(1)}, u32[]{:S(2)}, u32[]{:S(2)}) collective-permute-start(bf16[72,768]{1,0:T(8,128)(2,1)S(1)} %bitcast.427), channel_id=1, source_target_pairs={{0,2},{1,3},{2,0},{3,1},{4,6},{5,7},{6,4},{7,5},{8,10},{9,11},{10,... | collective-permute-start | bytes 331784 | tf_op jit(solution)/shard_map/ppermute | solution.py:439
  7.4 7.3 %collective-permute-start.2 = (bf16[72,768]{1,0:T(8,128)(2,1)S(1)}, bf16[72,768]{1,0:T(8,128)(2,1)S(1)}, u32[]{:S(2)}, u32[]{:S(2)}) collective-permute-start(bf16[72,768]{1,0:T(8,128)(2,1)S(1)} %bitcast.428), channel_id=1, source_target_pairs={{0,3},{1,0},{2,1},{3,2},{4,7},{5,4},{6,5},{7,6},{8,11},{9,8},{10,9... | collective-permute-start | bytes 331784 | tf_op jit(solution)/shard_map/ppermute | solution.py:439
  15.4 9.6 %collective-permute-start.4 = (bf16[3,72,768]{2,1,0:T(8,128)(2,1)S(1)}, bf16[3,72,768]{2,1,0:T(8,128)(2,1)S(1)}, u32[]{:S(2)}, u32[]{:S(2)}) collective-permute-start(bf16[3,72,768]{2,1,0:T(8,128)(2,1)S(1)} %get-tuple-element.197), channel_id=1, source_target_pairs={{0,8},{4,12},{8,0},{12,4},{16,24},{20,28},{24,16},{28,20},{1,9},{5... | collective-permute-start | bytes 995336 | tf_op jit(solution)/shard_map/ppermute | solution.py:434
  17.0 9.3 %collective-permute-start.5 = (bf16[3,72,768]{2,1,0:T(8,128)(2,1)S(1)}, bf16[3,72,768]{2,1,0:T(8,128)(2,1)S(1)}, u32[]{:S(2)}, u32[]{:S(2)}) collective-permute-start(bf16[3,72,768]{2,1,0:T(8,128)(2,1)S(1)} %get-tuple-element.197), channel_id=1, source_target_pairs={{0,16},{4,20},{8,24},{12,28},{16,0},{20,4},{24,8},{28,12},{1,17},{... | collective-permute-start | bytes 995336 | tf_op jit(solution)/shard_map/ppermute | solution.py:434
  19.3 5.5 %collective-permute-start.3 = (bf16[64,768]{1,0:T(8,128)(2,1)S(1)}, bf16[64,768]{1,0:T(8,128)(2,1)S(1)}, u32[]{:S(2)}, u32[]{:S(2)}) collective-permute-start(bf16[64,768]{1,0:T(8,128)(2,1)S(1)} %slice_select_fusion), channel_id=1, source_target_pairs={{0,1},{1,0},{2,3},{3,2},{4,5},{5,4},{6,7},{7,6},{8,9},{9,8},{10,11... | collective-permute-start | bytes 294920 | tf_op jit(solution)/shard_map/ppermute | solution.py:444
  24.3 28.8 %copy-start.6 = (f32[1152,128]{1,0:T(8,128)}, f32[1152,128]{1,0:T(8,128)S(1)}, u32[]{:S(2)}) copy-start(f32[1152,128]{1,0:T(8,128)S(1)} %get-tuple-element.213.sin_ref) | copy-start | bytes 1769476
  24.3 28.8 %copy-start.9 = (f32[1152,128]{1,0:T(8,128)}, f32[1152,128]{1,0:T(8,128)S(1)}, u32[]{:S(2)}) copy-start(f32[1152,128]{1,0:T(8,128)S(1)} %get-tuple-element.214.cos_ref) | copy-start | bytes 1769476
  25.1 6.5 %copy-start.45 = (bf16[3,72,768]{2,1,0:T(8,128)(2,1)}, bf16[3,72,768]{2,1,0:T(8,128)(2,1)S(1)}, u32[]{:S(2)}) copy-start(bf16[3,72,768]{2,1,0:T(8,128)(2,1)S(1)} %collective-permute-done.4) | copy-start | bytes 995332
  28.3 23.5 %collective-permute-start.6 = (bf16[3,3,72,768]{3,2,1,0:T(8,128)(2,1)S(1)}, bf16[3,3,72,768]{3,2,1,0:T(8,128)(2,1)S(1)}, u32[]{:S(2)}, u32[]{:S(2)}) collective-permute-start(bf16[3,3,72,768]{3,2,1,0:T(8,128)(2,1)S(1)} %pad_maximum_fusion.4), channel_id=1, source_target_pairs={{0,4},{4,0},{8,12},{12,8},{16,20},{20,16},{24,28},{28,24},{1,5},{5... | collective-permute-start | bytes 2985992 | tf_op jit(solution)/shard_map/ppermute | solution.py:434
  28.4 7.1 %collective-permute-start.7 = (bf16[3,40,768]{2,1,0:T(8,128)(2,1)S(1)}, bf16[3,40,768]{2,1,0:T(8,128)(2,1)S(1)}, u32[]{:S(2)}, u32[]{:S(2)}) collective-permute-start(bf16[3,40,768]{2,1,0:T(8,128)(2,1)S(1)} %slice.650), channel_id=1, source_target_pairs={{0,8},{4,12},{8,0},{12,4},{16,24},{20,28},{24,16},{28,20},{1,9},{5... | collective-permute-start | bytes 552968 | tf_op jit(solution)/shard_map/ppermute | solution.py:434
  29.0 9.4 %collective-permute-start.8 = (bf16[3,32,768]{2,1,0:T(8,128)(2,1)S(1)}, bf16[3,32,768]{2,1,0:T(8,128)(2,1)S(1)}, u32[]{:S(2)}, u32[]{:S(2)}) collective-permute-start(bf16[3,32,768]{2,1,0:T(8,128)(2,1)S(1)} %slice.651), channel_id=1, source_target_pairs={{0,16},{4,20},{8,24},{12,28},{16,0},{20,4},{24,8},{28,12},{1,17},{... | collective-permute-start | bytes 442376 | tf_op jit(solution)/shard_map/ppermute | solution.py:434
  31.5 10.0 %collective-permute-start.10 = (bf16[136,768]{1,0:T(8,128)(2,1)S(1)}, bf16[136,768]{1,0:T(8,128)(2,1)S(1)}, u32[]{:S(2)}, u32[]{:S(2)}) collective-permute-start(bf16[136,768]{1,0:T(8,128)(2,1)S(1)} %pad_maximum_fusion.9), channel_id=1, source_target_pairs={{0,1},{1,2},{2,3},{3,0},{4,5},{5,6},{6,7},{7,4},{8,9},{9,10},{10,1... | collective-permute-start | bytes 626696 | tf_op jit(solution)/shard_map/ppermute | solution.py:439
  34.5 14.9 %collective-permute-start.11 = (bf16[136,768]{1,0:T(8,128)(2,1)S(1)}, bf16[136,768]{1,0:T(8,128)(2,1)S(1)}, u32[]{:S(2)}, u32[]{:S(2)}) collective-permute-start(bf16[136,768]{1,0:T(8,128)(2,1)S(1)} %pad_maximum_fusion.9), channel_id=1, source_target_pairs={{0,2},{1,3},{2,0},{3,1},{4,6},{5,7},{6,4},{7,5},{8,10},{9,11},{10,... | collective-permute-start | bytes 626696 | tf_op jit(solution)/shard_map/ppermute | solution.py:439
  35.5 14.0 %collective-permute-start.12 = (bf16[136,768]{1,0:T(8,128)(2,1)S(1)}, bf16[136,768]{1,0:T(8,128)(2,1)S(1)}, u32[]{:S(2)}, u32[]{:S(2)}) collective-permute-start(bf16[136,768]{1,0:T(8,128)(2,1)S(1)} %pad_maximum_fusion.9), channel_id=1, source_target_pairs={{0,3},{1,0},{2,1},{3,2},{4,7},{5,4},{6,5},{7,6},{8,11},{9,8},{10,9... | collective-permute-start | bytes 626696 | tf_op jit(solution)/shard_map/ppermute | solution.py:439
  38.4 13.2 %collective-permute-start.9 = (bf16[3,72,768]{2,1,0:T(8,128)(2,1)S(1)}, bf16[3,72,768]{2,1,0:T(8,128)(2,1)S(1)}, u32[]{:S(2)}, u32[]{:S(2)}) collective-permute-start(bf16[3,72,768]{2,1,0:T(8,128)(2,1)S(1)} %constant_dynamic-update-slice_fusion.16), channel_id=1, source_target_pairs={{0,4},{4,0},{8,12},{12,8},{16,20},{20,16},{24,28},{28,24},{1,5},{5... | collective-permute-start | bytes 995336 | tf_op jit(solution)/shard_map/ppermute | solution.py:434
  41.5 10.2 %copy-start.59 = (bf16[136,768]{1,0:T(8,128)(2,1)}, bf16[136,768]{1,0:T(8,128)(2,1)S(1)}, u32[]{:S(2)}) copy-start(bf16[136,768]{1,0:T(8,128)(2,1)S(1)} %collective-permute-done.10) | copy-start | bytes 626692
  49.6 16.0 %collective-permute-start.13 = (bf16[3,136,768]{2,1,0:T(8,128)(2,1)S(1)}, bf16[3,136,768]{2,1,0:T(8,128)(2,1)S(1)}, u32[]{:S(2)}, u32[]{:S(2)}) collective-permute-start(bf16[3,136,768]{2,1,0:T(8,128)(2,1)S(1)} %get-tuple-element.191), channel_id=1, source_target_pairs={{0,8},{4,12},{8,0},{12,4},{16,24},{20,28},{24,16},{28,20},{1,9},{5... | collective-permute-start | bytes 1880072 | tf_op jit(solution)/shard_map/ppermute | solution.py:434
  51.1 15.7 %collective-permute-start.14 = (bf16[3,136,768]{2,1,0:T(8,128)(2,1)S(1)}, bf16[3,136,768]{2,1,0:T(8,128)(2,1)S(1)}, u32[]{:S(2)}, u32[]{:S(2)}) collective-permute-start(bf16[3,136,768]{2,1,0:T(8,128)(2,1)S(1)} %get-tuple-element.191), channel_id=1, source_target_pairs={{0,16},{4,20},{8,24},{12,28},{16,0},{20,4},{24,8},{28,12},{1,17},{... | collective-permute-start | bytes 1880072 | tf_op jit(solution)/shard_map/ppermute | solution.py:434
  61.4 8.5 %copy-start = (bf16[1152,768]{1,0:T(8,128)(2,1)}, bf16[1152,768]{1,0:T(8,128)(2,1)S(1)}, u32[]{:S(2)}) copy-start(bf16[1152,768]{1,0:T(8,128)(2,1)S(1)} %get-tuple-element.106.q_ref) | copy-start | bytes 5308420
  61.4 8.5 %copy-start.1 = (bf16[1152,768]{1,0:T(8,128)(2,1)}, bf16[1152,768]{1,0:T(8,128)(2,1)S(1)}, u32[]{:S(2)}) copy-start(bf16[1152,768]{1,0:T(8,128)(2,1)S(1)} %get-tuple-element.107.k_ref) | copy-start | bytes 5308420
  61.4 8.5 %copy-start.2 = (bf16[1152,768]{1,0:T(8,128)(2,1)}, bf16[1152,768]{1,0:T(8,128)(2,1)S(1)}, u32[]{:S(2)}) copy-start(bf16[1152,768]{1,0:T(8,128)(2,1)S(1)} %get-tuple-element.108.v_ref) | copy-start | bytes 5308420
  65.6 14.3 %copy-start.36 = (bf16[3,136,768]{2,1,0:T(8,128)(2,1)}, bf16[3,136,768]{2,1,0:T(8,128)(2,1)S(1)}, u32[]{:S(2)}) copy-start(bf16[3,136,768]{2,1,0:T(8,128)(2,1)S(1)} %collective-permute-done.13) | copy-start | bytes 1880068
  66.8 13.1 %copy-start.34 = (bf16[3,136,768]{2,1,0:T(8,128)(2,1)}, bf16[3,136,768]{2,1,0:T(8,128)(2,1)S(1)}, u32[]{:S(2)}) copy-start(bf16[3,136,768]{2,1,0:T(8,128)(2,1)S(1)} %collective-permute-done.14) | copy-start | bytes 1880068
  66.8 14.8 %collective-permute-start.16 = (bf16[3,72,768]{2,1,0:T(8,128)(2,1)S(1)}, bf16[3,72,768]{2,1,0:T(8,128)(2,1)S(1)}, u32[]{:S(2)}, u32[]{:S(2)}) collective-permute-start(bf16[3,72,768]{2,1,0:T(8,128)(2,1)S(1)} %slice.552), channel_id=1, source_target_pairs={{0,8},{4,12},{8,0},{12,4},{16,24},{20,28},{24,16},{28,20},{1,9},{5... | collective-permute-start | bytes 995336 | tf_op jit(solution)/shard_map/ppermute | solution.py:434
  68.9 18.3 %collective-permute-start.15 = (bf16[3,3,136,768]{3,2,1,0:T(8,128)(2,1)}, bf16[3,3,136,768]{3,2,1,0:T(8,128)(2,1)}, u32[]{:S(2)}, u32[]{:S(2)}) collective-permute-start(bf16[3,3,136,768]{3,2,1,0:T(8,128)(2,1)} %pad_maximum_fusion.1), channel_id=1, source_target_pairs={{0,4},{4,0},{8,12},{12,8},{16,20},{20,16},{24,28},{28,24},{1,5},{5... | collective-permute-start | bytes 5640200 | tf_op jit(solution)/shard_map/ppermute | solution.py:434
  69.0 13.4 %collective-permute-start.17 = (bf16[3,64,768]{2,1,0:T(8,128)(2,1)S(1)}, bf16[3,64,768]{2,1,0:T(8,128)(2,1)S(1)}, u32[]{:S(2)}, u32[]{:S(2)}) collective-permute-start(bf16[3,64,768]{2,1,0:T(8,128)(2,1)S(1)} %slice.553), channel_id=1, source_target_pairs={{0,16},{4,20},{8,24},{12,28},{16,0},{20,4},{24,8},{28,12},{1,17},{... | collective-permute-start | bytes 884744 | tf_op jit(solution)/shard_map/ppermute | solution.py:434
  69.9 10.0 %copy-start.3 = (f32[8,256,128]{2,1,0:T(8,128)}, f32[8,256,128]{2,1,0:T(8,128)S(1)}, u32[]{:S(2)}) copy-start(f32[8,256,128]{2,1,0:T(8,128)S(1)} %and_select_fusion.bias_ref) | copy-start | bytes 3145732
  70.0 13.4 %copy-start.78 = (f32[768]{0:T(1024)S(1)}, f32[768]{0:T(1024)}, u32[]{:S(2)}) copy-start(f32[768]{0:T(1024)} %param.20) | copy-start | bytes 9220
  83.2 2.5 collective-permute-start.18
  93.9 29.5 %copy-start.54 = (bf16[1024,768]{1,0:T(8,128)(2,1)S(1)}, bf16[1024,768]{1,0:T(8,128)(2,1)}, u32[]{:S(2)}) copy-start(bf16[1024,768]{1,0:T(8,128)(2,1)} %og_ref.1) | copy-start | bytes 4718596
  123.4 16.6 %copy-start.14 = (bf16[1024,768]{1,0:T(8,128)(2,1)}, bf16[1024,768]{1,0:T(8,128)(2,1)S(1)}, u32[]{:S(2)}) copy-start(bf16[1024,768]{1,0:T(8,128)(2,1)S(1)} %get-tuple-element.129.do_ref) | copy-start | bytes 4718596
  132.1 19.2 %collective-permute-start.19 = (bf16[2,4,4,72,384]{4,3,2,1,0:T(8,128)(2,1)}, bf16[2,4,4,72,384]{4,3,2,1,0:T(8,128)(2,1)S(1)}, u32[]{:S(2)}, u32[]{:S(2)}) collective-permute-start(bf16[2,4,4,72,384]{4,3,2,1,0:T(8,128)(2,1)} %bitcast.94), channel_id=1, source_target_pairs={{0,4},{4,0},{8,12},{12,8},{16,20},{20,16},{24,28},{28,24},{1,5},{5... | collective-permute-start | bytes 5308424 | tf_op jit(solution)/shard_map/ppermute | solution.py:434
  134.2 16.7 %collective-permute-start.20 = (bf16[4,4,72,384]{3,2,1,0:T(8,128)(2,1)}, bf16[4,4,72,384]{3,2,1,0:T(8,128)(2,1)S(1)}, u32[]{:S(2)}, u32[]{:S(2)}) collective-permute-start(bf16[4,4,72,384]{3,2,1,0:T(8,128)(2,1)} %bitcast.96), channel_id=1, source_target_pairs={{0,4},{4,0},{8,12},{12,8},{16,20},{20,16},{24,28},{28,24},{1,5},{5... | collective-permute-start | bytes 2654216 | tf_op jit(solution)/shard_map/ppermute | solution.py:434
  134.4 14.9 %collective-permute-start.21 = (bf16[4,4,48,384]{3,2,1,0:T(8,128)(2,1)}, bf16[4,4,48,384]{3,2,1,0:T(8,128)(2,1)}, u32[]{:S(2)}, u32[]{:S(2)}) collective-permute-start(bf16[4,4,48,384]{3,2,1,0:T(8,128)(2,1)} %bitcast.98), channel_id=1, source_target_pairs={{0,4},{4,0},{8,12},{12,8},{16,20},{20,16},{24,28},{28,24},{1,5},{5... | collective-permute-start | bytes 1769480 | tf_op jit(solution)/shard_map/ppermute | solution.py:434
  154.8 26.2 %collective-permute-start.22 = (bf16[2,2,264,384]{3,2,0,1:T(8,128)(2,1)}, bf16[2,2,264,384]{3,2,0,1:T(8,128)(2,1)}, u32[]{:S(2)}, u32[]{:S(2)}) collective-permute-start(bf16[2,2,264,384]{3,2,0,1:T(8,128)(2,1)} %bitcast.355), channel_id=1, source_target_pairs={{0,8},{4,12},{8,0},{12,4},{16,24},{20,28},{24,16},{28,20},{1,9},{5... | collective-permute-start | bytes 2433032 | tf_op jit(solution)/shard_map/ppermute | solution.py:434
  158.3 22.6 %collective-permute-start.23 = (bf16[2,2,264,384]{3,2,0,1:T(8,128)(2,1)}, bf16[2,2,264,384]{3,2,0,1:T(8,128)(2,1)}, u32[]{:S(2)}, u32[]{:S(2)}) collective-permute-start(bf16[2,2,264,384]{3,2,0,1:T(8,128)(2,1)} %bitcast.354), channel_id=1, source_target_pairs={{0,16},{4,20},{8,24},{12,28},{16,0},{20,4},{24,8},{28,12},{1,17},{... | collective-permute-start | bytes 2433032 | tf_op jit(solution)/shard_map/ppermute | solution.py:434
  168.3 12.7 %copy-start.15 = (bf16[1024,768]{1,0:T(8,128)(2,1)S(1)}, bf16[1024,768]{1,0:T(8,128)(2,1)}, u32[]{:S(2)}) copy-start(bf16[1024,768]{1,0:T(8,128)(2,1)} %copy-done.14) | copy-start | bytes 4718596
  168.3 12.7 %copy-start.27 = (f32[8,8,256]{2,1,0:T(8,128)S(1)}, f32[8,8,256]{2,1,0:T(8,128)}, u32[]{:S(2)}) copy-start(f32[8,8,256]{2,1,0:T(8,128)} %copy-done.24) | copy-start | bytes 196612
  180.9 12.0 %copy-start.39 = (bf16[2,2,1,264,384]{4,3,2,1,0:T(8,128)(2,1)S(1)}, bf16[2,2,1,264,384]{4,3,2,1,0:T(8,128)(2,1)}, u32[]{:S(2)}) copy-start(bf16[2,2,1,264,384]{4,3,2,1,0:T(8,128)(2,1)} %get-tuple-element.166) | copy-start | bytes 2433028
  187.9 9.8 %collective-permute-start.24 = (bf16[64,2,768]{2,0,1:T(8,128)(2,1)S(1)}, bf16[64,2,768]{2,0,1:T(8,128)(2,1)S(1)}, u32[]{:S(2)}, u32[]{:S(2)}) collective-permute-start(bf16[64,2,768]{2,0,1:T(8,128)(2,1)S(1)} %pad_maximum_fusion.13), channel_id=1, source_target_pairs={{0,1},{1,0},{2,3},{3,2},{4,5},{5,4},{6,7},{7,6},{8,9},{9,8},{10,11... | collective-permute-start | bytes 589832 | tf_op jit(solution)/shard_map/ppermute | solution.py:444
  194.3 6.5 %copy-start.40 = (bf16[2,2,264,384]{3,2,0,1:T(8,128)(2,1)}, bf16[2,2,264,384]{3,2,0,1:T(8,128)(2,1)S(1)}, u32[]{:S(2)}) copy-start(bf16[2,2,264,384]{3,2,0,1:T(8,128)(2,1)S(1)} %fusion.3) | copy-start | bytes 2433028
  194.4 17.1 %collective-permute-start.25 = (bf16[2,264,384]{2,1,0:T(8,128)(2,1)S(1)}, bf16[2,264,384]{2,1,0:T(8,128)(2,1)S(1)}, u32[]{:S(2)}, u32[]{:S(2)}) collective-permute-start(bf16[2,264,384]{2,1,0:T(8,128)(2,1)S(1)} %dynamic-slice_bitcast_fusion.2), channel_id=1, source_target_pairs={{0,16},{4,20},{8,24},{12,28},{16,0},{20,4},{24,8},{28,12},{1,17},{... | collective-permute-start | bytes 1216520 | tf_op jit(solution)/shard_map/ppermute | solution.py:434
  205.0 28.5 %collective-permute-start.30 = (bf16[3,4,4,48,384]{4,3,0,2,1:T(8,128)(2,1)}, bf16[3,4,4,48,384]{4,3,0,2,1:T(8,128)(2,1)}, u32[]{:S(2)}, u32[]{:S(2)}) collective-permute-start(bf16[3,4,4,48,384]{4,3,0,2,1:T(8,128)(2,1)} %copy.63), channel_id=1, source_target_pairs={{0,4},{4,0},{8,12},{12,8},{16,20},{20,16},{24,28},{28,24},{1,5},{5... | collective-permute-start | bytes 5308424 | tf_op jit(solution)/shard_map/ppermute | solution.py:434
  207.2 12.5 %copy-start.13 = (bf16[1024,768]{1,0:T(8,128)(2,1)S(1)}, bf16[1024,768]{1,0:T(8,128)(2,1)}, u32[]{:S(2)}) copy-start(bf16[1024,768]{1,0:T(8,128)(2,1)} %x_ref.3) | copy-start | bytes 4718596
  207.3 11.8 %collective-permute-start.26 = (bf16[2,264,384]{2,1,0:T(8,128)(2,1)S(1)}, bf16[2,264,384]{2,1,0:T(8,128)(2,1)S(1)}, u32[]{:S(2)}, u32[]{:S(2)}) collective-permute-start(bf16[2,264,384]{2,1,0:T(8,128)(2,1)S(1)} %dynamic-slice_bitcast_fusion.1), channel_id=1, source_target_pairs={{0,8},{4,12},{8,0},{12,4},{16,24},{20,28},{24,16},{28,20},{1,9},{5... | collective-permute-start | bytes 1216520 | tf_op jit(solution)/shard_map/ppermute | solution.py:434
  207.7 12.1 %copy-start.16 = (f32[1024,768]{1,0:T(8,128)S(1)}, f32[1024,768]{1,0:T(8,128)}, u32[]{:S(2)}) copy-start(f32[1024,768]{1,0:T(8,128)} %get-tuple-element.137.gmid_ref) | copy-start | bytes 9437188
  211.5 7.5 %copy-start.73 = (bf16[2,264,384]{2,1,0:T(8,128)(2,1)}, bf16[2,264,384]{2,1,0:T(8,128)(2,1)S(1)}, u32[]{:S(2)}) copy-start(bf16[2,264,384]{2,1,0:T(8,128)(2,1)S(1)} %collective-permute-done.25) | copy-start | bytes 1216516
  230.1 30.7 %collective-permute-start.27 = (bf16[264,384]{1,0:T(8,128)(2,1)S(1)}, bf16[264,384]{1,0:T(8,128)(2,1)S(1)}, u32[]{:S(2)}, u32[]{:S(2)}) collective-permute-start(bf16[264,384]{1,0:T(8,128)(2,1)S(1)} %slice_bitcast_fusion.17), channel_id=1, source_target_pairs={{0,3},{1,0},{2,1},{3,2},{4,7},{5,4},{6,5},{7,6},{8,11},{9,8},{10,9... | collective-permute-start | bytes 608264 | tf_op jit(solution)/shard_map/ppermute | solution.py:439
  235.8 11.6 %collective-permute-start.34 = (bf16[2,2,144,384]{3,2,0,1:T(8,128)(2,1)S(1)}, bf16[2,2,144,384]{3,2,0,1:T(8,128)(2,1)S(1)}, u32[]{:S(2)}, u32[]{:S(2)}) collective-permute-start(bf16[2,2,144,384]{3,2,0,1:T(8,128)(2,1)S(1)} %bitcast.418), channel_id=1, source_target_pairs={{0,16},{4,20},{8,24},{12,28},{16,0},{20,4},{24,8},{28,12},{1,17},{... | collective-permute-start | bytes 1327112 | tf_op jit(solution)/shard_map/ppermute | solution.py:434
  236.4 24.3 %collective-permute-start.28 = (bf16[264,384]{1,0:T(8,128)(2,1)S(1)}, bf16[264,384]{1,0:T(8,128)(2,1)S(1)}, u32[]{:S(2)}, u32[]{:S(2)}) collective-permute-start(bf16[264,384]{1,0:T(8,128)(2,1)S(1)} %get-tuple-element.194), channel_id=1, source_target_pairs={{0,2},{1,3},{2,0},{3,1},{4,6},{5,7},{6,4},{7,5},{8,10},{9,11},{10,... | collective-permute-start | bytes 608264 | tf_op jit(solution)/shard_map/ppermute | solution.py:439
  237.4 23.3 %collective-permute-start.29 = (bf16[264,384]{1,0:T(8,128)(2,1)S(1)}, bf16[264,384]{1,0:T(8,128)(2,1)S(1)}, u32[]{:S(2)}, u32[]{:S(2)}) collective-permute-start(bf16[264,384]{1,0:T(8,128)(2,1)S(1)} %get-tuple-element.195), channel_id=1, source_target_pairs={{0,1},{1,2},{2,3},{3,0},{4,5},{5,6},{6,7},{7,4},{8,9},{9,10},{10,1... | collective-permute-start | bytes 608264 | tf_op jit(solution)/shard_map/ppermute | solution.py:439
  237.4 11.0 %collective-permute-start.31 = (bf16[2,2,144,384]{3,2,1,0:T(8,128)(2,1)S(1)}, bf16[2,2,144,384]{3,2,1,0:T(8,128)(2,1)S(1)}, u32[]{:S(2)}, u32[]{:S(2)}) collective-permute-start(bf16[2,2,144,384]{3,2,1,0:T(8,128)(2,1)S(1)} %dynamic-slice_bitcast_fusion), channel_id=1, source_target_pairs={{0,8},{4,12},{8,0},{12,4},{16,24},{20,28},{24,16},{28,20},{1,9},{5... | collective-permute-start | bytes 1327112 | tf_op jit(solution)/shard_map/ppermute | solution.py:434
  247.5 6.0 %collective-permute-start.35 = (bf16[2,144,384]{2,1,0:T(8,128)(2,1)S(1)}, bf16[2,144,384]{2,1,0:T(8,128)(2,1)S(1)}, u32[]{:S(2)}, u32[]{:S(2)}) collective-permute-start(bf16[2,144,384]{2,1,0:T(8,128)(2,1)S(1)} %dynamic-slice_bitcast_fusion.3), channel_id=1, source_target_pairs={{0,8},{4,12},{8,0},{12,4},{16,24},{20,28},{24,16},{28,20},{1,9},{5... | collective-permute-start | bytes 663560 | tf_op jit(solution)/shard_map/ppermute | solution.py:434
  248.6 6.2 %collective-permute-start.32 = (bf16[2,144,384]{2,1,0:T(8,128)(2,1)S(1)}, bf16[2,144,384]{2,1,0:T(8,128)(2,1)S(1)}, u32[]{:S(2)}, u32[]{:S(2)}) collective-permute-start(bf16[2,144,384]{2,1,0:T(8,128)(2,1)S(1)} %dynamic-slice_bitcast_fusion.4), channel_id=1, source_target_pairs={{0,16},{4,20},{8,24},{12,28},{16,0},{20,4},{24,8},{28,12},{1,17},{... | collective-permute-start | bytes 663560 | tf_op jit(solution)/shard_map/ppermute | solution.py:434
  255.0 8.1 %collective-permute-start.33 = (bf16[152,384]{1,0:T(8,128)(2,1)S(1)}, bf16[152,384]{1,0:T(8,128)(2,1)S(1)}, u32[]{:S(2)}, u32[]{:S(2)}) collective-permute-start(bf16[152,384]{1,0:T(8,128)(2,1)S(1)} %get-tuple-element.219), channel_id=1, source_target_pairs={{0,3},{1,0},{2,1},{3,2},{4,7},{5,4},{6,5},{7,6},{8,11},{9,8},{10,9... | collective-permute-start | bytes 350216 | tf_op jit(solution)/shard_map/ppermute | solution.py:439
  260.8 7.0 %collective-permute-start.36 = (bf16[152,384]{1,0:T(8,128)(2,1)S(1)}, bf16[152,384]{1,0:T(8,128)(2,1)S(1)}, u32[]{:S(2)}, u32[]{:S(2)}) collective-permute-start(bf16[152,384]{1,0:T(8,128)(2,1)S(1)} %get-tuple-element.218), channel_id=1, source_target_pairs={{0,2},{1,3},{2,0},{3,1},{4,6},{5,7},{6,4},{7,5},{8,10},{9,11},{10,... | collective-permute-start | bytes 350216 | tf_op jit(solution)/shard_map/ppermute | solution.py:439
  261.0 7.5 %collective-permute-start.37 = (bf16[152,384]{1,0:T(8,128)(2,1)S(1)}, bf16[152,384]{1,0:T(8,128)(2,1)S(1)}, u32[]{:S(2)}, u32[]{:S(2)}) collective-permute-start(bf16[152,384]{1,0:T(8,128)(2,1)S(1)} %get-tuple-element.217), channel_id=1, source_target_pairs={{0,1},{1,2},{2,3},{3,0},{4,5},{5,6},{6,7},{7,4},{8,9},{9,10},{10,1... | collective-permute-start | bytes 350216 | tf_op jit(solution)/shard_map/ppermute | solution.py:439
  270.0 7.1 %collective-permute-start.38 = (bf16[416,384]{1,0:T(8,128)(2,1)S(1)}, bf16[416,384]{1,0:T(8,128)(2,1)S(1)}, u32[]{:S(2)}, u32[]{:S(2)}) collective-permute-start(bf16[416,384]{1,0:T(8,128)(2,1)S(1)} %get-tuple-element.199), channel_id=1, source_target_pairs={{0,8},{4,12},{8,0},{12,4},{16,24},{20,28},{24,16},{28,20},{1,9},{5... | collective-permute-start | bytes 958472 | tf_op jit(solution)/shard_map/ppermute | solution.py:434
  270.6 9.5 %collective-permute-start.39 = (bf16[416,384]{1,0:T(8,128)(2,1)S(1)}, bf16[416,384]{1,0:T(8,128)(2,1)S(1)}, u32[]{:S(2)}, u32[]{:S(2)}) collective-permute-start(bf16[416,384]{1,0:T(8,128)(2,1)S(1)} %get-tuple-element.199), channel_id=1, source_target_pairs={{0,16},{4,20},{8,24},{12,28},{16,0},{20,4},{24,8},{28,12},{1,17},{... | collective-permute-start | bytes 958472 | tf_op jit(solution)/shard_map/ppermute | solution.py:434
  272.2 9.3 %collective-permute-start.40 = (bf16[416,384]{1,0:T(8,128)(2,1)S(1)}, bf16[416,384]{1,0:T(8,128)(2,1)S(1)}, u32[]{:S(2)}, u32[]{:S(2)}) collective-permute-start(bf16[416,384]{1,0:T(8,128)(2,1)S(1)} %get-tuple-element.199), channel_id=1, source_target_pairs={{0,24},{4,28},{8,16},{12,20},{16,8},{20,12},{24,0},{28,4},{1,25},{... | collective-permute-start | bytes 958472 | tf_op jit(solution)/shard_map/ppermute | solution.py:434
  281.7 3.1 %collective-permute-start.41 = (bf16[4,416,384]{2,1,0:T(8,128)(2,1)S(1)}, bf16[4,416,384]{2,1,0:T(8,128)(2,1)S(1)}, u32[]{:S(2)}, u32[]{:S(2)}) collective-permute-start(bf16[4,416,384]{2,1,0:T(8,128)(2,1)S(1)} %pad_maximum_fusion.3), channel_id=1, source_target_pairs={{0,4},{4,0},{8,12},{12,8},{16,20},{20,16},{24,28},{28,24},{1,5},{5... | collective-permute-start | bytes 3833864 | tf_op jit(solution)/shard_map/ppermute | solution.py:434
  (59 other events, 123.0 us)
